TPU v7x, 256 devices: a whole 4x4x8 slice. The times are simulated.
256 devices in a mesh: row: 32 (over z, x_hi, core), col: 8 (over x_lo, y).
Axes of the slice: x: 4 (x_hi: 2, x_lo: 2; x = x_hi * 2 + x_lo), y: 4, z: 8, core: 2. Of those that a mesh axis runs over, the one named last changes fastest.
Arguments:
- features: bfloat16 [131072, 128], P(('row', 'col')), may hold values from -6 to 6
- weight: bfloat16 [128, 128], replicated, may hold values from -0.5 to 0.5
- adj_values: bfloat16 [32, 8, 256, 128, 128], P('row', 'col'), may hold values from -0.15625 to 0.15625
- block_coords: int32 [32, 8, 2, 256], P('row', 'col'), may hold values from 0 to 127, as said below
- block_counts: int32 [32, 8], P('row', 'col'), may hold values from 32 to 256, as said below
- cotangent: bfloat16 [131072, 128], P(('row', 'col')), may hold values from -6 to 6
Outputs:
- activated: bfloat16 [131072, 128], P(('row', 'col'))
- feature_grad: bfloat16 [131072, 128], P(('row', 'col'))
- weight_grad: float32 [128, 128], replicated
Inputs may be any that keep to these rules, and one draw needn't show every extreme that they name: `block_coords`: entry [g, h, 0, s] is a block-row of row group g (below 32); entry [g, h, 1, s] a block-column of column group h (below 128); blocks may repeat. `block_counts`: some device uses all 256 slots.
All inputs are finite; a program needn't handle non-finite values.
Results may differ from a plain program's by a relative error of at most 0.0065.
Values may be sent and summed in bfloat16 or wider, within the bound.
No kernel may reach another device: no remote copies, remote signals or barrier semaphores. Data moves between devices by JAX's collectives and lax.ppermute only.
A program may use at most 128 MiB of HBM per device.

v0:
```python
import jax
import jax.numpy as jnp
from jax import lax
from jax.sharding import PartitionSpec as P


def silu_grad(values):
    sigmoid_z = jax.nn.sigmoid(values)
    return sigmoid_z * (1.0 + values * (1.0 - sigmoid_z))


def per_device(features, weight, adj_values, block_coords, block_counts, cotangent):
    blocks = adj_values[0, 0]
    coords = block_coords[0, 0]
    block_total = block_counts[0, 0]
    slot_total = blocks.shape[0]
    block_size = blocks.shape[1]
    node_dev = features.shape[0]
    channels = features.shape[1]
    row_devices = lax.axis_size("row")
    col_devices = lax.axis_size("col")
    per_span = node_dev // block_size
    row_blocks = col_devices * per_span
    col_blocks = row_devices * per_span
    live_slots = (jnp.arange(slot_total, dtype=jnp.int32) < block_total)[:, None, None]
    row_index = coords[0]
    col_index = coords[1]
    hidden = jnp.dot(features, weight, preferred_element_type=jnp.float32).astype(jnp.bfloat16)
    gathered = lax.all_gather(hidden, "row", axis=0, tiled=True).reshape(
        col_blocks, block_size, channels
    )
    forward_terms = jnp.einsum(
        "sab,sbh->sah", blocks, gathered[col_index], preferred_element_type=jnp.float32
    )
    forward_terms = jnp.where(live_slots, forward_terms, 0.0)
    partial_value = jax.ops.segment_sum(forward_terms, row_index, num_segments=row_blocks).reshape(
        row_blocks * block_size, channels
    )
    own_rows = lax.psum_scatter(partial_value, "col", scatter_dimension=0, tiled=True)
    activated = jax.nn.silu(own_rows).astype(jnp.bfloat16)
    delta_local = (cotangent.astype(jnp.float32) * silu_grad(own_rows)).astype(jnp.bfloat16)
    delta_rows = lax.all_gather(delta_local, "col", axis=0, tiled=True)
    delta_blocks = delta_rows.reshape(row_blocks, block_size, channels)
    backward_terms = jnp.einsum(
        "sab,sah->sbh", blocks, delta_blocks[row_index], preferred_element_type=jnp.float32
    )
    backward_terms = jnp.where(live_slots, backward_terms, 0.0)
    col_partial = jax.ops.segment_sum(backward_terms, col_index, num_segments=col_blocks).reshape(
        col_blocks * block_size, channels
    )
    grad_hidden = lax.psum_scatter(col_partial, "row", scatter_dimension=0, tiled=True)
    grad_rounded = grad_hidden.astype(jnp.bfloat16)
    feature_grad = jnp.dot(grad_rounded, weight.T, preferred_element_type=jnp.float32).astype(
        jnp.bfloat16
    )
    weight_part = lax.dot_general(
        features, grad_rounded, (((0,), (0,)), ((), ())), preferred_element_type=jnp.float32
    )
    grad_scale = float(node_dev * row_devices * col_devices) ** (-0.5)
    weight_grad = lax.psum(weight_part, ("row", "col")) * grad_scale
    return (activated, feature_grad, weight_grad)


def solution(mesh):
    in_specs = (
        P(("row", "col"), None),
        P(),
        P("row", "col", None, None, None),
        P("row", "col", None, None),
        P("row", "col"),
        P(("row", "col"), None),
    )
    out_specs = (P(("row", "col"), None), P(("row", "col"), None), P())
    return jax.shard_map(
        per_device, mesh=mesh, in_specs=in_specs, out_specs=out_specs, check_vma=False
    )
```

profile of v0, /device:TPU:8, one launch (start us, length us, event | category | flops | bytes accessed | tf_op | source)
XLA Modules:
  0.0 763.1 jit_solution(5437621909453823179)
XLA Ops:
  7.2 0.0 all-gather.3.cloned.1.call-start
  7.2 0.8 copy-done
  8.1 1.6 convolution_convert_fusion.1
  9.7 0.0 all-gather.3.cloned.1.call-update
  9.7 0.0 reduce-scatter.3.cloned.1.call-start
  10.4 0.8 compare_select_fusion
  11.2 0.8 fusion.4
  11.9 89.2 %all-gather.3.cloned.1.call-done = bf16[16384,128]{1,0:T(8,128)(2,1)} async-done(((bf16[512,128]{1,0:T(8,128)(2,1)}), bf16[16384,128]{1,0:T(8,128)(2,1)}) %all-gather.3.cloned.1.call-update) | async-done | bytes 4194320 | tf_op jit(solution)/shard_map/all_gather | solution.py:29
  101.1 10.8 %gather_fusion = bf16[256,128,128]{2,1,0:T(8,128)(2,1)} fusion(bf16[128,128,128]{2,1,0:T(8,128)(2,1)} %bitcast.34, s32[1024]{0:T(1024)S(1)} %pad_clamp_fusion.1), kind=kCustom, calls=%fused_computation | custom fusion | bytes 16778240 | tf_op jit(solution)/shard_map/gather | solution.py:33
  111.9 13.2 %select_bitcast_fusion.1 = f32[256,128,128]{1,2,0:T(8,128)} fusion(bf16[256,128,128]{2,1,0:T(8,128)(2,1)} %gather_fusion, bf16[1,1,256,128,128]{4,3,2,1,0:T(8,128)(2,1)} %param.8, pred[256]{0:T(512)(128)(4,1)S(1)} %iota_compare_fusion), kind=kOutput, calls=%fused_computation.5 | convolution fusion | flops 1077936128 | bytes 33554688 | tf_op jit(solution)/shard_map/sab,sbh->sah/dot_general | solution.py:32
  125.1 17.4 %copy.13 = f32[256,128,128]{2,1,0:T(8,128)} copy(f32[256,128,128]{1,2,0:T(8,128)} %select_bitcast_fusion.1) | data formatting | bytes 33554432 | tf_op jit(solution)/shard_map/jit(_where)/select_n | solution.py:35
  142.5 0.2 broadcast_in_dim.25
  142.7 33.2 %scatter_fusion = f32[32,128,128]{2,1,0:T(8,128)S(1)} fusion(f32[32,128,128]{2,1,0:T(8,128)S(1)} %broadcast_in_dim.25, s32[256]{0:T(256)S(1)} %bitcast.36, f32[256,128,128]{2,1,0:T(8,128)} %copy.13), kind=kCustom, calls=%fused_computation.2 | custom fusion | flops 4194304 | bytes 50332672 | tf_op jit(solution)/shard_map/scatter-add | solution.py:36
  176.0 1.3 copy-done.1
  177.3 0.0 all-gather.5.cloned.1.call-start
  177.4 38.9 %reduce-scatter.3.cloned.1.call-done = f32[512,128]{1,0:T(8,128)} async-done(((f32[4096,128]{1,0:T(8,128)}), f32[512,128]{1,0:T(8,128)}) %reduce-scatter.3.cloned.1.call-update) | async-done | bytes 262160 | tf_op jit(solution)/shard_map/reduce_scatter | solution.py:39
  216.3 1.8 multiply_convert_fusion
  218.1 0.0 all-gather.5.cloned.1.call-update
  218.1 0.2 reduce-scatter.5.cloned.1.call-start
  218.4 41.3 %all-gather.5.cloned.1.call-done = bf16[4096,128]{1,0:T(8,128)(2,1)} async-done(((bf16[512,128]{1,0:T(8,128)(2,1)}), bf16[4096,128]{1,0:T(8,128)(2,1)}) %all-gather.5.cloned.1.call-update) | async-done | bytes 1048592 | tf_op jit(solution)/shard_map/all_gather | solution.py:42
  259.7 9.8 %gather_fusion.1 = bf16[256,128,128]{2,1,0:T(8,128)(2,1)} fusion(bf16[32,128,128]{2,1,0:T(8,128)(2,1)} %bitcast.33, s32[1024]{0:T(1024)S(1)} %pad_clamp_fusion), kind=kCustom, calls=%fused_computation.1 | custom fusion | bytes 16778240 | tf_op jit(solution)/shard_map/gather | solution.py:45
  269.5 15.4 %select_bitcast_fusion = f32[256,128,128]{1,2,0:T(8,128)} fusion(bf16[256,128,128]{2,1,0:T(8,128)(2,1)} %gather_fusion.1, bf16[1,1,256,128,128]{4,3,2,1,0:T(8,128)(2,1)} %param.8, pred[256]{0:T(512)(128)(4,1)S(1)} %iota_compare_fusion), kind=kOutput, calls=%fused_computation.4 | convolution fusion | flops 1077936128 | bytes 33554688 | tf_op jit(solution)/shard_map/sab,sah->sbh/dot_general | solution.py:44
  284.9 17.4 %copy.15 = f32[256,128,128]{2,1,0:T(8,128)} copy(f32[256,128,128]{1,2,0:T(8,128)} %select_bitcast_fusion) | data formatting | bytes 33554432 | tf_op jit(solution)/shard_map/jit(_where)/select_n | solution.py:47
  302.4 4.3 broadcast_in_dim.28
  306.7 51.8 %scatter_fusion.1 = f32[128,128,128]{2,1,0:T(8,128)} fusion(f32[128,128,128]{2,1,0:T(8,128)} %broadcast_in_dim.28, s32[256]{0:T(256)S(1)} %bitcast.35, f32[256,128,128]{2,1,0:T(8,128)} %copy.15), kind=kCustom, calls=%fused_computation.3 | custom fusion | flops 4194304 | bytes 50332672 | tf_op jit(solution)/shard_map/scatter-add | solution.py:48
  358.5 0.0 all-reduce.2.cloned.1.call-start
  358.6 155.6 %reduce-scatter.5.cloned.1.call-done = f32[512,128]{1,0:T(8,128)} async-done(((f32[16384,128]{1,0:T(8,128)}), f32[512,128]{1,0:T(8,128)}) %reduce-scatter.5.cloned.1.call-update) | async-done | bytes 262160 | tf_op jit(solution)/shard_map/reduce_scatter | solution.py:51
  514.1 1.8 convolution_bitcast_fusion
  516.0 1.8 convolution_convert_fusion
  517.8 237.2 %all-reduce.2.cloned.1.call-done = f32[128,128]{0,1:T(8,128)} async-done(((f32[128,128]{0,1:T(8,128)}), f32[128,128]{0,1:T(8,128)}) %all-reduce.2.cloned.1.call-update) | async-done | bytes 65552 | tf_op jit(solution)/shard_map/psum | solution.py:60
  755.0 0.8 broadcast_multiply_fusion
  755.8 0.7 copy.16
  (12 shorter events, 0.1 us)
Async XLA Ops:
  7.2 0.9 copy-start
  7.2 93.9 %all-gather.3.cloned.1.call-start = ((), (), s32[]{:S(2)}) async-start(), calls=%async_computation.2 | async-start | bytes 4325376 | tf_op jit(solution)/shard_map/all_gather | solution.py:29
  9.7 206.6 %reduce-scatter.3.cloned.1.call-start = ((), (), s32[]{:S(2)}) async-start(), calls=%async_computation.3 | async-start | bytes 2359296 | tf_op jit(solution)/shard_map/reduce_scatter | solution.py:39
  142.7 73.6 %copy-start.2 = (bf16[512,128]{1,0:T(8,128)(2,1)S(1)}, bf16[512,128]{1,0:T(8,128)(2,1)}, u32[]{:S(2)}) copy-start(bf16[512,128]{1,0:T(8,128)(2,1)} %param.11) | copy-start | bytes 393220
  176.0 1.3 copy-start.1
  177.3 82.3 %all-gather.5.cloned.1.call-start = ((), (), s32[]{:S(2)}) async-start(), calls=%async_computation.4 | async-start | bytes 1179648 | tf_op jit(solution)/shard_map/all_gather | solution.py:42
  218.1 296.0 %reduce-scatter.5.cloned.1.call-start = ((), (), s32[]{:S(2)}) async-start(), calls=%async_computation.5 | async-start | bytes 8650752 | tf_op jit(solution)/shard_map/reduce_scatter | solution.py:51
  358.5 157.5 %copy-start.3 = (bf16[128,128]{1,0:T(8,128)(2,1)S(1)}, bf16[128,128]{1,0:T(8,128)(2,1)}, u32[]{:S(2)}) copy-start(bf16[128,128]{1,0:T(8,128)(2,1)} %param.7) | copy-start | bytes 98308
  358.5 396.5 %all-reduce.2.cloned.1.call-start = ((), (), s32[]{:S(2)}) async-start(), calls=%async_computation.6 | async-start | bytes 131072 | tf_op jit(solution)/shard_map/psum | solution.py:60
Sparse Core Ops, SparseCore 0:
  11.4 89.6 all-gather.2
  177.5 38.8 reduce-scatter.2
  218.7 40.9 all-gather.4
  358.6 155.4 reduce-scatter.4
  520.0 234.8 all-reduce.1
where the time goes:
time: 767 us; the launch traced here: 763 us
  waiting for transfers between devices  562 us (73%)
  other arithmetic  88.4 us (12%)
  local copies, waits for them, and re-layouts  63.7 us (8%)
  matrix products  33.8 us (4%)
  between operations  14.5 us (2%)
    psum x1, waiting for transfers between devices, per_device(): weight_grad = lax.psum(weight_part, ('row', 'col')) * grad_scale  237 us
    reduce_scatter x1, waiting for transfers between devices, per_device(): lax.psum_scatter(col_partial, 'row', scatter_dimension=0, tiled=True)  156 us
    all_gather x1, waiting for transfers between devices, per_device(): lax.all_gather(hidden, 'row', axis=0, tiled=True)  89.2 us
    scatter-add x1, other arithmetic, per_device(): jax.ops.segment_sum(backward_terms, col_index, num_segments=col_blocks)  51.8 us
    all_gather x1, waiting for transfers between devices, per_device(): delta_rows = lax.all_gather(delta_local, 'col', axis=0, tiled=True)  41.3 us
    reduce_scatter x1, waiting for transfers between devices, per_device(): lax.psum_scatter(partial_value, 'col', scatter_dimension=0, tiled=True)  38.9 us
    scatter-add x1, other arithmetic, per_device(): jax.ops.segment_sum(forward_terms, row_index, num_segments=row_blocks)  33.2 us
    select_n x1, local copies, waits for them, and re-layouts, per_device(): forward_terms = jnp.where(live_slots, forward_terms, 0.0)  17.4 us
  transfers between devices with their start and end apart: 5, of which 5 were waited for; matrix products, arithmetic and copies ran while one was open for 0% of the time, Pallas kernels for 0%

commit v1 on v0

v1 whole, which is shorter than its diff:
```python
import jax
import jax.numpy as jnp
from jax import lax
from jax.experimental import pallas as pl
from jax.experimental.pallas import tpu as pltpu
from jax.sharding import PartitionSpec as P

NZ = 8
BLK = 128
BPD = 4
HALF = 2
CHUNK = 32
UNROLL = 16
VMEM_LIMIT = 24 << 20
BF = jnp.bfloat16
F32 = jnp.float32

PLACES = ((0, 4), (8, 16), (20, 32), (36, 48), (52, 60), (40, 56), (24, 44), (12, 28))


def silu_grad(values):
    sigmoid_z = jax.nn.sigmoid(values)
    return sigmoid_z * (1.0 + values * (1.0 - sigmoid_z))


def wide(value):
    return value.astype(F32)


def cat(*values):
    return jnp.concatenate(values, axis=0)


def z_shift(value, step):
    perm = [(r, ((r // 4 + step) % NZ) * 4 + r % 4) for r in range(4 * NZ)]
    return lax.ppermute(value, "row", perm)


def row_swap(value, mask):
    return lax.ppermute(value, "row", [(r, r ^ mask) for r in range(4 * NZ)])


def split(value):
    high = value.astype(BF)
    return high, (value - wide(high)).astype(BF)


def add_products(x_first, dst, src, count, blocks, held, acc, slots, sems):
    per_chunk = CHUNK // UNROLL
    groups = (jnp.clip(count[0], 0, slots.shape[0]) + UNROLL - 1) // UNROLL

    def body(j, carry):
        products = []
        for u in range(UNROLL):
            s = j * UNROLL + u
            a, x = slots[s], held[src[s]]
            pair = (x, a) if x_first else (a, x)
            products.append(jnp.dot(*pair, preferred_element_type=F32))
        for u in range(UNROLL):
            acc[dst[j * UNROLL + u]] += products[u]
        return carry

    def chunk(c, carry):
        load(blocks, slots, sems, c).wait()
        lax.fori_loop(c * per_chunk, jnp.minimum((c + 1) * per_chunk, groups), body, 0)
        return carry

    lax.fori_loop(0, slots.shape[0] // CHUNK, chunk, 0)


def load(blocks, slots, sems, c):
    part = pl.ds(c * CHUNK, CHUNK)
    return pltpu.make_async_copy(blocks.at[part], slots.at[part], sems.at[c])


def forward_kernel(dst, src, count, blocks, *refs):
    pieces, (out, acc, held, slots, sems, piece_sems) = refs[:-6], refs[-6:]
    for c in range(slots.shape[0] // CHUNK):
        load(blocks, slots, sems, c).start()
    copies, at = [], 0
    for k, piece in enumerate(pieces):
        size = piece.shape[0]
        copies.append(
            pltpu.make_async_copy(piece, held.at[pl.ds(at, size)], piece_sems.at[k])
        )
        at += size
    for copy in copies:
        copy.start()
    acc[...] = jnp.zeros_like(acc)
    for copy in copies:
        copy.wait()
    add_products(False, dst, src, count, blocks, held, acc, slots, sems)
    out[...] = acc[: out.shape[0]].astype(out.dtype)


def backward_kernel(dst, src, count, blocks, every, keep, send, sums, acc, slots, sems):
    for c in range(slots.shape[0] // CHUNK):
        load(blocks, slots, sems, c).start()
    acc[...] = jnp.zeros_like(acc)
    span = BPD + 1
    total = wide(every[BPD])
    for k in range(1, every.shape[0] // span):
        total = total + wide(every[k * span + BPD])
    high, low = split(total)
    half = keep.shape[0]
    send[half], send[half + 1] = high, low
    sums[...] = wide(high) + wide(low)
    add_products(True, dst, src, count, blocks, every, acc, slots, sems)
    keep[...] = acc[:half].astype(keep.dtype)
    send[:half] = acc[half : 2 * half].astype(send.dtype)


def product(kernel, name, blocks, dst, src, count, sources, out_shape, source_space, scratch):
    vmem = pl.BlockSpec(memory_space=pltpu.VMEM)
    smem = pl.BlockSpec(memory_space=pltpu.SMEM)
    slots = blocks.shape[0]
    return pl.pallas_call(
        kernel,
        name=name,
        in_specs=[smem] * 3
        + [pl.BlockSpec(memory_space=pltpu.HBM)]
        + [pl.BlockSpec(memory_space=source_space)] * len(sources),
        out_specs=[vmem] * len(out_shape),
        out_shape=out_shape,
        scratch_shapes=scratch,
        compiler_params=pltpu.CompilerParams(vmem_limit_bytes=VMEM_LIMIT),
        cost_estimate=pl.CostEstimate(
            flops=2 * slots * BLK**3, bytes_accessed=14 << 20, transcendentals=0
        ),
    )(dst, src, count, pltpu.with_memory_space_constraint(blocks, pltpu.HBM), *sources)


def forward_product(blocks, dst, src, count, pieces, num_dst):
    slots = blocks.shape[0]
    held = sum(piece.shape[0] for piece in pieces)
    (out,) = product(
        forward_kernel,
        "forward_product",
        blocks,
        dst,
        src,
        count,
        pieces,
        [jax.ShapeDtypeStruct((num_dst, BLK, BLK), BF)],
        pl.ANY,
        [
            pltpu.VMEM((num_dst + 1, BLK, BLK), F32),
            pltpu.VMEM((held, BLK, BLK), BF),
            pltpu.VMEM(blocks.shape, BF),
            pltpu.SemaphoreType.DMA((slots // CHUNK,)),
            pltpu.SemaphoreType.DMA((len(pieces),)),
        ],
    )
    return out


def backward_product(blocks, dst, src, count, every, num_dst):
    slots = blocks.shape[0]
    half = num_dst // 2
    return product(
        backward_kernel,
        "backward_product",
        blocks,
        dst,
        src,
        count,
        [every],
        [
            jax.ShapeDtypeStruct((half, BLK, BLK), BF),
            jax.ShapeDtypeStruct((half + 2, BLK, BLK), BF),
            jax.ShapeDtypeStruct((BLK, BLK), F32),
        ],
        pltpu.VMEM,
        [
            pltpu.VMEM((num_dst + 1, BLK, BLK), F32),
            pltpu.VMEM(blocks.shape, BF),
            pltpu.SemaphoreType.DMA((slots // CHUNK,)),
        ],
    )


def gather_rows(own):
    mate = row_swap(own, 2)
    up1, down1 = z_shift(own, 1), z_shift(own, -1)
    up2, down2 = z_shift(cat(mate, up1), 1), z_shift(cat(down1, mate), -1)
    up3, down3 = z_shift(up2, 1), z_shift(down2, -1)
    up4, down4 = z_shift(up3[: BPD + HALF], 1), z_shift(down3[HALF:], -1)
    up5, down5 = z_shift(up4[:HALF], 1), z_shift(down4[BPD:], -1)
    groups = [
        cat(own, mate, up1, down1),
        cat(up2, down2),
        cat(up3, down3),
        cat(up4, down4),
        cat(up5, down5),
    ]
    return groups + [row_swap(group, 1) for group in groups]


def scatter_rows(keep, send, sums):
    arrived = row_swap(send, 1)
    half = keep.shape[0]
    tag = (sums + wide(arrived[half]) + wide(arrived[half + 1])).astype(BF)[None]
    seen_up, seen_down = [], []

    def term(d, x, lo=0, hi=BPD):
        at = (2 * d + x) * BPD
        return wide(keep[at + lo : at + hi]) + wide(arrived[at + lo : at + hi])

    def step(up, down, up_tag, down_tag):
        up = cat(*[part.astype(BF) for part in up], up_tag)
        down = cat(*[part.astype(BF) for part in down], down_tag)
        up, down = lax.optimization_barrier((up, down))
        up, down = z_shift(up, 1), z_shift(down, -1)
        seen_up.append(up[-1:])
        seen_down.append(down[-1:])
        return wide(up[:-1]), wide(down[:-1]), up[-1:], down[-1:]

    def front(value):
        return jnp.pad(value, ((0, HALF), (0, 0), (0, 0)))

    def back(value):
        return jnp.pad(value, ((HALF, 0), (0, 0), (0, 0)))

    up, down, ut, dt = step([term(4, 1, 0, HALF)], [term(4, 1, HALF)], tag, tag)
    up, down, ut, dt = step(
        [term(3, 1) + front(up), term(4, 0, 0, HALF)],
        [term(4, 0, HALF), term(5, 1) + back(down)],
        ut,
        dt,
    )
    up, down, ut, dt = step(
        [term(2, 1) + up[:BPD], term(3, 0) + front(up[BPD:])],
        [term(5, 0) + back(down[:HALF]), term(6, 1) + down[HALF:]],
        ut,
        dt,
    )
    up, down, ut, dt = step(
        [term(1, 1) + up[:BPD], term(2, 0) + up[BPD:]],
        [term(6, 0) + down[:BPD], term(7, 1) + down[BPD:]],
        ut,
        dt,
    )
    near = [tag] + seen_up + seen_down[: NZ // 2 - 1][::-1]
    z = lax.axis_index("row") // 4
    summed = jnp.zeros((BLK, BLK), F32)
    for k in range(NZ):
        d = (z - k) % NZ
        chosen = near[0][0]
        for n in range(1, NZ):
            chosen = jnp.where(d == n, near[n][0], chosen)
        summed = summed + wide(chosen)
    high, low = split(summed)
    theirs = term(0, 1) + up[:BPD] + down[BPD:]
    theirs = cat(theirs.astype(BF), high[None], low[None])
    up = (term(1, 0) + up[BPD:]).astype(BF)
    down = (term(7, 0) + down[:BPD]).astype(BF)
    theirs, up, down = lax.optimization_barrier((theirs, up, down))
    mate, up, down = row_swap(theirs, 2), z_shift(up, 1), z_shift(down, -1)
    total = term(0, 0) + wide(mate[:BPD]) + wide(up) + wide(down)
    return total, (wide(high) + wide(low)) + (wide(mate[BPD]) + wide(mate[BPD + 1]))


def per_device(features, weight, adj_values, block_coords, block_counts, cotangent):
    blocks = adj_values[0, 0]
    coords = block_coords[0, 0]
    count = block_counts[0]
    slots = blocks.shape[0]
    row_devices = lax.axis_size("row")
    col_devices = lax.axis_size("col")
    row_blocks = col_devices * BPD
    col_blocks = row_devices * BPD
    nodes = features.shape[0]
    dot = lambda a, b: jnp.dot(a, b, preferred_element_type=F32)

    me = lax.axis_index("row")
    owner = coords[1] // BPD
    apart = (owner ^ me) & 3
    inner = coords[1] % BPD
    core_part = (apart & 1) * (col_blocks // 2)
    distance = (me // 4 - owner // 4) % NZ * 2 + (apart >> 1)
    from_place = core_part + inner
    for k, place in enumerate(place for pair in PLACES for place in pair):
        from_place = from_place + jnp.where(distance == k, place, 0)
    to_place = core_part + (((owner // 4 - me // 4) % NZ) * 2 + (apart >> 1)) * BPD + inner
    live = jnp.arange(slots, dtype=jnp.int32) < count[0]
    forward_dst = jnp.where(live, coords[0], row_blocks)
    backward_dst = jnp.where(live, to_place, col_blocks)
    delta_at = coords[0] // BPD * (BPD + 1) + coords[0] % BPD

    pieces = gather_rows(features.reshape(BPD, BLK, BLK))
    partial = forward_product(blocks, forward_dst, from_place, count, pieces, row_blocks)
    parts = lax.all_to_all(partial.reshape(col_devices, nodes, BLK), "col", 0, 0)
    spread = jnp.sum(wide(parts), axis=0)
    high, low = split(spread)
    preact = dot(high, weight) + dot(low, weight)
    activated = jax.nn.silu(preact).astype(BF)
    delta = (wide(cotangent) * silu_grad(preact)).astype(BF)
    delta_t = jnp.swapaxes(delta.reshape(BPD, BLK, BLK), 1, 2)

    weight_part = (dot(high.T, delta) + dot(low.T, delta)).astype(BF)
    message = cat(delta_t, weight_part[None])
    every = lax.all_to_all(
        jnp.broadcast_to(message[None], (col_devices,) + message.shape), "col", 0, 0
    ).reshape(-1, BLK, BLK)
    keep, send, sums = backward_product(blocks, backward_dst, delta_at, count, every, col_blocks)
    total, weight_sum = scatter_rows(keep, send, sums)
    grad_scale = float(nodes * row_devices * col_devices) ** (-0.5)
    feature_grad = jnp.einsum("khb,ih->kbi", total.astype(BF), weight, preferred_element_type=F32)
    return activated, feature_grad.astype(BF).reshape(nodes, BLK), weight_sum * grad_scale


def solution(mesh):
    in_specs = (
        P(("row", "col"), None),
        P(),
        P("row", "col", None, None, None),
        P("row", "col", None, None),
        P("row", "col"),
        P(("row", "col"), None),
    )
    out_specs = (P(("row", "col"), None), P(("row", "col"), None), P())
    return jax.shard_map(
        per_device, mesh=mesh, in_specs=in_specs, out_specs=out_specs, check_vma=False
    )
```

time: 767 us -> 156 us (0.20)
  waiting for transfers between devices: 562 us -> 48.1 us
  other arithmetic: 88.4 us -> 6.57 us
  local copies, waits for them, and re-layouts: 63.7 us -> 2.25 us
  starting transfers between devices: 0.39 us -> 44.7 us
  blocking collectives: 0 us -> 40.4 us
  matrix products: 33.8 us -> 3.37 us
  between operations: 14.5 us -> 1.77 us
  Pallas kernels: 0 us -> 8.67 us
    psum x1 -> x0, waiting for transfers between devices: 237 us -> none  [per_device(): weight_grad = lax.psum(weight_part, ('row', 'col')) * grad_scale]
    reduce_scatter x2 -> x0, waiting for transfers between devices: 194 us -> none  [the longest x1 156 us: per_device(): lax.psum_scatter(col_partial, 'row', scatter_dimension=0, tiled=True)]
    all_gather x2 -> x0, waiting for transfers between devices: 130 us -> none  [the longest x1 89.2 us: per_device(): lax.all_gather(hidden, 'row', axis=0, tiled=True)]
    scatter-add x2 -> x0, other arithmetic: 85 us -> none  [the longest x1 51.8 us: per_device(): jax.ops.segment_sum(backward_terms, col_index, num_segments=col_blocks)]
    ppermute x0 -> x28, waiting for transfers between devices: none -> 48.1 us  [the longest x20 41 us: z_shift(): return lax.ppermute(value, 'row', perm)]
    ppermute x0 -> x28, starting transfers between devices: none -> 44.7 us  [the longest x20 34.4 us: z_shift(): return lax.ppermute(value, 'row', perm)]
    all_to_all x0 -> x2, blocking collectives: none -> 40.4 us  [the longest x1 20.5 us: per_device(): lax.all_to_all(partial.reshape(col_devices, nodes, BLK), 'col', 0, 0)]
    select_n x2 -> x0, local copies, waits for them, and re-layouts: 34.9 us -> none  [the longest x1 17.4 us: per_device(): forward_terms = jnp.where(live_slots, forward_terms, 0.0)]
  transfers between devices with their start and end apart: 5 -> 28, of which waited for: 5 -> 17; matrix products, arithmetic and copies ran while one was open for 0% -> 2% of each run, Pallas kernels for 0% -> 0%
where the time goes in v1:
time: 156 us
  waiting for transfers between devices  48.1 us (31%)
  starting transfers between devices  44.7 us (29%)
  blocking collectives  40.4 us (26%)
  Pallas kernels  8.67 us (6%)
  other arithmetic  6.57 us (4%)
  matrix products  3.37 us (2%)
  local copies, waits for them, and re-layouts  2.25 us (1%)
  between operations  1.77 us (1%)
    ppermute x20, waiting for transfers between devices, z_shift(): return lax.ppermute(value, 'row', perm)  41 us
    ppermute x20, starting transfers between devices, z_shift(): return lax.ppermute(value, 'row', perm)  34.4 us
    all_to_all x1, blocking collectives, per_device(): lax.all_to_all(partial.reshape(col_devices, nodes, BLK), 'col', 0, 0)  20.5 us
    all_to_all x1, blocking collectives, per_device(): lax.all_to_all(jnp.broadcast_to(message[None], (col_devices,) + message.s...  19.9 us
    ppermute x8, starting transfers between devices, row_swap(): return lax.ppermute(value, 'row', [(r, r ^ mask) for r in range(4 * NZ)])  10.3 us
    pallas_call x2, Pallas kernels, product(): pl.pallas_call(kernel, name=name, in_specs=[smem] * 3 + [pl.BlockSpec(mem...  8.67 us
    ppermute x8, waiting for transfers between devices, row_swap(): return lax.ppermute(value, 'row', [(r, r ^ mask) for r in range(4 * NZ)])  7.09 us
  transfers between devices with their start and end apart: 28, of which 17 were waited for; matrix products, arithmetic and copies ran while one was open for 2% of the time, Pallas kernels for 0%

profile of v1, /device:TPU:8, one launch (start us, length us, event | category | flops | bytes accessed | tf_op | source)
XLA Modules:
  0.0 155.8 jit_solution(3466764011438288291)
XLA Ops:
  0.6 5.9 %collective-permute-start.2 = (bf16[4,128,128]{2,1,0:T(8,128)(2,1)}, bf16[4,128,128]{2,1,0:T(8,128)(2,1)S(1)}, u32[]{:S(2)}, u32[]{:S(2)}) collective-permute-start(bf16[4,128,128]{2,1,0:T(8,128)(2,1)} %bitcast.190), channel_id=1, source_target_pairs={{0,224},{8,232},{16,240},{24,248},{32,0},{40,8},{48,16},{56,24},{6... | collective-permute-start | bytes 393224 | tf_op jit(solution)/shard_map/ppermute | solution.py:36
  6.6 3.0 %collective-permute-start = (bf16[4,128,128]{2,1,0:T(8,128)(2,1)}, bf16[4,128,128]{2,1,0:T(8,128)(2,1)S(1)}, u32[]{:S(2)}, u32[]{:S(2)}) collective-permute-start(bf16[4,128,128]{2,1,0:T(8,128)(2,1)} %bitcast.192), channel_id=1, source_target_pairs={{0,16},{8,24},{16,0},{24,8},{32,48},{40,56},{48,32},{56,40},{64,80... | collective-permute-start | bytes 393224 | tf_op jit(solution)/shard_map/ppermute | solution.py:40
  9.6 3.3 %collective-permute-done.1 = bf16[4,128,128]{2,1,0:T(8,128)(2,1)S(1)} collective-permute-done((bf16[4,128,128]{2,1,0:T(8,128)(2,1)}, bf16[4,128,128]{2,1,0:T(8,128)(2,1)S(1)}, u32[]{:S(2)}, u32[]{:S(2)}) %collective-permute-start.1) | collective-permute-done | bytes 131104 | tf_op jit(solution)/shard_map/ppermute | solution.py:36
  13.4 3.3 %collective-permute-start.4 = (bf16[8,128,128]{2,1,0:T(8,128)(2,1)S(1)}, bf16[8,128,128]{2,1,0:T(8,128)(2,1)S(1)}, u32[]{:S(2)}, u32[]{:S(2)}) collective-permute-start(bf16[8,128,128]{2,1,0:T(8,128)(2,1)S(1)} %get-tuple-element.56), channel_id=1, source_target_pairs={{0,224},{8,232},{16,240},{24,248},{32,0},{40,8},{48,16},{56,24},{6... | collective-permute-start | bytes 786440 | tf_op jit(solution)/shard_map/ppermute | solution.py:36
  18.2 3.1 %collective-permute-done.3 = bf16[8,128,128]{2,1,0:T(8,128)(2,1)S(1)} collective-permute-done((bf16[8,128,128]{2,1,0:T(8,128)(2,1)S(1)}, bf16[8,128,128]{2,1,0:T(8,128)(2,1)S(1)}, u32[]{:S(2)}, u32[]{:S(2)}) %collective-permute-start.3) | collective-permute-done | bytes 262176 | tf_op jit(solution)/shard_map/ppermute | solution.py:36
  21.2 3.2 %collective-permute-start.6 = (bf16[8,128,128]{2,1,0:T(8,128)(2,1)S(1)}, bf16[8,128,128]{2,1,0:T(8,128)(2,1)S(1)}, u32[]{:S(2)}, u32[]{:S(2)}) collective-permute-start(bf16[8,128,128]{2,1,0:T(8,128)(2,1)S(1)} %collective-permute-done.4), channel_id=1, source_target_pairs={{0,224},{8,232},{16,240},{24,248},{32,0},{40,8},{48,16},{56,24},{6... | collective-permute-start | bytes 786440 | tf_op jit(solution)/shard_map/ppermute | solution.py:36
  26.2 2.6 %collective-permute-done.5 = bf16[8,128,128]{2,1,0:T(8,128)(2,1)S(1)} collective-permute-done((bf16[8,128,128]{2,1,0:T(8,128)(2,1)S(1)}, bf16[8,128,128]{2,1,0:T(8,128)(2,1)S(1)}, u32[]{:S(2)}, u32[]{:S(2)}) %collective-permute-start.5) | collective-permute-done | bytes 262176 | tf_op jit(solution)/shard_map/ppermute | solution.py:36
  28.9 3.3 %collective-permute-start.8 = (bf16[6,128,128]{2,1,0:T(8,128)(2,1)S(1)}, bf16[6,128,128]{2,1,0:T(8,128)(2,1)S(1)}, u32[]{:S(2)}, u32[]{:S(2)}) collective-permute-start(bf16[6,128,128]{2,1,0:T(8,128)(2,1)S(1)} %slice.308), channel_id=1, source_target_pairs={{0,224},{8,232},{16,240},{24,248},{32,0},{40,8},{48,16},{56,24},{6... | collective-permute-start | bytes 589832 | tf_op jit(solution)/shard_map/ppermute | solution.py:36
  32.4 3.4 %collective-permute-done.7 = bf16[6,128,128]{2,1,0:T(8,128)(2,1)S(1)} collective-permute-done((bf16[6,128,128]{2,1,0:T(8,128)(2,1)S(1)}, bf16[6,128,128]{2,1,0:T(8,128)(2,1)S(1)}, u32[]{:S(2)}, u32[]{:S(2)}) %collective-permute-start.7) | collective-permute-done | bytes 196640 | tf_op jit(solution)/shard_map/ppermute | solution.py:36
  35.8 3.3 %collective-permute-start.10 = (bf16[2,128,128]{2,1,0:T(8,128)(2,1)S(1)}, bf16[2,128,128]{2,1,0:T(8,128)(2,1)S(1)}, u32[]{:S(2)}, u32[]{:S(2)}) collective-permute-start(bf16[2,128,128]{2,1,0:T(8,128)(2,1)S(1)} %slice.310), channel_id=1, source_target_pairs={{0,224},{8,232},{16,240},{24,248},{32,0},{40,8},{48,16},{56,24},{6... | collective-permute-start | bytes 196616 | tf_op jit(solution)/shard_map/ppermute | solution.py:36
  39.2 2.1 %collective-permute-done.9 = bf16[2,128,128]{2,1,0:T(8,128)(2,1)S(1)} collective-permute-done((bf16[2,128,128]{2,1,0:T(8,128)(2,1)S(1)}, bf16[2,128,128]{2,1,0:T(8,128)(2,1)S(1)}, u32[]{:S(2)}, u32[]{:S(2)}) %collective-permute-start.9) | collective-permute-done | bytes 65568 | tf_op jit(solution)/shard_map/ppermute | solution.py:36
  43.2 4.2 %forward_product.1 = bf16[32,128,128]{2,1,0:T(8,128)(2,1)S(1)} custom-call(s32[256]{0:T(256)S(1)} %get-tuple-element.63.dst, s32[256]{0:T(256)S(1)} %get-tuple-element.64.src, s32[1]{0:T(128)} %bitcast.182.count, bf16[256,128,128]{2,1,0:T(8,128)(2,1)} %bitcast.186, bf16[16,128,128]{2,1,0:T(8,128)(2,1)S(1)} %pad_maximum_fusion.refs_0_, ...), custom_call_target="tpu_custom_call" | custom-call | flops 1073741824 | bytes 14680064 | tf_op jit(solution)/shard_map/forward_product/pallas_call | solution.py:117
  47.4 20.5 %all_to_all.10 = bf16[8,512,128]{2,1,0:T(8,128)(2,1)S(1)} all-to-all(bf16[8,512,128]{2,1,0:T(8,128)(2,1)S(1)} %bitcast.185), channel_id=1, replica_groups=mesh['row'=32,'col'=8] {'col'}, dimensions={0} | all-to-all | bytes 2097152 | tf_op jit(solution)/shard_map/all_to_all | solution.py:292
  70.3 19.9 %all_to_all.11 = bf16[8,5,128,128]{3,2,1,0:T(8,128)(2,1)S(1)} all-to-all(bf16[8,5,128,128]{3,2,1,0:T(8,128)(2,1)S(1)} %broadcast_in_dim.95), channel_id=1, replica_groups=mesh['row'=32,'col'=8] {'col'}, dimensions={0} | all-to-all | bytes 2621440 | tf_op jit(solution)/shard_map/all_to_all | solution.py:302
  90.2 4.4 %backward_product.1 = (bf16[64,128,128]{2,1,0:T(8,128)(2,1)S(1)}, bf16[66,128,128]{2,1,0:T(8,128)(2,1)S(1)}, f32[128,128]{1,0:T(8,128)S(1)}) custom-call(s32[256]{0:T(256)S(1)} %get-tuple-element.33.dst, s32[256]{0:T(256)S(1)} %get-tuple-element.62.src, s32[1]{0:T(128)} %bitcast.183.count, bf16[256,128,128]{2,1,0:T(8,128)(2,1)} %bitcast.187, ...), custom_call_target="tpu_custom_call" | custom-call | flops 1073741824 | bytes 14680064 | tf_op jit(solution)/shard_map/backward_product/pallas_call | solution.py:117
  94.7 4.2 %collective-permute-done.16 = bf16[66,128,128]{2,1,0:T(8,128)(2,1)S(1)} collective-permute-done((bf16[66,128,128]{2,1,0:T(8,128)(2,1)S(1)}, bf16[66,128,128]{2,1,0:T(8,128)(2,1)S(1)}, u32[]{:S(2)}, u32[]{:S(2)}) %collective-permute-start.16) | collective-permute-done | bytes 2162720 | tf_op jit(solution)/shard_map/ppermute | solution.py:40
  99.1 1.4 collective-permute-start.17
  100.5 1.9 %collective-permute-start.18 = (bf16[3,128,128]{2,1,0:T(8,128)(2,1)S(1)}, bf16[3,128,128]{2,1,0:T(8,128)(2,1)S(1)}, u32[]{:S(2)}, u32[]{:S(2)}) collective-permute-start(bf16[3,128,128]{2,1,0:T(8,128)(2,1)S(1)} %get-tuple-element.21), channel_id=1, source_target_pairs={{0,224},{8,232},{16,240},{24,248},{32,0},{40,8},{48,16},{56,24},{6... | collective-permute-start | bytes 294920 | tf_op jit(solution)/shard_map/ppermute | solution.py:36
  102.4 3.0 %collective-permute-done.17 = bf16[3,128,128]{2,1,0:T(8,128)(2,1)S(1)} collective-permute-done((bf16[3,128,128]{2,1,0:T(8,128)(2,1)S(1)}, bf16[3,128,128]{2,1,0:T(8,128)(2,1)S(1)}, u32[]{:S(2)}, u32[]{:S(2)}) %collective-permute-start.17) | collective-permute-done | bytes 98336 | tf_op jit(solution)/shard_map/ppermute | solution.py:36
  106.2 3.1 %collective-permute-start.20 = (bf16[7,128,128]{2,1,0:T(8,128)(2,1)S(1)}, bf16[7,128,128]{2,1,0:T(8,128)(2,1)S(1)}, u32[]{:S(2)}, u32[]{:S(2)}) collective-permute-start(bf16[7,128,128]{2,1,0:T(8,128)(2,1)S(1)} %pad_maximum_fusion.8), channel_id=1, source_target_pairs={{0,224},{8,232},{16,240},{24,248},{32,0},{40,8},{48,16},{56,24},{6... | collective-permute-start | bytes 688136 | tf_op jit(solution)/shard_map/ppermute | solution.py:36
  109.3 4.8 %collective-permute-done.20 = bf16[7,128,128]{2,1,0:T(8,128)(2,1)S(1)} collective-permute-done((bf16[7,128,128]{2,1,0:T(8,128)(2,1)S(1)}, bf16[7,128,128]{2,1,0:T(8,128)(2,1)S(1)}, u32[]{:S(2)}, u32[]{:S(2)}) %collective-permute-start.20) | collective-permute-done | bytes 229408 | tf_op jit(solution)/shard_map/ppermute | solution.py:36
  114.2 3.4 %collective-permute-done.19 = bf16[7,128,128]{2,1,0:T(8,128)(2,1)S(1)} collective-permute-done((bf16[7,128,128]{2,1,0:T(8,128)(2,1)S(1)}, bf16[7,128,128]{2,1,0:T(8,128)(2,1)S(1)}, u32[]{:S(2)}, u32[]{:S(2)}) %collective-permute-start.19) | collective-permute-done | bytes 229408 | tf_op jit(solution)/shard_map/ppermute | solution.py:36
  119.0 2.3 %collective-permute-start.22 = (bf16[9,128,128]{2,1,0:T(8,128)(2,1)S(1)}, bf16[9,128,128]{2,1,0:T(8,128)(2,1)S(1)}, u32[]{:S(2)}, u32[]{:S(2)}) collective-permute-start(bf16[9,128,128]{2,1,0:T(8,128)(2,1)S(1)} %pad_maximum_fusion.2), channel_id=1, source_target_pairs={{0,224},{8,232},{16,240},{24,248},{32,0},{40,8},{48,16},{56,24},{6... | collective-permute-start | bytes 884744 | tf_op jit(solution)/shard_map/ppermute | solution.py:36
  121.3 5.5 %collective-permute-done.21 = bf16[9,128,128]{2,1,0:T(8,128)(2,1)S(1)} collective-permute-done((bf16[9,128,128]{2,1,0:T(8,128)(2,1)S(1)}, bf16[9,128,128]{2,1,0:T(8,128)(2,1)S(1)}, u32[]{:S(2)}, u32[]{:S(2)}) %collective-permute-start.21) | collective-permute-done | bytes 294944 | tf_op jit(solution)/shard_map/ppermute | solution.py:36
  128.6 2.3 %collective-permute-start.23 = (bf16[9,128,128]{2,1,0:T(8,128)(2,1)}, bf16[9,128,128]{2,1,0:T(8,128)(2,1)S(1)}, u32[]{:S(2)}, u32[]{:S(2)}) collective-permute-start(bf16[9,128,128]{2,1,0:T(8,128)(2,1)} %pad_maximum_fusion.3), channel_id=1, source_target_pairs={{0,32},{8,40},{16,48},{24,56},{32,64},{40,72},{48,80},{56,88},{64,... | collective-permute-start | bytes 884744 | tf_op jit(solution)/shard_map/ppermute | solution.py:36
  131.8 4.9 %collective-permute-done.23 = bf16[9,128,128]{2,1,0:T(8,128)(2,1)S(1)} collective-permute-done((bf16[9,128,128]{2,1,0:T(8,128)(2,1)}, bf16[9,128,128]{2,1,0:T(8,128)(2,1)S(1)}, u32[]{:S(2)}, u32[]{:S(2)}) %collective-permute-start.23) | collective-permute-done | bytes 294944 | tf_op jit(solution)/shard_map/ppermute | solution.py:36
  138.8 1.2 fusion.2
  140.0 5.6 %collective-permute-start.25 = (bf16[6,128,128]{2,1,0:T(8,128)(2,1)S(1)}, bf16[6,128,128]{2,1,0:T(8,128)(2,1)S(1)}, u32[]{:S(2)}, u32[]{:S(2)}) collective-permute-start(bf16[6,128,128]{2,1,0:T(8,128)(2,1)S(1)} %pad_maximum_fusion.9), channel_id=1, source_target_pairs={{0,16},{8,24},{16,0},{24,8},{32,48},{40,56},{48,32},{56,40},{64,80... | collective-permute-start | bytes 589832 | tf_op jit(solution)/shard_map/ppermute | solution.py:40
  145.6 2.1 %collective-permute-start.27 = (bf16[4,128,128]{2,1,0:T(8,128)(2,1)S(1)}, bf16[4,128,128]{2,1,0:T(8,128)(2,1)S(1)}, u32[]{:S(2)}, u32[]{:S(2)}) collective-permute-start(bf16[4,128,128]{2,1,0:T(8,128)(2,1)S(1)} %get-tuple-element.30), channel_id=1, source_target_pairs={{0,224},{8,232},{16,240},{24,248},{32,0},{40,8},{48,16},{56,24},{6... | collective-permute-start | bytes 393224 | tf_op jit(solution)/shard_map/ppermute | solution.py:36
  147.8 1.5 collective-permute-done.25
  150.6 3.4 %collective-permute-done.26 = bf16[4,128,128]{2,1,0:T(8,128)(2,1)S(1)} collective-permute-done((bf16[4,128,128]{2,1,0:T(8,128)(2,1)S(1)}, bf16[4,128,128]{2,1,0:T(8,128)(2,1)S(1)}, u32[]{:S(2)}, u32[]{:S(2)}) %collective-permute-start.26) | collective-permute-done | bytes 131104 | tf_op jit(solution)/shard_map/ppermute | solution.py:36
  154.0 1.8 %convolution_convert_fusion = bf16[4,128,128]{2,1,0:T(8,128)(2,1)} fusion(bf16[4,128,128]{2,1,0:T(8,128)(2,1)S(1)} %collective-permute-done.27, bf16[4,128,128]{2,1,0:T(8,128)(2,1)S(1)} %collective-permute-done.26, bf16[6,128,128]{2,1,0:T(8,128)(2,1)S(1)} %collective-permute-done.25, bf16[66,128,128]{2,1,0:T(8,128)(2,1)} %copy-done.1, ...), kind=kOutput, calls=%fused_computation.2 | convolution fusion | flops 17498112 | bytes 819200 | tf_op jit(solution)/shard_map/khb,ih->kbi/dot_general | solution.py:308
  (98 shorter events, 16.1 us)
Async XLA Ops:
  0.6 67.4 %copy-start = (bf16[128,128]{1,0:T(8,128)(2,1)S(1)}, bf16[128,128]{1,0:T(8,128)(2,1)}, u32[]{:S(2)}) copy-start(bf16[128,128]{1,0:T(8,128)(2,1)} %param.7) | copy-start | bytes 98308
  0.6 9.0 %collective-permute-start.2 = (bf16[4,128,128]{2,1,0:T(8,128)(2,1)}, bf16[4,128,128]{2,1,0:T(8,128)(2,1)S(1)}, u32[]{:S(2)}, u32[]{:S(2)}) collective-permute-start(bf16[4,128,128]{2,1,0:T(8,128)(2,1)} %bitcast.190), channel_id=1, source_target_pairs={{0,224},{8,232},{16,240},{24,248},{32,0},{40,8},{48,16},{56,24},{6... | collective-permute-start | bytes 393224 | tf_op jit(solution)/shard_map/ppermute | solution.py:36
  6.6 6.4 %collective-permute-start.1 = (bf16[4,128,128]{2,1,0:T(8,128)(2,1)}, bf16[4,128,128]{2,1,0:T(8,128)(2,1)S(1)}, u32[]{:S(2)}, u32[]{:S(2)}) collective-permute-start(bf16[4,128,128]{2,1,0:T(8,128)(2,1)} %bitcast.191), channel_id=1, source_target_pairs={{0,32},{8,40},{16,48},{24,56},{32,64},{40,72},{48,80},{56,88},{64,... | collective-permute-start | bytes 393224 | tf_op jit(solution)/shard_map/ppermute | solution.py:36
  6.6 6.7 %collective-permute-start = (bf16[4,128,128]{2,1,0:T(8,128)(2,1)}, bf16[4,128,128]{2,1,0:T(8,128)(2,1)S(1)}, u32[]{:S(2)}, u32[]{:S(2)}) collective-permute-start(bf16[4,128,128]{2,1,0:T(8,128)(2,1)} %bitcast.192), channel_id=1, source_target_pairs={{0,16},{8,24},{16,0},{24,8},{32,48},{40,56},{48,32},{56,40},{64,80... | collective-permute-start | bytes 393224 | tf_op jit(solution)/shard_map/ppermute | solution.py:40
  13.3 7.9 %collective-permute-start.3 = (bf16[8,128,128]{2,1,0:T(8,128)(2,1)S(1)}, bf16[8,128,128]{2,1,0:T(8,128)(2,1)S(1)}, u32[]{:S(2)}, u32[]{:S(2)}) collective-permute-start(bf16[8,128,128]{2,1,0:T(8,128)(2,1)S(1)} %get-tuple-element.57), channel_id=1, source_target_pairs={{0,32},{8,40},{16,48},{24,56},{32,64},{40,72},{48,80},{56,88},{64,... | collective-permute-start | bytes 786440 | tf_op jit(solution)/shard_map/ppermute | solution.py:36
  13.4 7.8 %collective-permute-start.4 = (bf16[8,128,128]{2,1,0:T(8,128)(2,1)S(1)}, bf16[8,128,128]{2,1,0:T(8,128)(2,1)S(1)}, u32[]{:S(2)}, u32[]{:S(2)}) collective-permute-start(bf16[8,128,128]{2,1,0:T(8,128)(2,1)S(1)} %get-tuple-element.56), channel_id=1, source_target_pairs={{0,224},{8,232},{16,240},{24,248},{32,0},{40,8},{48,16},{56,24},{6... | collective-permute-start | bytes 786440 | tf_op jit(solution)/shard_map/ppermute | solution.py:36
  21.2 7.6 %collective-permute-start.5 = (bf16[8,128,128]{2,1,0:T(8,128)(2,1)S(1)}, bf16[8,128,128]{2,1,0:T(8,128)(2,1)S(1)}, u32[]{:S(2)}, u32[]{:S(2)}) collective-permute-start(bf16[8,128,128]{2,1,0:T(8,128)(2,1)S(1)} %collective-permute-done.3), channel_id=1, source_target_pairs={{0,32},{8,40},{16,48},{24,56},{32,64},{40,72},{48,80},{56,88},{64,... | collective-permute-start | bytes 786440 | tf_op jit(solution)/shard_map/ppermute | solution.py:36
  21.2 7.7 %collective-permute-start.6 = (bf16[8,128,128]{2,1,0:T(8,128)(2,1)S(1)}, bf16[8,128,128]{2,1,0:T(8,128)(2,1)S(1)}, u32[]{:S(2)}, u32[]{:S(2)}) collective-permute-start(bf16[8,128,128]{2,1,0:T(8,128)(2,1)S(1)} %collective-permute-done.4), channel_id=1, source_target_pairs={{0,224},{8,232},{16,240},{24,248},{32,0},{40,8},{48,16},{56,24},{6... | collective-permute-start | bytes 786440 | tf_op jit(solution)/shard_map/ppermute | solution.py:36
  25.4 16.7 %collective-permute-start.11 = (bf16[16,128,128]{2,1,0:T(8,128)(2,1)S(1)}, bf16[16,128,128]{2,1,0:T(8,128)(2,1)S(1)}, u32[]{:S(2)}, u32[]{:S(2)}) collective-permute-start(bf16[16,128,128]{2,1,0:T(8,128)(2,1)S(1)} %pad_maximum_fusion.refs_0_), channel_id=1, source_target_pairs={{0,8},{8,0},{16,24},{24,16},{32,40},{40,32},{48,56},{56,48},{64,72... | collective-permute-start | bytes 1572872 | tf_op jit(solution)/shard_map/ppermute | solution.py:40
  25.6 16.5 %collective-permute-start.12 = (bf16[16,128,128]{2,1,0:T(8,128)(2,1)S(1)}, bf16[16,128,128]{2,1,0:T(8,128)(2,1)S(1)}, u32[]{:S(2)}, u32[]{:S(2)}) collective-permute-start(bf16[16,128,128]{2,1,0:T(8,128)(2,1)S(1)} %constant_dynamic-update-slice_fusion.refs_1_), channel_id=1, source_target_pairs={{0,8},{8,0},{16,24},{24,16},{32,40},{40,32},{48,56},{56,48},{64,72... | collective-permute-start | bytes 1572872 | tf_op jit(solution)/shard_map/ppermute | solution.py:40
  28.8 7.0 %collective-permute-start.7 = (bf16[6,128,128]{2,1,0:T(8,128)(2,1)S(1)}, bf16[6,128,128]{2,1,0:T(8,128)(2,1)S(1)}, u32[]{:S(2)}, u32[]{:S(2)}) collective-permute-start(bf16[6,128,128]{2,1,0:T(8,128)(2,1)S(1)} %slice.307), channel_id=1, source_target_pairs={{0,32},{8,40},{16,48},{24,56},{32,64},{40,72},{48,80},{56,88},{64,... | collective-permute-start | bytes 589832 | tf_op jit(solution)/shard_map/ppermute | solution.py:36
  28.9 6.9 %collective-permute-start.8 = (bf16[6,128,128]{2,1,0:T(8,128)(2,1)S(1)}, bf16[6,128,128]{2,1,0:T(8,128)(2,1)S(1)}, u32[]{:S(2)}, u32[]{:S(2)}) collective-permute-start(bf16[6,128,128]{2,1,0:T(8,128)(2,1)S(1)} %slice.308), channel_id=1, source_target_pairs={{0,224},{8,232},{16,240},{24,248},{32,0},{40,8},{48,16},{56,24},{6... | collective-permute-start | bytes 589832 | tf_op jit(solution)/shard_map/ppermute | solution.py:36
  32.3 10.9 %collective-permute-start.13 = (bf16[16,128,128]{2,1,0:T(8,128)(2,1)S(1)}, bf16[16,128,128]{2,1,0:T(8,128)(2,1)S(1)}, u32[]{:S(2)}, u32[]{:S(2)}) collective-permute-start(bf16[16,128,128]{2,1,0:T(8,128)(2,1)S(1)} %constant_dynamic-update-slice_fusion.2.refs_2_), channel_id=1, source_target_pairs={{0,8},{8,0},{16,24},{24,16},{32,40},{40,32},{48,56},{56,48},{64,72... | collective-permute-start | bytes 1572872 | tf_op jit(solution)/shard_map/ppermute | solution.py:40
  35.8 5.5 %collective-permute-start.9 = (bf16[2,128,128]{2,1,0:T(8,128)(2,1)S(1)}, bf16[2,128,128]{2,1,0:T(8,128)(2,1)S(1)}, u32[]{:S(2)}, u32[]{:S(2)}) collective-permute-start(bf16[2,128,128]{2,1,0:T(8,128)(2,1)S(1)} %slice.309), channel_id=1, source_target_pairs={{0,32},{8,40},{16,48},{24,56},{32,64},{40,72},{48,80},{56,88},{64,... | collective-permute-start | bytes 196616 | tf_op jit(solution)/shard_map/ppermute | solution.py:36
  35.8 5.5 %collective-permute-start.10 = (bf16[2,128,128]{2,1,0:T(8,128)(2,1)S(1)}, bf16[2,128,128]{2,1,0:T(8,128)(2,1)S(1)}, u32[]{:S(2)}, u32[]{:S(2)}) collective-permute-start(bf16[2,128,128]{2,1,0:T(8,128)(2,1)S(1)} %slice.310), channel_id=1, source_target_pairs={{0,224},{8,232},{16,240},{24,248},{32,0},{40,8},{48,16},{56,24},{6... | collective-permute-start | bytes 196616 | tf_op jit(solution)/shard_map/ppermute | solution.py:36
  41.3 1.9 %collective-permute-start.14 = (bf16[12,128,128]{2,1,0:T(8,128)(2,1)S(1)}, bf16[12,128,128]{2,1,0:T(8,128)(2,1)S(1)}, u32[]{:S(2)}, u32[]{:S(2)}) collective-permute-start(bf16[12,128,128]{2,1,0:T(8,128)(2,1)S(1)} %constant_dynamic-update-slice_fusion.4.refs_3_), channel_id=1, source_target_pairs={{0,8},{8,0},{16,24},{24,16},{32,40},{40,32},{48,56},{56,48},{64,72... | collective-permute-start | bytes 1179656 | tf_op jit(solution)/shard_map/ppermute | solution.py:40
  41.3 1.9 %collective-permute-start.15 = (bf16[4,128,128]{2,1,0:T(8,128)(2,1)S(1)}, bf16[4,128,128]{2,1,0:T(8,128)(2,1)S(1)}, u32[]{:S(2)}, u32[]{:S(2)}) collective-permute-start(bf16[4,128,128]{2,1,0:T(8,128)(2,1)S(1)} %constant_dynamic-update-slice_fusion.6.refs_4_), channel_id=1, source_target_pairs={{0,8},{8,0},{16,24},{24,16},{32,40},{40,32},{48,56},{56,48},{64,72... | collective-permute-start | bytes 393224 | tf_op jit(solution)/shard_map/ppermute | solution.py:40
  47.4 20.8 %copy-start.4 = (bf16[512,128]{1,0:T(8,128)(2,1)S(1)}, bf16[512,128]{1,0:T(8,128)(2,1)}, u32[]{:S(2)}) copy-start(bf16[512,128]{1,0:T(8,128)(2,1)} %param.11) | copy-start | bytes 393220
  94.6 4.3 %collective-permute-start.16 = (bf16[66,128,128]{2,1,0:T(8,128)(2,1)S(1)}, bf16[66,128,128]{2,1,0:T(8,128)(2,1)S(1)}, u32[]{:S(2)}, u32[]{:S(2)}) collective-permute-start(bf16[66,128,128]{2,1,0:T(8,128)(2,1)S(1)} %get-tuple-element.18), channel_id=1, source_target_pairs={{0,8},{8,0},{16,24},{24,16},{32,40},{40,32},{48,56},{56,48},{64,72... | collective-permute-start | bytes 6488072 | tf_op jit(solution)/shard_map/ppermute | solution.py:40
  99.0 27.9 %copy-start.1 = (bf16[66,128,128]{2,1,0:T(8,128)(2,1)}, bf16[66,128,128]{2,1,0:T(8,128)(2,1)S(1)}, u32[]{:S(2)}) copy-start(bf16[66,128,128]{2,1,0:T(8,128)(2,1)S(1)} %collective-permute-done.16) | copy-start | bytes 6488068
  99.1 6.3 %collective-permute-start.17 = (bf16[3,128,128]{2,1,0:T(8,128)(2,1)S(1)}, bf16[3,128,128]{2,1,0:T(8,128)(2,1)S(1)}, u32[]{:S(2)}, u32[]{:S(2)}) collective-permute-start(bf16[3,128,128]{2,1,0:T(8,128)(2,1)S(1)} %get-tuple-element.20), channel_id=1, source_target_pairs={{0,32},{8,40},{16,48},{24,56},{32,64},{40,72},{48,80},{56,88},{64,... | collective-permute-start | bytes 294920 | tf_op jit(solution)/shard_map/ppermute | solution.py:36
  100.5 4.9 %collective-permute-start.18 = (bf16[3,128,128]{2,1,0:T(8,128)(2,1)S(1)}, bf16[3,128,128]{2,1,0:T(8,128)(2,1)S(1)}, u32[]{:S(2)}, u32[]{:S(2)}) collective-permute-start(bf16[3,128,128]{2,1,0:T(8,128)(2,1)S(1)} %get-tuple-element.21), channel_id=1, source_target_pairs={{0,224},{8,232},{16,240},{24,248},{32,0},{40,8},{48,16},{56,24},{6... | collective-permute-start | bytes 294920 | tf_op jit(solution)/shard_map/ppermute | solution.py:36
  106.0 11.6 %copy-start.3 = (bf16[3,128,128]{2,1,0:T(8,128)(2,1)}, bf16[3,128,128]{2,1,0:T(8,128)(2,1)S(1)}, u32[]{:S(2)}) copy-start(bf16[3,128,128]{2,1,0:T(8,128)(2,1)S(1)} %collective-permute-done.18) | copy-start | bytes 294916
  106.2 8.0 %collective-permute-start.20 = (bf16[7,128,128]{2,1,0:T(8,128)(2,1)S(1)}, bf16[7,128,128]{2,1,0:T(8,128)(2,1)S(1)}, u32[]{:S(2)}, u32[]{:S(2)}) collective-permute-start(bf16[7,128,128]{2,1,0:T(8,128)(2,1)S(1)} %pad_maximum_fusion.8), channel_id=1, source_target_pairs={{0,224},{8,232},{16,240},{24,248},{32,0},{40,8},{48,16},{56,24},{6... | collective-permute-start | bytes 688136 | tf_op jit(solution)/shard_map/ppermute | solution.py:36
  109.3 8.2 %collective-permute-start.19 = (bf16[7,128,128]{2,1,0:T(8,128)(2,1)S(1)}, bf16[7,128,128]{2,1,0:T(8,128)(2,1)S(1)}, u32[]{:S(2)}, u32[]{:S(2)}) collective-permute-start(bf16[7,128,128]{2,1,0:T(8,128)(2,1)S(1)} %pad_maximum_fusion.7), channel_id=1, source_target_pairs={{0,32},{8,40},{16,48},{24,56},{32,64},{40,72},{48,80},{56,88},{64,... | collective-permute-start | bytes 688136 | tf_op jit(solution)/shard_map/ppermute | solution.py:36
  118.0 8.8 %collective-permute-start.21 = (bf16[9,128,128]{2,1,0:T(8,128)(2,1)S(1)}, bf16[9,128,128]{2,1,0:T(8,128)(2,1)S(1)}, u32[]{:S(2)}, u32[]{:S(2)}) collective-permute-start(bf16[9,128,128]{2,1,0:T(8,128)(2,1)S(1)} %pad_maximum_fusion.1), channel_id=1, source_target_pairs={{0,32},{8,40},{16,48},{24,56},{32,64},{40,72},{48,80},{56,88},{64,... | collective-permute-start | bytes 884744 | tf_op jit(solution)/shard_map/ppermute | solution.py:36
  119.0 7.8 %collective-permute-start.22 = (bf16[9,128,128]{2,1,0:T(8,128)(2,1)S(1)}, bf16[9,128,128]{2,1,0:T(8,128)(2,1)S(1)}, u32[]{:S(2)}, u32[]{:S(2)}) collective-permute-start(bf16[9,128,128]{2,1,0:T(8,128)(2,1)S(1)} %pad_maximum_fusion.2), channel_id=1, source_target_pairs={{0,224},{8,232},{16,240},{24,248},{32,0},{40,8},{48,16},{56,24},{6... | collective-permute-start | bytes 884744 | tf_op jit(solution)/shard_map/ppermute | solution.py:36
  128.6 8.1 %collective-permute-start.23 = (bf16[9,128,128]{2,1,0:T(8,128)(2,1)}, bf16[9,128,128]{2,1,0:T(8,128)(2,1)S(1)}, u32[]{:S(2)}, u32[]{:S(2)}) collective-permute-start(bf16[9,128,128]{2,1,0:T(8,128)(2,1)} %pad_maximum_fusion.3), channel_id=1, source_target_pairs={{0,32},{8,40},{16,48},{24,56},{32,64},{40,72},{48,80},{56,88},{64,... | collective-permute-start | bytes 884744 | tf_op jit(solution)/shard_map/ppermute | solution.py:36
  130.9 7.9 %collective-permute-start.24 = (bf16[9,128,128]{2,1,0:T(8,128)(2,1)}, bf16[9,128,128]{2,1,0:T(8,128)(2,1)S(1)}, u32[]{:S(2)}, u32[]{:S(2)}) collective-permute-start(bf16[9,128,128]{2,1,0:T(8,128)(2,1)} %pad_maximum_fusion.4), channel_id=1, source_target_pairs={{0,224},{8,232},{16,240},{24,248},{32,0},{40,8},{48,16},{56,24},{6... | collective-permute-start | bytes 884744 | tf_op jit(solution)/shard_map/ppermute | solution.py:36
  140.0 9.3 %collective-permute-start.25 = (bf16[6,128,128]{2,1,0:T(8,128)(2,1)S(1)}, bf16[6,128,128]{2,1,0:T(8,128)(2,1)S(1)}, u32[]{:S(2)}, u32[]{:S(2)}) collective-permute-start(bf16[6,128,128]{2,1,0:T(8,128)(2,1)S(1)} %pad_maximum_fusion.9), channel_id=1, source_target_pairs={{0,16},{8,24},{16,0},{24,8},{32,48},{40,56},{48,32},{56,40},{64,80... | collective-permute-start | bytes 589832 | tf_op jit(solution)/shard_map/ppermute | solution.py:40
  145.6 5.0 %collective-permute-start.27 = (bf16[4,128,128]{2,1,0:T(8,128)(2,1)S(1)}, bf16[4,128,128]{2,1,0:T(8,128)(2,1)S(1)}, u32[]{:S(2)}, u32[]{:S(2)}) collective-permute-start(bf16[4,128,128]{2,1,0:T(8,128)(2,1)S(1)} %get-tuple-element.30), channel_id=1, source_target_pairs={{0,224},{8,232},{16,240},{24,248},{32,0},{40,8},{48,16},{56,24},{6... | collective-permute-start | bytes 393224 | tf_op jit(solution)/shard_map/ppermute | solution.py:36
  147.8 6.2 %collective-permute-start.26 = (bf16[4,128,128]{2,1,0:T(8,128)(2,1)S(1)}, bf16[4,128,128]{2,1,0:T(8,128)(2,1)S(1)}, u32[]{:S(2)}, u32[]{:S(2)}) collective-permute-start(bf16[4,128,128]{2,1,0:T(8,128)(2,1)S(1)} %get-tuple-element.29), channel_id=1, source_target_pairs={{0,32},{8,40},{16,48},{24,56},{32,64},{40,72},{48,80},{56,88},{64,... | collective-permute-start | bytes 393224 | tf_op jit(solution)/shard_map/ppermute | solution.py:36
  (1 other events, 0.6 us)

commit v2 on v1

--- a/solution.py
+++ b/solution.py
@@ -10,7 +10,7 @@
 BPD = 4
 HALF = 2
 CHUNK = 32
-UNROLL = 16
+UNROLL = 32
 VMEM_LIMIT = 24 << 20
 BF = jnp.bfloat16
 F32 = jnp.float32
@@ -18,6 +18,13 @@
 PLACES = ((0, 4), (8, 16), (20, 32), (36, 48), (52, 60), (40, 56), (24, 44), (12, 28))
 
 
+ORDER = (
+    (4, 1), (3, 1), (5, 1), (4, 0), (2, 1), (6, 1), (3, 0), (5, 0),
+    (1, 1), (7, 1), (2, 0), (6, 0), (0, 1), (1, 0), (7, 0), (0, 0),
+)
+SOON = 4 * BPD
+
+
 def silu_grad(values):
     sigmoid_z = jax.nn.sigmoid(values)
     return sigmoid_z * (1.0 + values * (1.0 - sigmoid_z))
@@ -41,8 +48,8 @@
 
 
 def split(value):
-    high = value.astype(BF)
-    return high, (value - wide(high)).astype(BF)
+    high = lax.reduce_precision(value, 8, 7)
+    return high.astype(BF), (value - high).astype(BF)
 
 
 def add_products(x_first, dst, src, count, blocks, held, acc, slots, sems):
@@ -93,7 +100,12 @@
     out[...] = acc[: out.shape[0]].astype(out.dtype)
 
 
-def backward_kernel(dst, src, count, blocks, every, keep, send, sums, acc, slots, sems):
+def split_here(value):
+    high = value.astype(BF)
+    return high, (value - wide(high)).astype(BF)
+
+
+def backward_kernel(dst, src, count, blocks, every, keep, soon, later, sums, acc, slots, sems):
     for c in range(slots.shape[0] // CHUNK):
         load(blocks, slots, sems, c).start()
     acc[...] = jnp.zeros_like(acc)
@@ -101,13 +113,14 @@
     total = wide(every[BPD])
     for k in range(1, every.shape[0] // span):
         total = total + wide(every[k * span + BPD])
-    high, low = split(total)
+    high, low = split_here(total)
     half = keep.shape[0]
-    send[half], send[half + 1] = high, low
+    soon[SOON], soon[SOON + 1] = high, low
     sums[...] = wide(high) + wide(low)
     add_products(True, dst, src, count, blocks, every, acc, slots, sems)
     keep[...] = acc[:half].astype(keep.dtype)
-    send[:half] = acc[half : 2 * half].astype(send.dtype)
+    soon[:SOON] = acc[half : half + SOON].astype(soon.dtype)
+    later[...] = acc[half + SOON : 2 * half].astype(later.dtype)
 
 
 def product(kernel, name, blocks, dst, src, count, sources, out_shape, source_space, scratch):
@@ -167,7 +180,8 @@
         [every],
         [
             jax.ShapeDtypeStruct((half, BLK, BLK), BF),
-            jax.ShapeDtypeStruct((half + 2, BLK, BLK), BF),
+            jax.ShapeDtypeStruct((SOON + 2, BLK, BLK), BF),
+            jax.ShapeDtypeStruct((half - SOON, BLK, BLK), BF),
             jax.ShapeDtypeStruct((BLK, BLK), F32),
         ],
         pltpu.VMEM,
@@ -179,6 +193,41 @@
     )
 
 
+def middle_kernel(parts, weight, cotangent, activated, message):
+    dot = lambda a, b: jnp.dot(a, b, preferred_element_type=F32)
+    spread = wide(parts[0])
+    for k in range(1, parts.shape[0]):
+        spread = spread + wide(parts[k])
+    high, low = split_here(spread)
+    preact = dot(high, weight[...]) + dot(low, weight[...])
+    activated[...] = (preact * jax.nn.sigmoid(preact)).astype(BF)
+    delta = wide(cotangent[...]) * silu_grad(preact)
+    rounded = delta.astype(BF)
+    blocks = [delta[b * BLK : (b + 1) * BLK].T.astype(BF) for b in range(BPD)]
+    blocks.append((dot(high.T, rounded) + dot(low.T, rounded)).astype(BF))
+    for k in range(message.shape[0]):
+        for b, block in enumerate(blocks):
+            message[k, b] = block
+
+
+def middle(parts, weight, cotangent):
+    vmem = pl.BlockSpec(memory_space=pltpu.VMEM)
+    return pl.pallas_call(
+        middle_kernel,
+        name="middle",
+        in_specs=[vmem] * 3,
+        out_specs=[vmem] * 2,
+        out_shape=[
+            jax.ShapeDtypeStruct(cotangent.shape, BF),
+            jax.ShapeDtypeStruct((parts.shape[0], BPD + 1, BLK, BLK), BF),
+        ],
+        compiler_params=pltpu.CompilerParams(vmem_limit_bytes=VMEM_LIMIT),
+        cost_estimate=pl.CostEstimate(
+            flops=8 * cotangent.size * BLK, bytes_accessed=4 << 20, transcendentals=cotangent.size
+        ),
+    )(parts, weight, cotangent)
+
+
 def gather_rows(own):
     mate = row_swap(own, 2)
     up1, down1 = z_shift(own, 1), z_shift(own, -1)
@@ -186,34 +235,31 @@
     up3, down3 = z_shift(up2, 1), z_shift(down2, -1)
     up4, down4 = z_shift(up3[: BPD + HALF], 1), z_shift(down3[HALF:], -1)
     up5, down5 = z_shift(up4[:HALF], 1), z_shift(down4[BPD:], -1)
-    groups = [
-        cat(own, mate, up1, down1),
-        cat(up2, down2),
-        cat(up3, down3),
-        cat(up4, down4),
-        cat(up5, down5),
-    ]
+    groups = [cat(own, mate, up1, down1), cat(up2, down2), cat(up3, down3)]
+    groups, up4, down4 = lax.optimization_barrier((groups, up4, down4))
+    groups += [cat(up4, down4), cat(up5, down5)]
     return groups + [row_swap(group, 1) for group in groups]
 
 
-def scatter_rows(keep, send, sums):
-    arrived = row_swap(send, 1)
-    half = keep.shape[0]
-    tag = (sums + wide(arrived[half]) + wide(arrived[half + 1])).astype(BF)[None]
+def scatter_rows(keep, soon, later, sums):
+    soon, later = row_swap(soon, 1), row_swap(later, 1)
+    tag = (sums + wide(soon[SOON]) + wide(soon[SOON + 1])).astype(BF)[None]
     seen_up, seen_down = [], []
 
     def term(d, x, lo=0, hi=BPD):
-        at = (2 * d + x) * BPD
-        return wide(keep[at + lo : at + hi]) + wide(arrived[at + lo : at + hi])
-
-    def step(up, down, up_tag, down_tag):
+        at = ORDER.index((d, x)) * BPD
+        arrived, first = (soon, at) if at < SOON else (later, at - SOON)
+        return wide(keep[at + lo : at + hi]) + wide(arrived[first + lo : first + hi])
+
+    def step(up, down, up_tag, down_tag, ahead=()):
         up = cat(*[part.astype(BF) for part in up], up_tag)
         down = cat(*[part.astype(BF) for part in down], down_tag)
-        up, down = lax.optimization_barrier((up, down))
+        up, down, ahead = lax.optimization_barrier((up, down, ahead))
         up, down = z_shift(up, 1), z_shift(down, -1)
-        seen_up.append(up[-1:])
-        seen_down.append(down[-1:])
-        return wide(up[:-1]), wide(down[:-1]), up[-1:], down[-1:]
+        up_tag, down_tag = lax.optimization_barrier((up[-1:], down[-1:]))
+        seen_up.append(up_tag)
+        seen_down.append(down_tag)
+        return wide(up[:-1]), wide(down[:-1]), up_tag, down_tag, ahead
 
     def front(value):
         return jnp.pad(value, ((0, HALF), (0, 0), (0, 0)))
@@ -221,24 +267,26 @@
     def back(value):
         return jnp.pad(value, ((HALF, 0), (0, 0), (0, 0)))
 
-    up, down, ut, dt = step([term(4, 1, 0, HALF)], [term(4, 1, HALF)], tag, tag)
-    up, down, ut, dt = step(
+    up, down, ut, dt, _ = step([term(4, 1, 0, HALF)], [term(4, 1, HALF)], tag, tag)
+    up, down, ut, dt, _ = step(
         [term(3, 1) + front(up), term(4, 0, 0, HALF)],
         [term(4, 0, HALF), term(5, 1) + back(down)],
         ut,
         dt,
     )
-    up, down, ut, dt = step(
+    up, down, ut, dt, ahead = step(
         [term(2, 1) + up[:BPD], term(3, 0) + front(up[BPD:])],
         [term(5, 0) + back(down[:HALF]), term(6, 1) + down[HALF:]],
         ut,
         dt,
-    )
-    up, down, ut, dt = step(
-        [term(1, 1) + up[:BPD], term(2, 0) + up[BPD:]],
-        [term(6, 0) + down[:BPD], term(7, 1) + down[BPD:]],
+        [term(1, 1), term(2, 0), term(6, 0), term(7, 1)],
+    )
+    up, down, ut, dt, ahead = step(
+        [ahead[0] + up[:BPD], ahead[1] + up[BPD:]],
+        [ahead[2] + down[:BPD], ahead[3] + down[BPD:]],
         ut,
         dt,
+        [term(0, 1), term(1, 0), term(7, 0), term(0, 0)],
     )
     near = [tag] + seen_up + seen_down[: NZ // 2 - 1][::-1]
     z = lax.axis_index("row") // 4
@@ -249,14 +297,14 @@
         for n in range(1, NZ):
             chosen = jnp.where(d == n, near[n][0], chosen)
         summed = summed + wide(chosen)
-    high, low = split(summed)
-    theirs = term(0, 1) + up[:BPD] + down[BPD:]
+    high, low = lax.optimization_barrier(split(summed))
+    theirs = ahead[0] + up[:BPD] + down[BPD:]
+    up = (ahead[1] + up[BPD:]).astype(BF)
+    down = (ahead[2] + down[:BPD]).astype(BF)
+    up, down = lax.optimization_barrier((up, down))
     theirs = cat(theirs.astype(BF), high[None], low[None])
-    up = (term(1, 0) + up[BPD:]).astype(BF)
-    down = (term(7, 0) + down[:BPD]).astype(BF)
-    theirs, up, down = lax.optimization_barrier((theirs, up, down))
     mate, up, down = row_swap(theirs, 2), z_shift(up, 1), z_shift(down, -1)
-    total = term(0, 0) + wide(mate[:BPD]) + wide(up) + wide(down)
+    total = ahead[3] + wide(mate[:BPD]) + wide(up) + wide(down)
     return total, (wide(high) + wide(low)) + (wide(mate[BPD]) + wide(mate[BPD + 1]))
 
 
@@ -270,7 +318,6 @@
     row_blocks = col_devices * BPD
     col_blocks = row_devices * BPD
     nodes = features.shape[0]
-    dot = lambda a, b: jnp.dot(a, b, preferred_element_type=F32)
 
     me = lax.axis_index("row")
     owner = coords[1] // BPD
@@ -281,7 +328,10 @@
     from_place = core_part + inner
     for k, place in enumerate(place for pair in PLACES for place in pair):
         from_place = from_place + jnp.where(distance == k, place, 0)
-    to_place = core_part + (((owner // 4 - me // 4) % NZ) * 2 + (apart >> 1)) * BPD + inner
+    to_place = core_part + inner
+    toward = (owner // 4 - me // 4) % NZ * 2 + (apart >> 1)
+    for k, (d, x) in enumerate(ORDER):
+        to_place = to_place + jnp.where(toward == 2 * d + x, k * BPD, 0)
     live = jnp.arange(slots, dtype=jnp.int32) < count[0]
     forward_dst = jnp.where(live, coords[0], row_blocks)
     backward_dst = jnp.where(live, to_place, col_blocks)
@@ -290,22 +340,14 @@
     pieces = gather_rows(features.reshape(BPD, BLK, BLK))
     partial = forward_product(blocks, forward_dst, from_place, count, pieces, row_blocks)
     parts = lax.all_to_all(partial.reshape(col_devices, nodes, BLK), "col", 0, 0)
-    spread = jnp.sum(wide(parts), axis=0)
-    high, low = split(spread)
-    preact = dot(high, weight) + dot(low, weight)
-    activated = jax.nn.silu(preact).astype(BF)
-    delta = (wide(cotangent) * silu_grad(preact)).astype(BF)
-    delta_t = jnp.swapaxes(delta.reshape(BPD, BLK, BLK), 1, 2)
-
-    weight_part = (dot(high.T, delta) + dot(low.T, delta)).astype(BF)
-    message = cat(delta_t, weight_part[None])
-    every = lax.all_to_all(
-        jnp.broadcast_to(message[None], (col_devices,) + message.shape), "col", 0, 0
-    ).reshape(-1, BLK, BLK)
-    keep, send, sums = backward_product(blocks, backward_dst, delta_at, count, every, col_blocks)
-    total, weight_sum = scatter_rows(keep, send, sums)
+    activated, message = middle(parts, weight, cotangent)
+    every = lax.all_to_all(message, "col", 0, 0).reshape(-1, BLK, BLK)
+    total, weight_sum = scatter_rows(
+        *backward_product(blocks, backward_dst, delta_at, count, every, col_blocks)
+    )
+    grad = lax.optimization_barrier(total.astype(BF))
     grad_scale = float(nodes * row_devices * col_devices) ** (-0.5)
-    feature_grad = jnp.einsum("khb,ih->kbi", total.astype(BF), weight, preferred_element_type=F32)
+    feature_grad = jnp.einsum("khb,ih->kbi", grad, weight, preferred_element_type=F32)
     return activated, feature_grad.astype(BF).reshape(nodes, BLK), weight_sum * grad_scale
 
 

time: 156 us -> 144 us (0.923)
  waiting for transfers between devices: 48.1 us -> 38.7 us
  Pallas kernels: 8.67 us -> 13.2 us
  other arithmetic: 6.57 us -> 3.7 us
  matrix products: 3.37 us -> 0.87 us
    ppermute x20, waiting for transfers between devices: 41 us -> 35.6 us  [z_shift(): return lax.ppermute(value, 'row', perm)]
    ppermute x8 -> x9, waiting for transfers between devices: 7.09 us -> 3.08 us  [row_swap(): return lax.ppermute(value, 'row', [(r, r ^ mask) for r in range(4 * NZ)])]
    pallas_call x2, Pallas kernels: 8.67 us -> 12.1 us  [product(): pl.pallas_call(kernel, name=name, in_specs=[smem] * 3 + [pl.BlockSpec(mem...]
    dot_general x5 -> x1, matrix products: 3.37 us -> 0.87 us  [per_device(): jnp.einsum('khb,ih->kbi', grad, weight, preferred_element_type=F32)]
    ppermute x8 -> x9, starting transfers between devices: 10.3 us -> 8.15 us  [row_swap(): return lax.ppermute(value, 'row', [(r, r ^ mask) for r in range(4 * NZ)])]
    all_to_all x1, blocking collectives: 20.5 us -> 18.9 us  [per_device(): lax.all_to_all(partial.reshape(col_devices, nodes, BLK), 'col', 0, 0)]
    all_to_all x1, blocking collectives: 19.9 us -> 21.5 us  [per_device(): every = lax.all_to_all(message, 'col', 0, 0).reshape(-1, BLK, BLK)]
  transfers between devices with their start and end apart: 28 -> 29, of which waited for: 17 -> 13; matrix products, arithmetic and copies ran while one was open for 2% -> 2% of each run, Pallas kernels for 0% -> 0%
where the time goes in v2:
time: 144 us
  starting transfers between devices  43.9 us (30%)
  blocking collectives  40.4 us (28%)
  waiting for transfers between devices  38.7 us (27%)
  Pallas kernels  13.2 us (9%)
  other arithmetic  3.7 us (3%)
  between operations  1.99 us (1%)
    ppermute x20, starting transfers between devices, z_shift(): return lax.ppermute(value, 'row', perm)  35.7 us
    ppermute x20, waiting for transfers between devices, z_shift(): return lax.ppermute(value, 'row', perm)  35.6 us
    all_to_all x1, blocking collectives, per_device(): every = lax.all_to_all(message, 'col', 0, 0).reshape(-1, BLK, BLK)  21.5 us
    all_to_all x1, blocking collectives, per_device(): lax.all_to_all(partial.reshape(col_devices, nodes, BLK), 'col', 0, 0)  18.9 us
    pallas_call x2, Pallas kernels, product(): pl.pallas_call(kernel, name=name, in_specs=[smem] * 3 + [pl.BlockSpec(mem...  12.1 us
    ppermute x9, starting transfers between devices, row_swap(): return lax.ppermute(value, 'row', [(r, r ^ mask) for r in range(4 * NZ)])  8.15 us
    ppermute x9, waiting for transfers between devices, row_swap(): return lax.ppermute(value, 'row', [(r, r ^ mask) for r in range(4 * NZ)])  3.08 us
  transfers between devices with their start and end apart: 29, of which 13 were waited for; matrix products, arithmetic and copies ran while one was open for 2% of the time, Pallas kernels for 0%

profile of v2, /device:TPU:8, one launch (start us, length us, event | category | flops | bytes accessed | tf_op | source)
XLA Modules:
  0.0 143.6 jit_solution(14866343574322486893)
XLA Ops:
  0.6 5.9 %collective-permute-start.2 = (bf16[4,128,128]{2,1,0:T(8,128)(2,1)}, bf16[4,128,128]{2,1,0:T(8,128)(2,1)S(1)}, u32[]{:S(2)}, u32[]{:S(2)}) collective-permute-start(bf16[4,128,128]{2,1,0:T(8,128)(2,1)} %bitcast.181), channel_id=1, source_target_pairs={{0,224},{8,232},{16,240},{24,248},{32,0},{40,8},{48,16},{56,24},{6... | collective-permute-start | bytes 393224 | tf_op jit(solution)/shard_map/ppermute | solution.py:43
  6.6 3.0 %collective-permute-start = (bf16[4,128,128]{2,1,0:T(8,128)(2,1)}, bf16[4,128,128]{2,1,0:T(8,128)(2,1)S(1)}, u32[]{:S(2)}, u32[]{:S(2)}) collective-permute-start(bf16[4,128,128]{2,1,0:T(8,128)(2,1)} %bitcast.183), channel_id=1, source_target_pairs={{0,16},{8,24},{16,0},{24,8},{32,48},{40,56},{48,32},{56,40},{64,80... | collective-permute-start | bytes 393224 | tf_op jit(solution)/shard_map/ppermute | solution.py:47
  9.6 3.3 %collective-permute-done.1 = bf16[4,128,128]{2,1,0:T(8,128)(2,1)S(1)} collective-permute-done((bf16[4,128,128]{2,1,0:T(8,128)(2,1)}, bf16[4,128,128]{2,1,0:T(8,128)(2,1)S(1)}, u32[]{:S(2)}, u32[]{:S(2)}) %collective-permute-start.1) | collective-permute-done | bytes 131104 | tf_op jit(solution)/shard_map/ppermute | solution.py:43
  13.4 3.3 %collective-permute-start.4 = (bf16[8,128,128]{2,1,0:T(8,128)(2,1)S(1)}, bf16[8,128,128]{2,1,0:T(8,128)(2,1)S(1)}, u32[]{:S(2)}, u32[]{:S(2)}) collective-permute-start(bf16[8,128,128]{2,1,0:T(8,128)(2,1)S(1)} %get-tuple-element.105), channel_id=1, source_target_pairs={{0,224},{8,232},{16,240},{24,248},{32,0},{40,8},{48,16},{56,24},{6... | collective-permute-start | bytes 786440 | tf_op jit(solution)/shard_map/ppermute | solution.py:43
  17.3 3.8 %collective-permute-done.3 = bf16[8,128,128]{2,1,0:T(8,128)(2,1)S(1)} collective-permute-done((bf16[8,128,128]{2,1,0:T(8,128)(2,1)S(1)}, bf16[8,128,128]{2,1,0:T(8,128)(2,1)S(1)}, u32[]{:S(2)}, u32[]{:S(2)}) %collective-permute-start.3) | collective-permute-done | bytes 262176 | tf_op jit(solution)/shard_map/ppermute | solution.py:43
  21.2 3.2 %collective-permute-start.6 = (bf16[8,128,128]{2,1,0:T(8,128)(2,1)S(1)}, bf16[8,128,128]{2,1,0:T(8,128)(2,1)S(1)}, u32[]{:S(2)}, u32[]{:S(2)}) collective-permute-start(bf16[8,128,128]{2,1,0:T(8,128)(2,1)S(1)} %collective-permute-done.4), channel_id=1, source_target_pairs={{0,224},{8,232},{16,240},{24,248},{32,0},{40,8},{48,16},{56,24},{6... | collective-permute-start | bytes 786440 | tf_op jit(solution)/shard_map/ppermute | solution.py:43
  25.2 1.0 pad_maximum_fusion.refs_0_
  26.2 2.6 %collective-permute-done.5 = bf16[8,128,128]{2,1,0:T(8,128)(2,1)S(1)} collective-permute-done((bf16[8,128,128]{2,1,0:T(8,128)(2,1)S(1)}, bf16[8,128,128]{2,1,0:T(8,128)(2,1)S(1)}, u32[]{:S(2)}, u32[]{:S(2)}) %collective-permute-start.5) | collective-permute-done | bytes 262176 | tf_op jit(solution)/shard_map/ppermute | solution.py:43
  28.9 3.3 %collective-permute-start.8 = (bf16[6,128,128]{2,1,0:T(8,128)(2,1)S(1)}, bf16[6,128,128]{2,1,0:T(8,128)(2,1)S(1)}, u32[]{:S(2)}, u32[]{:S(2)}) collective-permute-start(bf16[6,128,128]{2,1,0:T(8,128)(2,1)S(1)} %slice.303), channel_id=1, source_target_pairs={{0,224},{8,232},{16,240},{24,248},{32,0},{40,8},{48,16},{56,24},{6... | collective-permute-start | bytes 589832 | tf_op jit(solution)/shard_map/ppermute | solution.py:43
  32.3 4.1 %collective-permute-done.7 = bf16[6,128,128]{2,1,0:T(8,128)(2,1)S(1)} collective-permute-done((bf16[6,128,128]{2,1,0:T(8,128)(2,1)S(1)}, bf16[6,128,128]{2,1,0:T(8,128)(2,1)S(1)}, u32[]{:S(2)}, u32[]{:S(2)}) %collective-permute-start.7) | collective-permute-done | bytes 196640 | tf_op jit(solution)/shard_map/ppermute | solution.py:43
  36.5 3.3 %collective-permute-start.10 = (bf16[2,128,128]{2,1,0:T(8,128)(2,1)S(1)}, bf16[2,128,128]{2,1,0:T(8,128)(2,1)S(1)}, u32[]{:S(2)}, u32[]{:S(2)}) collective-permute-start(bf16[2,128,128]{2,1,0:T(8,128)(2,1)S(1)} %slice.305), channel_id=1, source_target_pairs={{0,224},{8,232},{16,240},{24,248},{32,0},{40,8},{48,16},{56,24},{6... | collective-permute-start | bytes 196616 | tf_op jit(solution)/shard_map/ppermute | solution.py:43
  40.6 1.4 collective-permute-done.9
  42.0 0.8 collective-permute-start.15
  42.8 1.3 collective-permute-done.15.refs_9_
  44.1 5.9 %forward_product.1 = bf16[32,128,128]{2,1,0:T(8,128)(2,1)S(1)} custom-call(s32[256]{0:T(256)S(1)} %get-tuple-element.111.dst, s32[256]{0:T(256)S(1)} %get-tuple-element.114.src, s32[1]{0:T(128)} %bitcast.171.count, bf16[256,128,128]{2,1,0:T(8,128)(2,1)} %bitcast.175, bf16[16,128,128]{2,1,0:T(8,128)(2,1)S(1)} %pad_maximum_fusion.refs_0_, ...), custom_call_target="tpu_custom_call" | custom-call | flops 1073741824 | bytes 14680064 | tf_op jit(solution)/shard_map/forward_product/pallas_call | solution.py:130
  50.0 18.9 %all_to_all.10.parts = bf16[8,512,128]{2,1,0:T(8,128)(2,1)S(1)} all-to-all(bf16[8,512,128]{2,1,0:T(8,128)(2,1)S(1)} %bitcast.174), channel_id=1, replica_groups=mesh['row'=32,'col'=8] {'col'}, dimensions={0} | all-to-all | bytes 2097152 | tf_op jit(solution)/shard_map/all_to_all | solution.py:342
  68.9 1.0 middle.1
  69.9 21.5 %all_to_all.11 = bf16[8,5,128,128]{3,2,1,0:T(8,128)(2,1)S(1)} all-to-all(bf16[8,5,128,128]{3,2,1,0:T(8,128)(2,1)S(1)} %get-tuple-element.46), channel_id=1, replica_groups=mesh['row'=32,'col'=8] {'col'}, dimensions={0} | all-to-all | bytes 2621440 | tf_op jit(solution)/shard_map/all_to_all | solution.py:344
  91.4 6.2 %backward_product.1 = (bf16[64,128,128]{2,1,0:T(8,128)(2,1)S(1)}, bf16[18,128,128]{2,1,0:T(8,128)(2,1)S(1)}, bf16[48,128,128]{2,1,0:T(8,128)(2,1)S(1)}, f32[128,128]{1,0:T(8,128)S(1)}) custom-call(s32[256]{0:T(256)S(1)} %get-tuple-element.115.dst, s32[256]{0:T(256)S(1)} %get-tuple-element.110.src, s32[1]{0:T(128)} %bitcast.172.count, ...), custom_call_target="tpu_custom_call" | custom-call | flops 1073741824 | bytes 14680064 | tf_op jit(solution)/shard_map/backward_product/pallas_call | solution.py:130
  98.3 1.5 %collective-permute-done.17 = bf16[18,128,128]{2,1,0:T(8,128)(2,1)S(1)} collective-permute-done((bf16[18,128,128]{2,1,0:T(8,128)(2,1)S(1)}, bf16[18,128,128]{2,1,0:T(8,128)(2,1)S(1)}, u32[]{:S(2)}, u32[]{:S(2)}) %collective-permute-start.17) | collective-permute-done | bytes 589856 | tf_op jit(solution)/shard_map/ppermute | solution.py:47
  100.0 3.2 %collective-permute-start.19 = (bf16[3,128,128]{2,1,0:T(8,128)(2,1)S(1)}, bf16[3,128,128]{2,1,0:T(8,128)(2,1)S(1)}, u32[]{:S(2)}, u32[]{:S(2)}) collective-permute-start(bf16[3,128,128]{2,1,0:T(8,128)(2,1)S(1)} %get-tuple-element.52), channel_id=1, source_target_pairs={{0,224},{8,232},{16,240},{24,248},{32,0},{40,8},{48,16},{56,24},{6... | collective-permute-start | bytes 294920 | tf_op jit(solution)/shard_map/ppermute | solution.py:43
  103.2 2.8 %collective-permute-done.18 = bf16[3,128,128]{2,1,0:T(8,128)(2,1)S(1)} collective-permute-done((bf16[3,128,128]{2,1,0:T(8,128)(2,1)S(1)}, bf16[3,128,128]{2,1,0:T(8,128)(2,1)S(1)}, u32[]{:S(2)}, u32[]{:S(2)}) %collective-permute-start.18) | collective-permute-done | bytes 98336 | tf_op jit(solution)/shard_map/ppermute | solution.py:43
  106.3 3.2 %collective-permute-start.21 = (bf16[7,128,128]{2,1,0:T(8,128)(2,1)S(1)}, bf16[7,128,128]{2,1,0:T(8,128)(2,1)S(1)}, u32[]{:S(2)}, u32[]{:S(2)}) collective-permute-start(bf16[7,128,128]{2,1,0:T(8,128)(2,1)S(1)} %pad_maximum_fusion.10), channel_id=1, source_target_pairs={{0,224},{8,232},{16,240},{24,248},{32,0},{40,8},{48,16},{56,24},{6... | collective-permute-start | bytes 688136 | tf_op jit(solution)/shard_map/ppermute | solution.py:43
  109.6 4.8 %collective-permute-done.20 = bf16[7,128,128]{2,1,0:T(8,128)(2,1)S(1)} collective-permute-done((bf16[7,128,128]{2,1,0:T(8,128)(2,1)S(1)}, bf16[7,128,128]{2,1,0:T(8,128)(2,1)S(1)}, u32[]{:S(2)}, u32[]{:S(2)}) %collective-permute-start.20) | collective-permute-done | bytes 229408 | tf_op jit(solution)/shard_map/ppermute | solution.py:43
  115.2 3.2 %collective-permute-start.23 = (bf16[9,128,128]{2,1,0:T(8,128)(2,1)S(1)}, bf16[9,128,128]{2,1,0:T(8,128)(2,1)S(1)}, u32[]{:S(2)}, u32[]{:S(2)}) collective-permute-start(bf16[9,128,128]{2,1,0:T(8,128)(2,1)S(1)} %pad_maximum_fusion.4), channel_id=1, source_target_pairs={{0,224},{8,232},{16,240},{24,248},{32,0},{40,8},{48,16},{56,24},{6... | collective-permute-start | bytes 884744 | tf_op jit(solution)/shard_map/ppermute | solution.py:43
  118.4 5.3 %collective-permute-done.22 = bf16[9,128,128]{2,1,0:T(8,128)(2,1)S(1)} collective-permute-done((bf16[9,128,128]{2,1,0:T(8,128)(2,1)S(1)}, bf16[9,128,128]{2,1,0:T(8,128)(2,1)S(1)}, u32[]{:S(2)}, u32[]{:S(2)}) %collective-permute-start.22) | collective-permute-done | bytes 294944 | tf_op jit(solution)/shard_map/ppermute | solution.py:43
  124.4 3.2 %collective-permute-start.25 = (bf16[9,128,128]{2,1,0:T(8,128)(2,1)S(1)}, bf16[9,128,128]{2,1,0:T(8,128)(2,1)S(1)}, u32[]{:S(2)}, u32[]{:S(2)}) collective-permute-start(bf16[9,128,128]{2,1,0:T(8,128)(2,1)S(1)} %pad_maximum_fusion.6), channel_id=1, source_target_pairs={{0,224},{8,232},{16,240},{24,248},{32,0},{40,8},{48,16},{56,24},{6... | collective-permute-start | bytes 884744 | tf_op jit(solution)/shard_map/ppermute | solution.py:43
  127.6 4.4 %collective-permute-done.24 = bf16[9,128,128]{2,1,0:T(8,128)(2,1)S(1)} collective-permute-done((bf16[9,128,128]{2,1,0:T(8,128)(2,1)S(1)}, bf16[9,128,128]{2,1,0:T(8,128)(2,1)S(1)}, u32[]{:S(2)}, u32[]{:S(2)}) %collective-permute-start.24) | collective-permute-done | bytes 294944 | tf_op jit(solution)/shard_map/ppermute | solution.py:43
  132.7 3.1 %collective-permute-start.26 = (bf16[6,128,128]{2,1,0:T(8,128)(2,1)S(1)}, bf16[6,128,128]{2,1,0:T(8,128)(2,1)S(1)}, u32[]{:S(2)}, u32[]{:S(2)}) collective-permute-start(bf16[6,128,128]{2,1,0:T(8,128)(2,1)S(1)} %pad_maximum_fusion.11), channel_id=1, source_target_pairs={{0,16},{8,24},{16,0},{24,8},{32,48},{40,56},{48,32},{56,40},{64,80... | collective-permute-start | bytes 589832 | tf_op jit(solution)/shard_map/ppermute | solution.py:47
  135.8 3.2 %collective-permute-start.28 = (bf16[4,128,128]{2,1,0:T(8,128)(2,1)S(1)}, bf16[4,128,128]{2,1,0:T(8,128)(2,1)S(1)}, u32[]{:S(2)}, u32[]{:S(2)}) collective-permute-start(bf16[4,128,128]{2,1,0:T(8,128)(2,1)S(1)} %get-tuple-element.76), channel_id=1, source_target_pairs={{0,224},{8,232},{16,240},{24,248},{32,0},{40,8},{48,16},{56,24},{6... | collective-permute-start | bytes 393224 | tf_op jit(solution)/shard_map/ppermute | solution.py:43
  139.0 2.9 %collective-permute-done.27 = bf16[4,128,128]{2,1,0:T(8,128)(2,1)S(1)} collective-permute-done((bf16[4,128,128]{2,1,0:T(8,128)(2,1)S(1)}, bf16[4,128,128]{2,1,0:T(8,128)(2,1)S(1)}, u32[]{:S(2)}, u32[]{:S(2)}) %collective-permute-start.27) | collective-permute-done | bytes 131104 | tf_op jit(solution)/shard_map/ppermute | solution.py:43
  142.1 0.9 convolution_convert_fusion
  (87 shorter events, 5.8 us)
Async XLA Ops:
  0.6 9.0 %collective-permute-start.2 = (bf16[4,128,128]{2,1,0:T(8,128)(2,1)}, bf16[4,128,128]{2,1,0:T(8,128)(2,1)S(1)}, u32[]{:S(2)}, u32[]{:S(2)}) collective-permute-start(bf16[4,128,128]{2,1,0:T(8,128)(2,1)} %bitcast.181), channel_id=1, source_target_pairs={{0,224},{8,232},{16,240},{24,248},{32,0},{40,8},{48,16},{56,24},{6... | collective-permute-start | bytes 393224 | tf_op jit(solution)/shard_map/ppermute | solution.py:43
  6.6 6.4 %collective-permute-start.1 = (bf16[4,128,128]{2,1,0:T(8,128)(2,1)}, bf16[4,128,128]{2,1,0:T(8,128)(2,1)S(1)}, u32[]{:S(2)}, u32[]{:S(2)}) collective-permute-start(bf16[4,128,128]{2,1,0:T(8,128)(2,1)} %bitcast.182), channel_id=1, source_target_pairs={{0,32},{8,40},{16,48},{24,56},{32,64},{40,72},{48,80},{56,88},{64,... | collective-permute-start | bytes 393224 | tf_op jit(solution)/shard_map/ppermute | solution.py:43
  6.6 6.7 %collective-permute-start = (bf16[4,128,128]{2,1,0:T(8,128)(2,1)}, bf16[4,128,128]{2,1,0:T(8,128)(2,1)S(1)}, u32[]{:S(2)}, u32[]{:S(2)}) collective-permute-start(bf16[4,128,128]{2,1,0:T(8,128)(2,1)} %bitcast.183), channel_id=1, source_target_pairs={{0,16},{8,24},{16,0},{24,8},{32,48},{40,56},{48,32},{56,40},{64,80... | collective-permute-start | bytes 393224 | tf_op jit(solution)/shard_map/ppermute | solution.py:47
  13.3 7.9 %collective-permute-start.3 = (bf16[8,128,128]{2,1,0:T(8,128)(2,1)S(1)}, bf16[8,128,128]{2,1,0:T(8,128)(2,1)S(1)}, u32[]{:S(2)}, u32[]{:S(2)}) collective-permute-start(bf16[8,128,128]{2,1,0:T(8,128)(2,1)S(1)} %get-tuple-element.104), channel_id=1, source_target_pairs={{0,32},{8,40},{16,48},{24,56},{32,64},{40,72},{48,80},{56,88},{64,... | collective-permute-start | bytes 786440 | tf_op jit(solution)/shard_map/ppermute | solution.py:43
  13.4 7.8 %collective-permute-start.4 = (bf16[8,128,128]{2,1,0:T(8,128)(2,1)S(1)}, bf16[8,128,128]{2,1,0:T(8,128)(2,1)S(1)}, u32[]{:S(2)}, u32[]{:S(2)}) collective-permute-start(bf16[8,128,128]{2,1,0:T(8,128)(2,1)S(1)} %get-tuple-element.105), channel_id=1, source_target_pairs={{0,224},{8,232},{16,240},{24,248},{32,0},{40,8},{48,16},{56,24},{6... | collective-permute-start | bytes 786440 | tf_op jit(solution)/shard_map/ppermute | solution.py:43
  21.2 7.6 %collective-permute-start.5 = (bf16[8,128,128]{2,1,0:T(8,128)(2,1)S(1)}, bf16[8,128,128]{2,1,0:T(8,128)(2,1)S(1)}, u32[]{:S(2)}, u32[]{:S(2)}) collective-permute-start(bf16[8,128,128]{2,1,0:T(8,128)(2,1)S(1)} %collective-permute-done.3), channel_id=1, source_target_pairs={{0,32},{8,40},{16,48},{24,56},{32,64},{40,72},{48,80},{56,88},{64,... | collective-permute-start | bytes 786440 | tf_op jit(solution)/shard_map/ppermute | solution.py:43
  21.2 7.7 %collective-permute-start.6 = (bf16[8,128,128]{2,1,0:T(8,128)(2,1)S(1)}, bf16[8,128,128]{2,1,0:T(8,128)(2,1)S(1)}, u32[]{:S(2)}, u32[]{:S(2)}) collective-permute-start(bf16[8,128,128]{2,1,0:T(8,128)(2,1)S(1)} %collective-permute-done.4), channel_id=1, source_target_pairs={{0,224},{8,232},{16,240},{24,248},{32,0},{40,8},{48,16},{56,24},{6... | collective-permute-start | bytes 786440 | tf_op jit(solution)/shard_map/ppermute | solution.py:43
  28.8 7.7 %collective-permute-start.7 = (bf16[6,128,128]{2,1,0:T(8,128)(2,1)S(1)}, bf16[6,128,128]{2,1,0:T(8,128)(2,1)S(1)}, u32[]{:S(2)}, u32[]{:S(2)}) collective-permute-start(bf16[6,128,128]{2,1,0:T(8,128)(2,1)S(1)} %slice.302), channel_id=1, source_target_pairs={{0,32},{8,40},{16,48},{24,56},{32,64},{40,72},{48,80},{56,88},{64,... | collective-permute-start | bytes 589832 | tf_op jit(solution)/shard_map/ppermute | solution.py:43
  28.9 7.6 %collective-permute-start.8 = (bf16[6,128,128]{2,1,0:T(8,128)(2,1)S(1)}, bf16[6,128,128]{2,1,0:T(8,128)(2,1)S(1)}, u32[]{:S(2)}, u32[]{:S(2)}) collective-permute-start(bf16[6,128,128]{2,1,0:T(8,128)(2,1)S(1)} %slice.303), channel_id=1, source_target_pairs={{0,224},{8,232},{16,240},{24,248},{32,0},{40,8},{48,16},{56,24},{6... | collective-permute-start | bytes 589832 | tf_op jit(solution)/shard_map/ppermute | solution.py:43
  36.5 5.5 %collective-permute-start.9 = (bf16[2,128,128]{2,1,0:T(8,128)(2,1)S(1)}, bf16[2,128,128]{2,1,0:T(8,128)(2,1)S(1)}, u32[]{:S(2)}, u32[]{:S(2)}) collective-permute-start(bf16[2,128,128]{2,1,0:T(8,128)(2,1)S(1)} %slice.304), channel_id=1, source_target_pairs={{0,32},{8,40},{16,48},{24,56},{32,64},{40,72},{48,80},{56,88},{64,... | collective-permute-start | bytes 196616 | tf_op jit(solution)/shard_map/ppermute | solution.py:43
  36.5 5.5 %collective-permute-start.10 = (bf16[2,128,128]{2,1,0:T(8,128)(2,1)S(1)}, bf16[2,128,128]{2,1,0:T(8,128)(2,1)S(1)}, u32[]{:S(2)}, u32[]{:S(2)}) collective-permute-start(bf16[2,128,128]{2,1,0:T(8,128)(2,1)S(1)} %slice.305), channel_id=1, source_target_pairs={{0,224},{8,232},{16,240},{24,248},{32,0},{40,8},{48,16},{56,24},{6... | collective-permute-start | bytes 196616 | tf_op jit(solution)/shard_map/ppermute | solution.py:43
  39.8 4.3 %collective-permute-start.11 = (bf16[16,128,128]{2,1,0:T(8,128)(2,1)S(1)}, bf16[16,128,128]{2,1,0:T(8,128)(2,1)S(1)}, u32[]{:S(2)}, u32[]{:S(2)}) collective-permute-start(bf16[16,128,128]{2,1,0:T(8,128)(2,1)S(1)} %pad_maximum_fusion.refs_0_), channel_id=1, source_target_pairs={{0,8},{8,0},{16,24},{24,16},{32,40},{40,32},{48,56},{56,48},{64,72... | collective-permute-start | bytes 1572872 | tf_op jit(solution)/shard_map/ppermute | solution.py:47
  39.9 4.2 %collective-permute-start.12 = (bf16[16,128,128]{2,1,0:T(8,128)(2,1)S(1)}, bf16[16,128,128]{2,1,0:T(8,128)(2,1)S(1)}, u32[]{:S(2)}, u32[]{:S(2)}) collective-permute-start(bf16[16,128,128]{2,1,0:T(8,128)(2,1)S(1)} %pad_maximum_fusion.1.refs_1_), channel_id=1, source_target_pairs={{0,8},{8,0},{16,24},{24,16},{32,40},{40,32},{48,56},{56,48},{64,72... | collective-permute-start | bytes 1572872 | tf_op jit(solution)/shard_map/ppermute | solution.py:47
  40.4 3.7 %collective-permute-start.13 = (bf16[16,128,128]{2,1,0:T(8,128)(2,1)S(1)}, bf16[16,128,128]{2,1,0:T(8,128)(2,1)S(1)}, u32[]{:S(2)}, u32[]{:S(2)}) collective-permute-start(bf16[16,128,128]{2,1,0:T(8,128)(2,1)S(1)} %pad_maximum_fusion.2.refs_2_), channel_id=1, source_target_pairs={{0,8},{8,0},{16,24},{24,16},{32,40},{40,32},{48,56},{56,48},{64,72... | collective-permute-start | bytes 1572872 | tf_op jit(solution)/shard_map/ppermute | solution.py:47
  41.9 2.1 %collective-permute-start.14 = (bf16[12,128,128]{2,1,0:T(8,128)(2,1)S(1)}, bf16[12,128,128]{2,1,0:T(8,128)(2,1)S(1)}, u32[]{:S(2)}, u32[]{:S(2)}) collective-permute-start(bf16[12,128,128]{2,1,0:T(8,128)(2,1)S(1)} %constant_dynamic-update-slice_fusion.refs_3_), channel_id=1, source_target_pairs={{0,8},{8,0},{16,24},{24,16},{32,40},{40,32},{48,56},{56,48},{64,72... | collective-permute-start | bytes 1179656 | tf_op jit(solution)/shard_map/ppermute | solution.py:47
  42.0 2.1 %collective-permute-start.15 = (bf16[4,128,128]{2,1,0:T(8,128)(2,1)S(1)}, bf16[4,128,128]{2,1,0:T(8,128)(2,1)S(1)}, u32[]{:S(2)}, u32[]{:S(2)}) collective-permute-start(bf16[4,128,128]{2,1,0:T(8,128)(2,1)S(1)} %constant_dynamic-update-slice_fusion.2.refs_4_), channel_id=1, source_target_pairs={{0,8},{8,0},{16,24},{24,16},{32,40},{40,32},{48,56},{56,48},{64,72... | collective-permute-start | bytes 393224 | tf_op jit(solution)/shard_map/ppermute | solution.py:47
  50.0 18.9 %copy-start = (bf16[512,128]{1,0:T(8,128)(2,1)S(1)}, bf16[512,128]{1,0:T(8,128)(2,1)}, u32[]{:S(2)}) copy-start(bf16[512,128]{1,0:T(8,128)(2,1)} %cotangent.1) | copy-start | bytes 393220
  50.0 18.9 %copy-start.1 = (bf16[128,128]{1,0:T(8,128)(2,1)S(1)}, bf16[128,128]{1,0:T(8,128)(2,1)}, u32[]{:S(2)}) copy-start(bf16[128,128]{1,0:T(8,128)(2,1)} %weight.1) | copy-start | bytes 98308
  97.7 2.1 %collective-permute-start.17 = (bf16[18,128,128]{2,1,0:T(8,128)(2,1)S(1)}, bf16[18,128,128]{2,1,0:T(8,128)(2,1)S(1)}, u32[]{:S(2)}, u32[]{:S(2)}) collective-permute-start(bf16[18,128,128]{2,1,0:T(8,128)(2,1)S(1)} %get-tuple-element.49), channel_id=1, source_target_pairs={{0,8},{8,0},{16,24},{24,16},{32,40},{40,32},{48,56},{56,48},{64,72... | collective-permute-start | bytes 1769480 | tf_op jit(solution)/shard_map/ppermute | solution.py:47
  97.8 16.7 %collective-permute-start.16 = (bf16[48,128,128]{2,1,0:T(8,128)(2,1)S(1)}, bf16[48,128,128]{2,1,0:T(8,128)(2,1)S(1)}, u32[]{:S(2)}, u32[]{:S(2)}) collective-permute-start(bf16[48,128,128]{2,1,0:T(8,128)(2,1)S(1)} %get-tuple-element.48), channel_id=1, source_target_pairs={{0,8},{8,0},{16,24},{24,16},{32,40},{40,32},{48,56},{56,48},{64,72... | collective-permute-start | bytes 4718600 | tf_op jit(solution)/shard_map/ppermute | solution.py:47
  99.9 6.1 %collective-permute-start.18 = (bf16[3,128,128]{2,1,0:T(8,128)(2,1)S(1)}, bf16[3,128,128]{2,1,0:T(8,128)(2,1)S(1)}, u32[]{:S(2)}, u32[]{:S(2)}) collective-permute-start(bf16[3,128,128]{2,1,0:T(8,128)(2,1)S(1)} %get-tuple-element.51), channel_id=1, source_target_pairs={{0,32},{8,40},{16,48},{24,56},{32,64},{40,72},{48,80},{56,88},{64,... | collective-permute-start | bytes 294920 | tf_op jit(solution)/shard_map/ppermute | solution.py:43
  100.0 6.0 %collective-permute-start.19 = (bf16[3,128,128]{2,1,0:T(8,128)(2,1)S(1)}, bf16[3,128,128]{2,1,0:T(8,128)(2,1)S(1)}, u32[]{:S(2)}, u32[]{:S(2)}) collective-permute-start(bf16[3,128,128]{2,1,0:T(8,128)(2,1)S(1)} %get-tuple-element.52), channel_id=1, source_target_pairs={{0,224},{8,232},{16,240},{24,248},{32,0},{40,8},{48,16},{56,24},{6... | collective-permute-start | bytes 294920 | tf_op jit(solution)/shard_map/ppermute | solution.py:43
  106.2 8.1 %collective-permute-start.20 = (bf16[7,128,128]{2,1,0:T(8,128)(2,1)S(1)}, bf16[7,128,128]{2,1,0:T(8,128)(2,1)S(1)}, u32[]{:S(2)}, u32[]{:S(2)}) collective-permute-start(bf16[7,128,128]{2,1,0:T(8,128)(2,1)S(1)} %pad_maximum_fusion.9), channel_id=1, source_target_pairs={{0,32},{8,40},{16,48},{24,56},{32,64},{40,72},{48,80},{56,88},{64,... | collective-permute-start | bytes 688136 | tf_op jit(solution)/shard_map/ppermute | solution.py:43
  106.3 8.1 %collective-permute-start.21 = (bf16[7,128,128]{2,1,0:T(8,128)(2,1)S(1)}, bf16[7,128,128]{2,1,0:T(8,128)(2,1)S(1)}, u32[]{:S(2)}, u32[]{:S(2)}) collective-permute-start(bf16[7,128,128]{2,1,0:T(8,128)(2,1)S(1)} %pad_maximum_fusion.10), channel_id=1, source_target_pairs={{0,224},{8,232},{16,240},{24,248},{32,0},{40,8},{48,16},{56,24},{6... | collective-permute-start | bytes 688136 | tf_op jit(solution)/shard_map/ppermute | solution.py:43
  115.1 8.6 %collective-permute-start.22 = (bf16[9,128,128]{2,1,0:T(8,128)(2,1)S(1)}, bf16[9,128,128]{2,1,0:T(8,128)(2,1)S(1)}, u32[]{:S(2)}, u32[]{:S(2)}) collective-permute-start(bf16[9,128,128]{2,1,0:T(8,128)(2,1)S(1)} %pad_maximum_fusion.3), channel_id=1, source_target_pairs={{0,32},{8,40},{16,48},{24,56},{32,64},{40,72},{48,80},{56,88},{64,... | collective-permute-start | bytes 884744 | tf_op jit(solution)/shard_map/ppermute | solution.py:43
  115.2 8.5 %collective-permute-start.23 = (bf16[9,128,128]{2,1,0:T(8,128)(2,1)S(1)}, bf16[9,128,128]{2,1,0:T(8,128)(2,1)S(1)}, u32[]{:S(2)}, u32[]{:S(2)}) collective-permute-start(bf16[9,128,128]{2,1,0:T(8,128)(2,1)S(1)} %pad_maximum_fusion.4), channel_id=1, source_target_pairs={{0,224},{8,232},{16,240},{24,248},{32,0},{40,8},{48,16},{56,24},{6... | collective-permute-start | bytes 884744 | tf_op jit(solution)/shard_map/ppermute | solution.py:43
  124.1 8.0 %collective-permute-start.24 = (bf16[9,128,128]{2,1,0:T(8,128)(2,1)S(1)}, bf16[9,128,128]{2,1,0:T(8,128)(2,1)S(1)}, u32[]{:S(2)}, u32[]{:S(2)}) collective-permute-start(bf16[9,128,128]{2,1,0:T(8,128)(2,1)S(1)} %pad_maximum_fusion.5), channel_id=1, source_target_pairs={{0,32},{8,40},{16,48},{24,56},{32,64},{40,72},{48,80},{56,88},{64,... | collective-permute-start | bytes 884744 | tf_op jit(solution)/shard_map/ppermute | solution.py:43
  124.4 8.1 %collective-permute-start.25 = (bf16[9,128,128]{2,1,0:T(8,128)(2,1)S(1)}, bf16[9,128,128]{2,1,0:T(8,128)(2,1)S(1)}, u32[]{:S(2)}, u32[]{:S(2)}) collective-permute-start(bf16[9,128,128]{2,1,0:T(8,128)(2,1)S(1)} %pad_maximum_fusion.6), channel_id=1, source_target_pairs={{0,224},{8,232},{16,240},{24,248},{32,0},{40,8},{48,16},{56,24},{6... | collective-permute-start | bytes 884744 | tf_op jit(solution)/shard_map/ppermute | solution.py:43
  132.7 9.3 %collective-permute-start.26 = (bf16[6,128,128]{2,1,0:T(8,128)(2,1)S(1)}, bf16[6,128,128]{2,1,0:T(8,128)(2,1)S(1)}, u32[]{:S(2)}, u32[]{:S(2)}) collective-permute-start(bf16[6,128,128]{2,1,0:T(8,128)(2,1)S(1)} %pad_maximum_fusion.11), channel_id=1, source_target_pairs={{0,16},{8,24},{16,0},{24,8},{32,48},{40,56},{48,32},{56,40},{64,80... | collective-permute-start | bytes 589832 | tf_op jit(solution)/shard_map/ppermute | solution.py:47
  135.8 6.2 %collective-permute-start.27 = (bf16[4,128,128]{2,1,0:T(8,128)(2,1)S(1)}, bf16[4,128,128]{2,1,0:T(8,128)(2,1)S(1)}, u32[]{:S(2)}, u32[]{:S(2)}) collective-permute-start(bf16[4,128,128]{2,1,0:T(8,128)(2,1)S(1)} %get-tuple-element.75), channel_id=1, source_target_pairs={{0,32},{8,40},{16,48},{24,56},{32,64},{40,72},{48,80},{56,88},{64,... | collective-permute-start | bytes 393224 | tf_op jit(solution)/shard_map/ppermute | solution.py:43
  135.8 6.2 %collective-permute-start.28 = (bf16[4,128,128]{2,1,0:T(8,128)(2,1)S(1)}, bf16[4,128,128]{2,1,0:T(8,128)(2,1)S(1)}, u32[]{:S(2)}, u32[]{:S(2)}) collective-permute-start(bf16[4,128,128]{2,1,0:T(8,128)(2,1)S(1)} %get-tuple-element.76), channel_id=1, source_target_pairs={{0,224},{8,232},{16,240},{24,248},{32,0},{40,8},{48,16},{56,24},{6... | collective-permute-start | bytes 393224 | tf_op jit(solution)/shard_map/ppermute | solution.py:43

commit v3 on v2

--- a/solution.py
+++ b/solution.py
@@ -15,8 +15,7 @@
 BF = jnp.bfloat16
 F32 = jnp.float32
 
-PLACES = ((0, 4), (8, 16), (20, 32), (36, 48), (52, 60), (40, 56), (24, 44), (12, 28))
-
+PLACES = ((0, 4), (8, 12), (24, 28), (40, 44), (56, 60), (48, 52), (32, 36), (16, 20))
 
 ORDER = (
     (4, 1), (3, 1), (5, 1), (4, 0), (2, 1), (6, 1), (3, 0), (5, 0),
@@ -38,8 +37,8 @@
     return jnp.concatenate(values, axis=0)
 
 
-def z_shift(value, step):
-    perm = [(r, ((r // 4 + step) % NZ) * 4 + r % 4) for r in range(4 * NZ)]
+def z_shift(value, step, mask=0):
+    perm = [(r, ((r // 4 + step) % NZ) * 4 + (r % 4 ^ mask)) for r in range(4 * NZ)]
     return lax.ppermute(value, "row", perm)
 
 
@@ -48,8 +47,8 @@
 
 
 def split(value):
-    high = lax.reduce_precision(value, 8, 7)
-    return high.astype(BF), (value - high).astype(BF)
+    high = value.astype(BF)
+    return high, (value - wide(high)).astype(BF)
 
 
 def add_products(x_first, dst, src, count, blocks, held, acc, slots, sems):
@@ -100,11 +99,6 @@
     out[...] = acc[: out.shape[0]].astype(out.dtype)
 
 
-def split_here(value):
-    high = value.astype(BF)
-    return high, (value - wide(high)).astype(BF)
-
-
 def backward_kernel(dst, src, count, blocks, every, keep, soon, later, sums, acc, slots, sems):
     for c in range(slots.shape[0] // CHUNK):
         load(blocks, slots, sems, c).start()
@@ -113,7 +107,7 @@
     total = wide(every[BPD])
     for k in range(1, every.shape[0] // span):
         total = total + wide(every[k * span + BPD])
-    high, low = split_here(total)
+    high, low = split(total)
     half = keep.shape[0]
     soon[SOON], soon[SOON + 1] = high, low
     sums[...] = wide(high) + wide(low)
@@ -153,9 +147,9 @@
         dst,
         src,
         count,
-        pieces,
+        [pltpu.with_memory_space_constraint(piece, pltpu.VMEM) for piece in pieces],
         [jax.ShapeDtypeStruct((num_dst, BLK, BLK), BF)],
-        pl.ANY,
+        pltpu.VMEM,
         [
             pltpu.VMEM((num_dst + 1, BLK, BLK), F32),
             pltpu.VMEM((held, BLK, BLK), BF),
@@ -198,7 +192,7 @@
     spread = wide(parts[0])
     for k in range(1, parts.shape[0]):
         spread = spread + wide(parts[k])
-    high, low = split_here(spread)
+    high, low = split(spread)
     preact = dot(high, weight[...]) + dot(low, weight[...])
     activated[...] = (preact * jax.nn.sigmoid(preact)).astype(BF)
     delta = wide(cotangent[...]) * silu_grad(preact)
@@ -231,13 +225,20 @@
 def gather_rows(own):
     mate = row_swap(own, 2)
     up1, down1 = z_shift(own, 1), z_shift(own, -1)
-    up2, down2 = z_shift(cat(mate, up1), 1), z_shift(cat(down1, mate), -1)
+    mate_up1, mate_down1 = z_shift(own, 1, 2), z_shift(own, -1, 2)
+    up2, down2 = z_shift(cat(up1, mate_up1), 1), z_shift(cat(down1, mate_down1), -1)
     up3, down3 = z_shift(up2, 1), z_shift(down2, -1)
-    up4, down4 = z_shift(up3[: BPD + HALF], 1), z_shift(down3[HALF:], -1)
-    up5, down5 = z_shift(up4[:HALF], 1), z_shift(down4[BPD:], -1)
-    groups = [cat(own, mate, up1, down1), cat(up2, down2), cat(up3, down3)]
+    up4 = cat(up3[:HALF], up3[BPD : BPD + HALF])
+    down4 = cat(down3[HALF:BPD], down3[BPD + HALF :])
+    groups = [
+        cat(own, mate, up1, mate_up1),
+        cat(down1, mate_down1, up2),
+        cat(down2, up3),
+        down3,
+    ]
     groups, up4, down4 = lax.optimization_barrier((groups, up4, down4))
-    groups += [cat(up4, down4), cat(up5, down5)]
+    up4, down4 = z_shift(up4, 1), z_shift(down4, -1)
+    groups.append(cat(up4[:HALF], down4[:HALF], up4[HALF:], down4[HALF:]))
     return groups + [row_swap(group, 1) for group in groups]
 
 
@@ -297,15 +298,43 @@
         for n in range(1, NZ):
             chosen = jnp.where(d == n, near[n][0], chosen)
         summed = summed + wide(chosen)
-    high, low = lax.optimization_barrier(split(summed))
+    high = lax.optimization_barrier(summed.astype(BF))
     theirs = ahead[0] + up[:BPD] + down[BPD:]
     up = (ahead[1] + up[BPD:]).astype(BF)
     down = (ahead[2] + down[:BPD]).astype(BF)
     up, down = lax.optimization_barrier((up, down))
-    theirs = cat(theirs.astype(BF), high[None], low[None])
-    mate, up, down = row_swap(theirs, 2), z_shift(up, 1), z_shift(down, -1)
-    total = ahead[3] + wide(mate[:BPD]) + wide(up) + wide(down)
-    return total, (wide(high) + wide(low)) + (wide(mate[BPD]) + wide(mate[BPD + 1]))
+    up, down = z_shift(up, 1), z_shift(down, -1)
+    mate = row_swap(cat(theirs.astype(BF), high[None]), 2)
+    near = lax.optimization_barrier(ahead[3] + wide(up) + wide(down))
+    return near, mate, high
+
+
+def finish_kernel(scale, near, mate, high, weight, feature_grad, weight_grad):
+    weight_grad[...] = (wide(high[...]) + wide(mate[BPD])) * scale
+    for b in range(BPD):
+        grad = (near[b] + wide(mate[b])).T.astype(BF)
+        out = lax.dot_general(
+            grad, weight[...], (((1,), (1,)), ((), ())), preferred_element_type=F32
+        )
+        feature_grad[b * BLK : (b + 1) * BLK] = out.astype(BF)
+
+
+def finish(near, mate, high, weight, scale):
+    vmem = pl.BlockSpec(memory_space=pltpu.VMEM)
+    return pl.pallas_call(
+        lambda *refs: finish_kernel(scale, *refs),
+        name="finish",
+        in_specs=[vmem] * 4,
+        out_specs=[vmem] * 2,
+        out_shape=[
+            jax.ShapeDtypeStruct((BPD * BLK, BLK), BF),
+            jax.ShapeDtypeStruct((BLK, BLK), F32),
+        ],
+        compiler_params=pltpu.CompilerParams(vmem_limit_bytes=VMEM_LIMIT),
+        cost_estimate=pl.CostEstimate(
+            flops=2 * BPD * BLK**3, bytes_accessed=1 << 20, transcendentals=0
+        ),
+    )(near, mate, high, weight)
 
 
 def per_device(features, weight, adj_values, block_coords, block_counts, cotangent):
@@ -342,13 +371,10 @@
     parts = lax.all_to_all(partial.reshape(col_devices, nodes, BLK), "col", 0, 0)
     activated, message = middle(parts, weight, cotangent)
     every = lax.all_to_all(message, "col", 0, 0).reshape(-1, BLK, BLK)
-    total, weight_sum = scatter_rows(
-        *backward_product(blocks, backward_dst, delta_at, count, every, col_blocks)
-    )
-    grad = lax.optimization_barrier(total.astype(BF))
+    sums = backward_product(blocks, backward_dst, delta_at, count, every, col_blocks)
     grad_scale = float(nodes * row_devices * col_devices) ** (-0.5)
-    feature_grad = jnp.einsum("khb,ih->kbi", grad, weight, preferred_element_type=F32)
-    return activated, feature_grad.astype(BF).reshape(nodes, BLK), weight_sum * grad_scale
+    feature_grad, weight_grad = finish(*scatter_rows(*sums), weight, grad_scale)
+    return activated, feature_grad, weight_grad
 
 
 def solution(mesh):

time: 144 us -> 145 us (level)
  waiting for transfers between devices: 38.7 us -> 42.8 us
  Pallas kernels: 13.2 us -> 11.2 us
  blocking collectives: 40.4 us -> 41.9 us
    ppermute x9, waiting for transfers between devices: 3.08 us -> 6.54 us  [row_swap(): return lax.ppermute(value, 'row', [(r, r ^ mask) for r in range(4 * NZ)])]
    ppermute x9, starting transfers between devices: 8.15 us -> 4.95 us  [row_swap(): return lax.ppermute(value, 'row', [(r, r ^ mask) for r in range(4 * NZ)])]
    ppermute x20, starting transfers between devices: 35.7 us -> 38.8 us  [z_shift(): return lax.ppermute(value, 'row', perm)]
    pallas_call x2, Pallas kernels: 12.1 us -> 9.23 us  [product(): pl.pallas_call(kernel, name=name, in_specs=[smem] * 3 + [pl.BlockSpec(mem...]
    all_to_all x1, blocking collectives: 18.9 us -> 20.7 us  [per_device(): lax.all_to_all(partial.reshape(col_devices, nodes, BLK), 'col', 0, 0)]
  transfers between devices with their start and end apart: 29 -> 29, of which waited for: 13 -> 15; matrix products, arithmetic and copies ran while one was open for 2% -> 1% of each run, Pallas kernels for 0% -> 0%
where the time goes in v3:
time: 145 us
  starting transfers between devices  43.8 us (30%)
  waiting for transfers between devices  42.8 us (30%)
  blocking collectives  41.9 us (29%)
  Pallas kernels  11.2 us (8%)
  other arithmetic  2.92 us (2%)
  between operations  1.76 us (1%)
    ppermute x20, starting transfers between devices, z_shift(): return lax.ppermute(value, 'row', perm)  38.8 us
    ppermute x20, waiting for transfers between devices, z_shift(): return lax.ppermute(value, 'row', perm)  36.3 us
    all_to_all x1, blocking collectives, per_device(): every = lax.all_to_all(message, 'col', 0, 0).reshape(-1, BLK, BLK)  21.2 us
    all_to_all x1, blocking collectives, per_device(): lax.all_to_all(partial.reshape(col_devices, nodes, BLK), 'col', 0, 0)  20.7 us
    pallas_call x2, Pallas kernels, product(): pl.pallas_call(kernel, name=name, in_specs=[smem] * 3 + [pl.BlockSpec(mem...  9.23 us
    ppermute x9, waiting for transfers between devices, row_swap(): return lax.ppermute(value, 'row', [(r, r ^ mask) for r in range(4 * NZ)])  6.54 us
    ppermute x9, starting transfers between devices, row_swap(): return lax.ppermute(value, 'row', [(r, r ^ mask) for r in range(4 * NZ)])  4.95 us
  transfers between devices with their start and end apart: 29, of which 15 were waited for; matrix products, arithmetic and copies ran while one was open for 1% of the time, Pallas kernels for 0%

profile of v3, /device:TPU:8, one launch (start us, length us, event | category | flops | bytes accessed | tf_op | source)
XLA Modules:
  0.0 144.5 jit_solution(890469411644926553)
XLA Ops:
  0.6 8.4 %collective-permute-start.4 = (bf16[4,128,128]{2,1,0:T(8,128)(2,1)}, bf16[4,128,128]{2,1,0:T(8,128)(2,1)S(1)}, u32[]{:S(2)}, u32[]{:S(2)}) collective-permute-start(bf16[4,128,128]{2,1,0:T(8,128)(2,1)} %bitcast.162), channel_id=1, source_target_pairs={{0,240},{8,248},{16,224},{24,232},{32,16},{40,24},{48,0},{56,8},{6... | collective-permute-start | bytes 393224 | tf_op jit(solution)/shard_map/ppermute | solution.py:42
  9.0 1.0 collective-permute-start.3
  11.1 2.2 %collective-permute-done.4 = bf16[4,128,128]{2,1,0:T(8,128)(2,1)S(1)} collective-permute-done((bf16[4,128,128]{2,1,0:T(8,128)(2,1)}, bf16[4,128,128]{2,1,0:T(8,128)(2,1)S(1)}, u32[]{:S(2)}, u32[]{:S(2)}) %collective-permute-start.4) | collective-permute-done | bytes 131104 | tf_op jit(solution)/shard_map/ppermute | solution.py:42
  13.2 1.7 %collective-permute-done.3 = bf16[4,128,128]{2,1,0:T(8,128)(2,1)S(1)} collective-permute-done((bf16[4,128,128]{2,1,0:T(8,128)(2,1)}, bf16[4,128,128]{2,1,0:T(8,128)(2,1)S(1)}, u32[]{:S(2)}, u32[]{:S(2)}) %collective-permute-start.3) | collective-permute-done | bytes 131104 | tf_op jit(solution)/shard_map/ppermute | solution.py:42
  14.9 3.7 %collective-permute-start.6 = (bf16[8,128,128]{2,1,0:T(8,128)(2,1)S(1)}, bf16[8,128,128]{2,1,0:T(8,128)(2,1)S(1)}, u32[]{:S(2)}, u32[]{:S(2)}) collective-permute-start(bf16[8,128,128]{2,1,0:T(8,128)(2,1)S(1)} %pad_maximum_fusion.8), channel_id=1, source_target_pairs={{0,224},{8,232},{16,240},{24,248},{32,0},{40,8},{48,16},{56,24},{6... | collective-permute-start | bytes 786440 | tf_op jit(solution)/shard_map/ppermute | solution.py:42
  18.6 1.3 collective-permute-done.2
  20.1 2.1 %collective-permute-start = (bf16[4,128,128]{2,1,0:T(8,128)(2,1)}, bf16[4,128,128]{2,1,0:T(8,128)(2,1)S(1)}, u32[]{:S(2)}, u32[]{:S(2)}) collective-permute-start(bf16[4,128,128]{2,1,0:T(8,128)(2,1)} %bitcast.166), channel_id=1, source_target_pairs={{0,16},{8,24},{16,0},{24,8},{32,48},{40,56},{48,32},{56,40},{64,80... | collective-permute-start | bytes 393224 | tf_op jit(solution)/shard_map/ppermute | solution.py:46
  22.1 1.2 collective-permute-done.6
  23.3 3.7 %collective-permute-start.8 = (bf16[8,128,128]{2,1,0:T(8,128)(2,1)S(1)}, bf16[8,128,128]{2,1,0:T(8,128)(2,1)S(1)}, u32[]{:S(2)}, u32[]{:S(2)}) collective-permute-start(bf16[8,128,128]{2,1,0:T(8,128)(2,1)S(1)} %collective-permute-done.6), channel_id=1, source_target_pairs={{0,224},{8,232},{16,240},{24,248},{32,0},{40,8},{48,16},{56,24},{6... | collective-permute-start | bytes 786440 | tf_op jit(solution)/shard_map/ppermute | solution.py:42
  27.0 1.0 pad_maximum_fusion.refs_0_
  28.1 2.7 %collective-permute-done.8.refs_3_ = bf16[8,128,128]{2,1,0:T(8,128)(2,1)S(1)} collective-permute-done((bf16[8,128,128]{2,1,0:T(8,128)(2,1)S(1)}, bf16[8,128,128]{2,1,0:T(8,128)(2,1)S(1)}, u32[]{:S(2)}, u32[]{:S(2)}) %collective-permute-start.8) | collective-permute-done | bytes 262176 | tf_op jit(solution)/shard_map/ppermute | solution.py:42
  30.9 4.7 %collective-permute-done.7 = bf16[8,128,128]{2,1,0:T(8,128)(2,1)S(1)} collective-permute-done((bf16[8,128,128]{2,1,0:T(8,128)(2,1)S(1)}, bf16[8,128,128]{2,1,0:T(8,128)(2,1)S(1)}, u32[]{:S(2)}, u32[]{:S(2)}) %collective-permute-start.7) | collective-permute-done | bytes 262176 | tf_op jit(solution)/shard_map/ppermute | solution.py:42
  35.8 3.3 %collective-permute-start.10 = (bf16[4,128,128]{2,1,0:T(8,128)(2,1)S(1)}, bf16[4,128,128]{2,1,0:T(8,128)(2,1)S(1)}, u32[]{:S(2)}, u32[]{:S(2)}) collective-permute-start(bf16[4,128,128]{2,1,0:T(8,128)(2,1)S(1)} %pad_maximum_fusion.14), channel_id=1, source_target_pairs={{0,224},{8,232},{16,240},{24,248},{32,0},{40,8},{48,16},{56,24},{6... | collective-permute-start | bytes 393224 | tf_op jit(solution)/shard_map/ppermute | solution.py:42
  39.6 2.4 %collective-permute-done.9 = bf16[4,128,128]{2,1,0:T(8,128)(2,1)S(1)} collective-permute-done((bf16[4,128,128]{2,1,0:T(8,128)(2,1)S(1)}, bf16[4,128,128]{2,1,0:T(8,128)(2,1)S(1)}, u32[]{:S(2)}, u32[]{:S(2)}) %collective-permute-start.9) | collective-permute-done | bytes 131104 | tf_op jit(solution)/shard_map/ppermute | solution.py:42
  44.4 4.8 %forward_product.1 = bf16[32,128,128]{2,1,0:T(8,128)(2,1)S(1)} custom-call(s32[256]{0:T(256)S(1)} %get-tuple-element.117.dst, s32[256]{0:T(256)S(1)} %get-tuple-element.120.src, s32[1]{0:T(128)} %bitcast.154.count, bf16[256,128,128]{2,1,0:T(8,128)(2,1)} %bitcast.159, bf16[16,128,128]{2,1,0:T(8,128)(2,1)S(1)} %pad_maximum_fusion.refs_0_, ...), custom_call_target="tpu_custom_call" | custom-call | flops 1073741824 | bytes 14680064 | tf_op jit(solution)/shard_map/forward_product/pallas_call | solution.py:124
  49.2 20.7 %all_to_all.10.parts = bf16[8,512,128]{2,1,0:T(8,128)(2,1)S(1)} all-to-all(bf16[8,512,128]{2,1,0:T(8,128)(2,1)S(1)} %bitcast.157), channel_id=1, replica_groups=mesh['row'=32,'col'=8] {'col'}, dimensions={0} | all-to-all | bytes 2097152 | tf_op jit(solution)/shard_map/all_to_all | solution.py:371
  69.9 1.0 middle.1
  70.9 21.2 %all_to_all.11 = bf16[8,5,128,128]{3,2,1,0:T(8,128)(2,1)S(1)} all-to-all(bf16[8,5,128,128]{3,2,1,0:T(8,128)(2,1)S(1)} %get-tuple-element.48), channel_id=1, replica_groups=mesh['row'=32,'col'=8] {'col'}, dimensions={0} | all-to-all | bytes 2621440 | tf_op jit(solution)/shard_map/all_to_all | solution.py:373
  92.2 4.4 %backward_product.1 = (bf16[64,128,128]{2,1,0:T(8,128)(2,1)S(1)}, bf16[18,128,128]{2,1,0:T(8,128)(2,1)S(1)}, bf16[48,128,128]{2,1,0:T(8,128)(2,1)S(1)}, f32[128,128]{1,0:T(8,128)S(1)}) custom-call(s32[256]{0:T(256)S(1)} %get-tuple-element.121.dst, s32[256]{0:T(256)S(1)} %get-tuple-element.116.src, s32[1]{0:T(128)} %bitcast.155.count, ...), custom_call_target="tpu_custom_call" | custom-call | flops 1073741824 | bytes 14680064 | tf_op jit(solution)/shard_map/backward_product/pallas_call | solution.py:124
  97.2 1.5 %collective-permute-done.17 = bf16[18,128,128]{2,1,0:T(8,128)(2,1)S(1)} collective-permute-done((bf16[18,128,128]{2,1,0:T(8,128)(2,1)S(1)}, bf16[18,128,128]{2,1,0:T(8,128)(2,1)S(1)}, u32[]{:S(2)}, u32[]{:S(2)}) %collective-permute-start.17) | collective-permute-done | bytes 589856 | tf_op jit(solution)/shard_map/ppermute | solution.py:46
  99.0 4.2 %collective-permute-start.19 = (bf16[3,128,128]{2,1,0:T(8,128)(2,1)S(1)}, bf16[3,128,128]{2,1,0:T(8,128)(2,1)S(1)}, u32[]{:S(2)}, u32[]{:S(2)}) collective-permute-start(bf16[3,128,128]{2,1,0:T(8,128)(2,1)S(1)} %get-tuple-element.54), channel_id=1, source_target_pairs={{0,224},{8,232},{16,240},{24,248},{32,0},{40,8},{48,16},{56,24},{6... | collective-permute-start | bytes 294920 | tf_op jit(solution)/shard_map/ppermute | solution.py:42
  103.1 3.0 %collective-permute-done.18 = bf16[3,128,128]{2,1,0:T(8,128)(2,1)S(1)} collective-permute-done((bf16[3,128,128]{2,1,0:T(8,128)(2,1)S(1)}, bf16[3,128,128]{2,1,0:T(8,128)(2,1)S(1)}, u32[]{:S(2)}, u32[]{:S(2)}) %collective-permute-start.18) | collective-permute-done | bytes 98336 | tf_op jit(solution)/shard_map/ppermute | solution.py:42
  106.5 3.2 %collective-permute-start.21 = (bf16[7,128,128]{2,1,0:T(8,128)(2,1)S(1)}, bf16[7,128,128]{2,1,0:T(8,128)(2,1)S(1)}, u32[]{:S(2)}, u32[]{:S(2)}) collective-permute-start(bf16[7,128,128]{2,1,0:T(8,128)(2,1)S(1)} %pad_maximum_fusion.11), channel_id=1, source_target_pairs={{0,224},{8,232},{16,240},{24,248},{32,0},{40,8},{48,16},{56,24},{6... | collective-permute-start | bytes 688136 | tf_op jit(solution)/shard_map/ppermute | solution.py:42
  109.7 5.1 %collective-permute-done.20 = bf16[7,128,128]{2,1,0:T(8,128)(2,1)S(1)} collective-permute-done((bf16[7,128,128]{2,1,0:T(8,128)(2,1)S(1)}, bf16[7,128,128]{2,1,0:T(8,128)(2,1)S(1)}, u32[]{:S(2)}, u32[]{:S(2)}) %collective-permute-start.20) | collective-permute-done | bytes 229408 | tf_op jit(solution)/shard_map/ppermute | solution.py:42
  115.7 3.2 %collective-permute-start.23 = (bf16[9,128,128]{2,1,0:T(8,128)(2,1)S(1)}, bf16[9,128,128]{2,1,0:T(8,128)(2,1)S(1)}, u32[]{:S(2)}, u32[]{:S(2)}) collective-permute-start(bf16[9,128,128]{2,1,0:T(8,128)(2,1)S(1)} %pad_maximum_fusion.4), channel_id=1, source_target_pairs={{0,224},{8,232},{16,240},{24,248},{32,0},{40,8},{48,16},{56,24},{6... | collective-permute-start | bytes 884744 | tf_op jit(solution)/shard_map/ppermute | solution.py:42
  118.9 5.6 %collective-permute-done.22 = bf16[9,128,128]{2,1,0:T(8,128)(2,1)S(1)} collective-permute-done((bf16[9,128,128]{2,1,0:T(8,128)(2,1)S(1)}, bf16[9,128,128]{2,1,0:T(8,128)(2,1)S(1)}, u32[]{:S(2)}, u32[]{:S(2)}) %collective-permute-start.22) | collective-permute-done | bytes 294944 | tf_op jit(solution)/shard_map/ppermute | solution.py:42
  125.0 3.2 %collective-permute-start.25 = (bf16[9,128,128]{2,1,0:T(8,128)(2,1)S(1)}, bf16[9,128,128]{2,1,0:T(8,128)(2,1)S(1)}, u32[]{:S(2)}, u32[]{:S(2)}) collective-permute-start(bf16[9,128,128]{2,1,0:T(8,128)(2,1)S(1)} %pad_maximum_fusion.6), channel_id=1, source_target_pairs={{0,224},{8,232},{16,240},{24,248},{32,0},{40,8},{48,16},{56,24},{6... | collective-permute-start | bytes 884744 | tf_op jit(solution)/shard_map/ppermute | solution.py:42
  128.2 4.7 %collective-permute-done.24 = bf16[9,128,128]{2,1,0:T(8,128)(2,1)S(1)} collective-permute-done((bf16[9,128,128]{2,1,0:T(8,128)(2,1)S(1)}, bf16[9,128,128]{2,1,0:T(8,128)(2,1)S(1)}, u32[]{:S(2)}, u32[]{:S(2)}) %collective-permute-start.24) | collective-permute-done | bytes 294944 | tf_op jit(solution)/shard_map/ppermute | solution.py:42
  133.2 3.3 %collective-permute-start.27 = (bf16[4,128,128]{2,1,0:T(8,128)(2,1)S(1)}, bf16[4,128,128]{2,1,0:T(8,128)(2,1)S(1)}, u32[]{:S(2)}, u32[]{:S(2)}) collective-permute-start(bf16[4,128,128]{2,1,0:T(8,128)(2,1)S(1)} %get-tuple-element.75), channel_id=1, source_target_pairs={{0,224},{8,232},{16,240},{24,248},{32,0},{40,8},{48,16},{56,24},{6... | collective-permute-start | bytes 393224 | tf_op jit(solution)/shard_map/ppermute | solution.py:42
  136.7 1.0 collective-permute-start.28
  137.7 1.6 %collective-permute-done.26 = bf16[4,128,128]{2,1,0:T(8,128)(2,1)S(1)} collective-permute-done((bf16[4,128,128]{2,1,0:T(8,128)(2,1)S(1)}, bf16[4,128,128]{2,1,0:T(8,128)(2,1)S(1)}, u32[]{:S(2)}, u32[]{:S(2)}) %collective-permute-start.26) | collective-permute-done | bytes 131104 | tf_op jit(solution)/shard_map/ppermute | solution.py:42
  139.4 4.2 %collective-permute-done.28.refs_1_ = bf16[5,128,128]{2,1,0:T(8,128)(2,1)S(1)} collective-permute-done((bf16[5,128,128]{2,1,0:T(8,128)(2,1)S(1)}, bf16[5,128,128]{2,1,0:T(8,128)(2,1)S(1)}, u32[]{:S(2)}, u32[]{:S(2)}) %collective-permute-start.28) | collective-permute-done | bytes 163872 | tf_op jit(solution)/shard_map/ppermute | solution.py:46
  (87 shorter events, 7.4 us)
Async XLA Ops:
  0.6 12.6 %collective-permute-start.4 = (bf16[4,128,128]{2,1,0:T(8,128)(2,1)}, bf16[4,128,128]{2,1,0:T(8,128)(2,1)S(1)}, u32[]{:S(2)}, u32[]{:S(2)}) collective-permute-start(bf16[4,128,128]{2,1,0:T(8,128)(2,1)} %bitcast.162), channel_id=1, source_target_pairs={{0,240},{8,248},{16,224},{24,232},{32,16},{40,24},{48,0},{56,8},{6... | collective-permute-start | bytes 393224 | tf_op jit(solution)/shard_map/ppermute | solution.py:42
  9.0 5.9 %collective-permute-start.3 = (bf16[4,128,128]{2,1,0:T(8,128)(2,1)}, bf16[4,128,128]{2,1,0:T(8,128)(2,1)S(1)}, u32[]{:S(2)}, u32[]{:S(2)}) collective-permute-start(bf16[4,128,128]{2,1,0:T(8,128)(2,1)} %bitcast.163), channel_id=1, source_target_pairs={{0,224},{8,232},{16,240},{24,248},{32,0},{40,8},{48,16},{56,24},{6... | collective-permute-start | bytes 393224 | tf_op jit(solution)/shard_map/ppermute | solution.py:42
  10.0 9.9 %collective-permute-start.2 = (bf16[4,128,128]{2,1,0:T(8,128)(2,1)}, bf16[4,128,128]{2,1,0:T(8,128)(2,1)S(1)}, u32[]{:S(2)}, u32[]{:S(2)}) collective-permute-start(bf16[4,128,128]{2,1,0:T(8,128)(2,1)} %bitcast.164), channel_id=1, source_target_pairs={{0,48},{8,56},{16,32},{24,40},{32,80},{40,88},{48,64},{56,72},{64,... | collective-permute-start | bytes 393224 | tf_op jit(solution)/shard_map/ppermute | solution.py:42
  11.0 8.9 %collective-permute-start.1 = (bf16[4,128,128]{2,1,0:T(8,128)(2,1)}, bf16[4,128,128]{2,1,0:T(8,128)(2,1)S(1)}, u32[]{:S(2)}, u32[]{:S(2)}) collective-permute-start(bf16[4,128,128]{2,1,0:T(8,128)(2,1)} %bitcast.165), channel_id=1, source_target_pairs={{0,32},{8,40},{16,48},{24,56},{32,64},{40,72},{48,80},{56,88},{64,... | collective-permute-start | bytes 393224 | tf_op jit(solution)/shard_map/ppermute | solution.py:42
  14.9 8.4 %collective-permute-start.6 = (bf16[8,128,128]{2,1,0:T(8,128)(2,1)S(1)}, bf16[8,128,128]{2,1,0:T(8,128)(2,1)S(1)}, u32[]{:S(2)}, u32[]{:S(2)}) collective-permute-start(bf16[8,128,128]{2,1,0:T(8,128)(2,1)S(1)} %pad_maximum_fusion.8), channel_id=1, source_target_pairs={{0,224},{8,232},{16,240},{24,248},{32,0},{40,8},{48,16},{56,24},{6... | collective-permute-start | bytes 786440 | tf_op jit(solution)/shard_map/ppermute | solution.py:42
  20.0 8.0 %collective-permute-start.5 = (bf16[8,128,128]{2,1,0:T(8,128)(2,1)S(1)}, bf16[8,128,128]{2,1,0:T(8,128)(2,1)S(1)}, u32[]{:S(2)}, u32[]{:S(2)}) collective-permute-start(bf16[8,128,128]{2,1,0:T(8,128)(2,1)S(1)} %pad_maximum_fusion.7), channel_id=1, source_target_pairs={{0,32},{8,40},{16,48},{24,56},{32,64},{40,72},{48,80},{56,88},{64,... | collective-permute-start | bytes 786440 | tf_op jit(solution)/shard_map/ppermute | solution.py:42
  20.1 6.9 %collective-permute-start = (bf16[4,128,128]{2,1,0:T(8,128)(2,1)}, bf16[4,128,128]{2,1,0:T(8,128)(2,1)S(1)}, u32[]{:S(2)}, u32[]{:S(2)}) collective-permute-start(bf16[4,128,128]{2,1,0:T(8,128)(2,1)} %bitcast.166), channel_id=1, source_target_pairs={{0,16},{8,24},{16,0},{24,8},{32,48},{40,56},{48,32},{56,40},{64,80... | collective-permute-start | bytes 393224 | tf_op jit(solution)/shard_map/ppermute | solution.py:46
  23.3 7.6 %collective-permute-start.8 = (bf16[8,128,128]{2,1,0:T(8,128)(2,1)S(1)}, bf16[8,128,128]{2,1,0:T(8,128)(2,1)S(1)}, u32[]{:S(2)}, u32[]{:S(2)}) collective-permute-start(bf16[8,128,128]{2,1,0:T(8,128)(2,1)S(1)} %collective-permute-done.6), channel_id=1, source_target_pairs={{0,224},{8,232},{16,240},{24,248},{32,0},{40,8},{48,16},{56,24},{6... | collective-permute-start | bytes 786440 | tf_op jit(solution)/shard_map/ppermute | solution.py:42
  28.0 14.9 %copy-start.2 = (s32[1,1,2,256]{3,2,1,0:T(2,128)S(1)}, s32[1,1,2,256]{3,2,1,0:T(2,128)}, u32[]{:S(2)}) copy-start(s32[1,1,2,256]{3,2,1,0:T(2,128)} %param.9) | copy-start | bytes 6148
  28.0 7.7 %collective-permute-start.7 = (bf16[8,128,128]{2,1,0:T(8,128)(2,1)S(1)}, bf16[8,128,128]{2,1,0:T(8,128)(2,1)S(1)}, u32[]{:S(2)}, u32[]{:S(2)}) collective-permute-start(bf16[8,128,128]{2,1,0:T(8,128)(2,1)S(1)} %collective-permute-done.5), channel_id=1, source_target_pairs={{0,32},{8,40},{16,48},{24,56},{32,64},{40,72},{48,80},{56,88},{64,... | collective-permute-start | bytes 786440 | tf_op jit(solution)/shard_map/ppermute | solution.py:42
  35.7 6.3 %collective-permute-start.9 = (bf16[4,128,128]{2,1,0:T(8,128)(2,1)S(1)}, bf16[4,128,128]{2,1,0:T(8,128)(2,1)S(1)}, u32[]{:S(2)}, u32[]{:S(2)}) collective-permute-start(bf16[4,128,128]{2,1,0:T(8,128)(2,1)S(1)} %pad_maximum_fusion.13), channel_id=1, source_target_pairs={{0,32},{8,40},{16,48},{24,56},{32,64},{40,72},{48,80},{56,88},{64,... | collective-permute-start | bytes 393224 | tf_op jit(solution)/shard_map/ppermute | solution.py:42
  35.8 6.2 %collective-permute-start.10 = (bf16[4,128,128]{2,1,0:T(8,128)(2,1)S(1)}, bf16[4,128,128]{2,1,0:T(8,128)(2,1)S(1)}, u32[]{:S(2)}, u32[]{:S(2)}) collective-permute-start(bf16[4,128,128]{2,1,0:T(8,128)(2,1)S(1)} %pad_maximum_fusion.14), channel_id=1, source_target_pairs={{0,224},{8,232},{16,240},{24,248},{32,0},{40,8},{48,16},{56,24},{6... | collective-permute-start | bytes 393224 | tf_op jit(solution)/shard_map/ppermute | solution.py:42
  39.1 4.5 %collective-permute-start.14 = (bf16[8,128,128]{2,1,0:T(8,128)(2,1)S(1)}, bf16[8,128,128]{2,1,0:T(8,128)(2,1)S(1)}, u32[]{:S(2)}, u32[]{:S(2)}) collective-permute-start(bf16[8,128,128]{2,1,0:T(8,128)(2,1)S(1)} %collective-permute-done.8.refs_3_), channel_id=1, source_target_pairs={{0,8},{8,0},{16,24},{24,16},{32,40},{40,32},{48,56},{56,48},{64,72... | collective-permute-start | bytes 786440 | tf_op jit(solution)/shard_map/ppermute | solution.py:46
  39.1 5.3 %collective-permute-start.11 = (bf16[16,128,128]{2,1,0:T(8,128)(2,1)S(1)}, bf16[16,128,128]{2,1,0:T(8,128)(2,1)S(1)}, u32[]{:S(2)}, u32[]{:S(2)}) collective-permute-start(bf16[16,128,128]{2,1,0:T(8,128)(2,1)S(1)} %pad_maximum_fusion.refs_0_), channel_id=1, source_target_pairs={{0,8},{8,0},{16,24},{24,16},{32,40},{40,32},{48,56},{56,48},{64,72... | collective-permute-start | bytes 1572872 | tf_op jit(solution)/shard_map/ppermute | solution.py:46
  39.6 4.8 %collective-permute-start.12 = (bf16[16,128,128]{2,1,0:T(8,128)(2,1)S(1)}, bf16[16,128,128]{2,1,0:T(8,128)(2,1)S(1)}, u32[]{:S(2)}, u32[]{:S(2)}) collective-permute-start(bf16[16,128,128]{2,1,0:T(8,128)(2,1)S(1)} %pad_maximum_fusion.1.refs_1_), channel_id=1, source_target_pairs={{0,8},{8,0},{16,24},{24,16},{32,40},{40,32},{48,56},{56,48},{64,72... | collective-permute-start | bytes 1572872 | tf_op jit(solution)/shard_map/ppermute | solution.py:46
  42.0 2.4 %collective-permute-start.13 = (bf16[16,128,128]{2,1,0:T(8,128)(2,1)S(1)}, bf16[16,128,128]{2,1,0:T(8,128)(2,1)}, u32[]{:S(2)}, u32[]{:S(2)}) collective-permute-start(bf16[16,128,128]{2,1,0:T(8,128)(2,1)S(1)} %pad_maximum_fusion.2.refs_2_), channel_id=1, source_target_pairs={{0,8},{8,0},{16,24},{24,16},{32,40},{40,32},{48,56},{56,48},{64,72... | collective-permute-start | bytes 1572872 | tf_op jit(solution)/shard_map/ppermute | solution.py:46
  42.1 2.3 %collective-permute-start.15 = (bf16[8,128,128]{2,1,0:T(8,128)(2,1)S(1)}, bf16[8,128,128]{2,1,0:T(8,128)(2,1)}, u32[]{:S(2)}, u32[]{:S(2)}) collective-permute-start(bf16[8,128,128]{2,1,0:T(8,128)(2,1)S(1)} %pad_maximum_fusion.9.refs_4_), channel_id=1, source_target_pairs={{0,8},{8,0},{16,24},{24,16},{32,40},{40,32},{48,56},{56,48},{64,72... | collective-permute-start | bytes 786440 | tf_op jit(solution)/shard_map/ppermute | solution.py:46
  49.2 20.7 %copy-start = (bf16[512,128]{1,0:T(8,128)(2,1)S(1)}, bf16[512,128]{1,0:T(8,128)(2,1)}, u32[]{:S(2)}) copy-start(bf16[512,128]{1,0:T(8,128)(2,1)} %cotangent.1) | copy-start | bytes 393220
  49.2 20.7 %copy-start.1 = (bf16[128,128]{1,0:T(8,128)(2,1)S(1)}, bf16[128,128]{1,0:T(8,128)(2,1)}, u32[]{:S(2)}) copy-start(bf16[128,128]{1,0:T(8,128)(2,1)} %refs_3_.1) | copy-start | bytes 98308
  96.6 2.1 %collective-permute-start.17 = (bf16[18,128,128]{2,1,0:T(8,128)(2,1)S(1)}, bf16[18,128,128]{2,1,0:T(8,128)(2,1)S(1)}, u32[]{:S(2)}, u32[]{:S(2)}) collective-permute-start(bf16[18,128,128]{2,1,0:T(8,128)(2,1)S(1)} %get-tuple-element.51), channel_id=1, source_target_pairs={{0,8},{8,0},{16,24},{24,16},{32,40},{40,32},{48,56},{56,48},{64,72... | collective-permute-start | bytes 1769480 | tf_op jit(solution)/shard_map/ppermute | solution.py:46
  96.7 18.2 %collective-permute-start.16 = (bf16[48,128,128]{2,1,0:T(8,128)(2,1)S(1)}, bf16[48,128,128]{2,1,0:T(8,128)(2,1)S(1)}, u32[]{:S(2)}, u32[]{:S(2)}) collective-permute-start(bf16[48,128,128]{2,1,0:T(8,128)(2,1)S(1)} %get-tuple-element.50), channel_id=1, source_target_pairs={{0,8},{8,0},{16,24},{24,16},{32,40},{40,32},{48,56},{56,48},{64,72... | collective-permute-start | bytes 4718600 | tf_op jit(solution)/shard_map/ppermute | solution.py:46
  98.9 7.3 %collective-permute-start.18 = (bf16[3,128,128]{2,1,0:T(8,128)(2,1)S(1)}, bf16[3,128,128]{2,1,0:T(8,128)(2,1)S(1)}, u32[]{:S(2)}, u32[]{:S(2)}) collective-permute-start(bf16[3,128,128]{2,1,0:T(8,128)(2,1)S(1)} %get-tuple-element.53), channel_id=1, source_target_pairs={{0,32},{8,40},{16,48},{24,56},{32,64},{40,72},{48,80},{56,88},{64,... | collective-permute-start | bytes 294920 | tf_op jit(solution)/shard_map/ppermute | solution.py:42
  99.0 7.2 %collective-permute-start.19 = (bf16[3,128,128]{2,1,0:T(8,128)(2,1)S(1)}, bf16[3,128,128]{2,1,0:T(8,128)(2,1)S(1)}, u32[]{:S(2)}, u32[]{:S(2)}) collective-permute-start(bf16[3,128,128]{2,1,0:T(8,128)(2,1)S(1)} %get-tuple-element.54), channel_id=1, source_target_pairs={{0,224},{8,232},{16,240},{24,248},{32,0},{40,8},{48,16},{56,24},{6... | collective-permute-start | bytes 294920 | tf_op jit(solution)/shard_map/ppermute | solution.py:42
  106.4 8.4 %collective-permute-start.20 = (bf16[7,128,128]{2,1,0:T(8,128)(2,1)S(1)}, bf16[7,128,128]{2,1,0:T(8,128)(2,1)S(1)}, u32[]{:S(2)}, u32[]{:S(2)}) collective-permute-start(bf16[7,128,128]{2,1,0:T(8,128)(2,1)S(1)} %pad_maximum_fusion.10), channel_id=1, source_target_pairs={{0,32},{8,40},{16,48},{24,56},{32,64},{40,72},{48,80},{56,88},{64,... | collective-permute-start | bytes 688136 | tf_op jit(solution)/shard_map/ppermute | solution.py:42
  106.5 8.4 %collective-permute-start.21 = (bf16[7,128,128]{2,1,0:T(8,128)(2,1)S(1)}, bf16[7,128,128]{2,1,0:T(8,128)(2,1)S(1)}, u32[]{:S(2)}, u32[]{:S(2)}) collective-permute-start(bf16[7,128,128]{2,1,0:T(8,128)(2,1)S(1)} %pad_maximum_fusion.11), channel_id=1, source_target_pairs={{0,224},{8,232},{16,240},{24,248},{32,0},{40,8},{48,16},{56,24},{6... | collective-permute-start | bytes 688136 | tf_op jit(solution)/shard_map/ppermute | solution.py:42
  115.6 8.9 %collective-permute-start.22 = (bf16[9,128,128]{2,1,0:T(8,128)(2,1)S(1)}, bf16[9,128,128]{2,1,0:T(8,128)(2,1)S(1)}, u32[]{:S(2)}, u32[]{:S(2)}) collective-permute-start(bf16[9,128,128]{2,1,0:T(8,128)(2,1)S(1)} %pad_maximum_fusion.3), channel_id=1, source_target_pairs={{0,32},{8,40},{16,48},{24,56},{32,64},{40,72},{48,80},{56,88},{64,... | collective-permute-start | bytes 884744 | tf_op jit(solution)/shard_map/ppermute | solution.py:42
  115.7 8.8 %collective-permute-start.23 = (bf16[9,128,128]{2,1,0:T(8,128)(2,1)S(1)}, bf16[9,128,128]{2,1,0:T(8,128)(2,1)S(1)}, u32[]{:S(2)}, u32[]{:S(2)}) collective-permute-start(bf16[9,128,128]{2,1,0:T(8,128)(2,1)S(1)} %pad_maximum_fusion.4), channel_id=1, source_target_pairs={{0,224},{8,232},{16,240},{24,248},{32,0},{40,8},{48,16},{56,24},{6... | collective-permute-start | bytes 884744 | tf_op jit(solution)/shard_map/ppermute | solution.py:42
  124.9 8.0 %collective-permute-start.24 = (bf16[9,128,128]{2,1,0:T(8,128)(2,1)S(1)}, bf16[9,128,128]{2,1,0:T(8,128)(2,1)S(1)}, u32[]{:S(2)}, u32[]{:S(2)}) collective-permute-start(bf16[9,128,128]{2,1,0:T(8,128)(2,1)S(1)} %pad_maximum_fusion.5), channel_id=1, source_target_pairs={{0,32},{8,40},{16,48},{24,56},{32,64},{40,72},{48,80},{56,88},{64,... | collective-permute-start | bytes 884744 | tf_op jit(solution)/shard_map/ppermute | solution.py:42
  125.0 8.0 %collective-permute-start.25 = (bf16[9,128,128]{2,1,0:T(8,128)(2,1)S(1)}, bf16[9,128,128]{2,1,0:T(8,128)(2,1)S(1)}, u32[]{:S(2)}, u32[]{:S(2)}) collective-permute-start(bf16[9,128,128]{2,1,0:T(8,128)(2,1)S(1)} %pad_maximum_fusion.6), channel_id=1, source_target_pairs={{0,224},{8,232},{16,240},{24,248},{32,0},{40,8},{48,16},{56,24},{6... | collective-permute-start | bytes 884744 | tf_op jit(solution)/shard_map/ppermute | solution.py:42
  133.1 6.3 %collective-permute-start.26 = (bf16[4,128,128]{2,1,0:T(8,128)(2,1)S(1)}, bf16[4,128,128]{2,1,0:T(8,128)(2,1)S(1)}, u32[]{:S(2)}, u32[]{:S(2)}) collective-permute-start(bf16[4,128,128]{2,1,0:T(8,128)(2,1)S(1)} %get-tuple-element.74), channel_id=1, source_target_pairs={{0,32},{8,40},{16,48},{24,56},{32,64},{40,72},{48,80},{56,88},{64,... | collective-permute-start | bytes 393224 | tf_op jit(solution)/shard_map/ppermute | solution.py:42
  133.2 6.2 %collective-permute-start.27 = (bf16[4,128,128]{2,1,0:T(8,128)(2,1)S(1)}, bf16[4,128,128]{2,1,0:T(8,128)(2,1)S(1)}, u32[]{:S(2)}, u32[]{:S(2)}) collective-permute-start(bf16[4,128,128]{2,1,0:T(8,128)(2,1)S(1)} %get-tuple-element.75), channel_id=1, source_target_pairs={{0,224},{8,232},{16,240},{24,248},{32,0},{40,8},{48,16},{56,24},{6... | collective-permute-start | bytes 393224 | tf_op jit(solution)/shard_map/ppermute | solution.py:42
  136.7 6.9 %collective-permute-start.28 = (bf16[5,128,128]{2,1,0:T(8,128)(2,1)S(1)}, bf16[5,128,128]{2,1,0:T(8,128)(2,1)S(1)}, u32[]{:S(2)}, u32[]{:S(2)}) collective-permute-start(bf16[5,128,128]{2,1,0:T(8,128)(2,1)S(1)} %pad_maximum_fusion.12), channel_id=1, source_target_pairs={{0,16},{8,24},{16,0},{24,8},{32,48},{40,56},{48,32},{56,40},{64,80... | collective-permute-start | bytes 491528 | tf_op jit(solution)/shard_map/ppermute | solution.py:46

commit v4 on v3

--- a/solution.py
+++ b/solution.py
@@ -9,13 +9,14 @@
 BLK = 128
 BPD = 4
 HALF = 2
-CHUNK = 32
-UNROLL = 32
+CHUNK = 64
+UNROLL = 64
 VMEM_LIMIT = 24 << 20
 BF = jnp.bfloat16
 F32 = jnp.float32
 
-PLACES = ((0, 4), (8, 12), (24, 28), (40, 44), (56, 60), (48, 52), (32, 36), (16, 20))
+PLACES = ((0, 4), (8, 16), (20, 32), (36, 48), (52, 60), (40, 56), (24, 44), (12, 28))
+
 
 ORDER = (
     (4, 1), (3, 1), (5, 1), (4, 0), (2, 1), (6, 1), (3, 0), (5, 0),
@@ -37,8 +38,8 @@
     return jnp.concatenate(values, axis=0)
 
 
-def z_shift(value, step, mask=0):
-    perm = [(r, ((r // 4 + step) % NZ) * 4 + (r % 4 ^ mask)) for r in range(4 * NZ)]
+def z_shift(value, step):
+    perm = [(r, ((r // 4 + step) % NZ) * 4 + r % 4) for r in range(4 * NZ)]
     return lax.ppermute(value, "row", perm)
 
 
@@ -147,9 +148,9 @@
         dst,
         src,
         count,
-        [pltpu.with_memory_space_constraint(piece, pltpu.VMEM) for piece in pieces],
+        pieces,
         [jax.ShapeDtypeStruct((num_dst, BLK, BLK), BF)],
-        pltpu.VMEM,
+        pl.ANY,
         [
             pltpu.VMEM((num_dst + 1, BLK, BLK), F32),
             pltpu.VMEM((held, BLK, BLK), BF),
@@ -225,20 +226,13 @@
 def gather_rows(own):
     mate = row_swap(own, 2)
     up1, down1 = z_shift(own, 1), z_shift(own, -1)
-    mate_up1, mate_down1 = z_shift(own, 1, 2), z_shift(own, -1, 2)
-    up2, down2 = z_shift(cat(up1, mate_up1), 1), z_shift(cat(down1, mate_down1), -1)
+    up2, down2 = z_shift(cat(mate, up1), 1), z_shift(cat(down1, mate), -1)
     up3, down3 = z_shift(up2, 1), z_shift(down2, -1)
-    up4 = cat(up3[:HALF], up3[BPD : BPD + HALF])
-    down4 = cat(down3[HALF:BPD], down3[BPD + HALF :])
-    groups = [
-        cat(own, mate, up1, mate_up1),
-        cat(down1, mate_down1, up2),
-        cat(down2, up3),
-        down3,
-    ]
+    up4, down4 = z_shift(up3[: BPD + HALF], 1), z_shift(down3[HALF:], -1)
+    up5, down5 = z_shift(up4[:HALF], 1), z_shift(down4[BPD:], -1)
+    groups = [cat(own, mate, up1, down1), cat(up2, down2), cat(up3, down3)]
     groups, up4, down4 = lax.optimization_barrier((groups, up4, down4))
-    up4, down4 = z_shift(up4, 1), z_shift(down4, -1)
-    groups.append(cat(up4[:HALF], down4[:HALF], up4[HALF:], down4[HALF:]))
+    groups += [cat(up4, down4), cat(up5, down5)]
     return groups + [row_swap(group, 1) for group in groups]
 
 

time: 145 us -> 144 us (level)
  blocking collectives: 41.9 us -> 39.5 us
    ppermute x9, starting transfers between devices: 4.95 us -> 8.19 us  [row_swap(): return lax.ppermute(value, 'row', [(r, r ^ mask) for r in range(4 * NZ)])]
    ppermute x20, starting transfers between devices: 38.8 us -> 36.8 us  [z_shift(): return lax.ppermute(value, 'row', perm)]
    all_to_all x1, blocking collectives: 21.2 us -> 19.3 us  [per_device(): every = lax.all_to_all(message, 'col', 0, 0).reshape(-1, BLK, BLK)]
  transfers between devices with their start and end apart: 29 -> 29, of which waited for: 15 -> 17; matrix products, arithmetic and copies ran while one was open for 1% -> 2% of each run, Pallas kernels for 0% -> 0%
where the time goes in v4:
time: 144 us; the launch traced here: 142 us
  starting transfers between devices  45 us (31%)
  waiting for transfers between devices  41.9 us (29%)
  blocking collectives  39.5 us (27%)
  Pallas kernels  10.7 us (7%)
  other arithmetic  2.82 us (2%)
  between operations  1.68 us (1%)
    ppermute x20, starting transfers between devices, z_shift(): return lax.ppermute(value, 'row', perm)  36.8 us
    ppermute x20, waiting for transfers between devices, z_shift(): return lax.ppermute(value, 'row', perm)  35.2 us
    all_to_all x1, blocking collectives, per_device(): lax.all_to_all(partial.reshape(col_devices, nodes, BLK), 'col', 0, 0)  20.2 us
    all_to_all x1, blocking collectives, per_device(): every = lax.all_to_all(message, 'col', 0, 0).reshape(-1, BLK, BLK)  19.3 us
    pallas_call x2, Pallas kernels, product(): pl.pallas_call(kernel, name=name, in_specs=[smem] * 3 + [pl.BlockSpec(mem...  8.73 us
    ppermute x9, starting transfers between devices, row_swap(): return lax.ppermute(value, 'row', [(r, r ^ mask) for r in range(4 * NZ)])  8.19 us
    ppermute x9, waiting for transfers between devices, row_swap(): return lax.ppermute(value, 'row', [(r, r ^ mask) for r in range(4 * NZ)])  6.71 us
  transfers between devices with their start and end apart: 29, of which 17 were waited for; matrix products, arithmetic and copies ran while one was open for 2% of the time, Pallas kernels for 0%

profile of v4, /device:TPU:8, one launch (start us, length us, event | category | flops | bytes accessed | tf_op | source)
XLA Modules:
  0.0 142.5 jit_solution(1353263530553394483)
XLA Ops:
  0.6 5.9 %collective-permute-start.2 = (bf16[4,128,128]{2,1,0:T(8,128)(2,1)}, bf16[4,128,128]{2,1,0:T(8,128)(2,1)S(1)}, u32[]{:S(2)}, u32[]{:S(2)}) collective-permute-start(bf16[4,128,128]{2,1,0:T(8,128)(2,1)} %bitcast.162), channel_id=1, source_target_pairs={{0,224},{8,232},{16,240},{24,248},{32,0},{40,8},{48,16},{56,24},{6... | collective-permute-start | bytes 393224 | tf_op jit(solution)/shard_map/ppermute | solution.py:43
  6.6 3.0 %collective-permute-start = (bf16[4,128,128]{2,1,0:T(8,128)(2,1)}, bf16[4,128,128]{2,1,0:T(8,128)(2,1)S(1)}, u32[]{:S(2)}, u32[]{:S(2)}) collective-permute-start(bf16[4,128,128]{2,1,0:T(8,128)(2,1)} %bitcast.164), channel_id=1, source_target_pairs={{0,16},{8,24},{16,0},{24,8},{32,48},{40,56},{48,32},{56,40},{64,80... | collective-permute-start | bytes 393224 | tf_op jit(solution)/shard_map/ppermute | solution.py:47
  9.6 3.3 %collective-permute-done.1 = bf16[4,128,128]{2,1,0:T(8,128)(2,1)S(1)} collective-permute-done((bf16[4,128,128]{2,1,0:T(8,128)(2,1)}, bf16[4,128,128]{2,1,0:T(8,128)(2,1)S(1)}, u32[]{:S(2)}, u32[]{:S(2)}) %collective-permute-start.1) | collective-permute-done | bytes 131104 | tf_op jit(solution)/shard_map/ppermute | solution.py:43
  13.4 3.3 %collective-permute-start.4 = (bf16[8,128,128]{2,1,0:T(8,128)(2,1)S(1)}, bf16[8,128,128]{2,1,0:T(8,128)(2,1)S(1)}, u32[]{:S(2)}, u32[]{:S(2)}) collective-permute-start(bf16[8,128,128]{2,1,0:T(8,128)(2,1)S(1)} %get-tuple-element.103), channel_id=1, source_target_pairs={{0,224},{8,232},{16,240},{24,248},{32,0},{40,8},{48,16},{56,24},{6... | collective-permute-start | bytes 786440 | tf_op jit(solution)/shard_map/ppermute | solution.py:43
  17.3 3.8 %collective-permute-done.3 = bf16[8,128,128]{2,1,0:T(8,128)(2,1)S(1)} collective-permute-done((bf16[8,128,128]{2,1,0:T(8,128)(2,1)S(1)}, bf16[8,128,128]{2,1,0:T(8,128)(2,1)S(1)}, u32[]{:S(2)}, u32[]{:S(2)}) %collective-permute-start.3) | collective-permute-done | bytes 262176 | tf_op jit(solution)/shard_map/ppermute | solution.py:43
  21.2 3.2 %collective-permute-start.6 = (bf16[8,128,128]{2,1,0:T(8,128)(2,1)S(1)}, bf16[8,128,128]{2,1,0:T(8,128)(2,1)S(1)}, u32[]{:S(2)}, u32[]{:S(2)}) collective-permute-start(bf16[8,128,128]{2,1,0:T(8,128)(2,1)S(1)} %collective-permute-done.4), channel_id=1, source_target_pairs={{0,224},{8,232},{16,240},{24,248},{32,0},{40,8},{48,16},{56,24},{6... | collective-permute-start | bytes 786440 | tf_op jit(solution)/shard_map/ppermute | solution.py:43
  26.2 2.6 %collective-permute-done.5 = bf16[8,128,128]{2,1,0:T(8,128)(2,1)S(1)} collective-permute-done((bf16[8,128,128]{2,1,0:T(8,128)(2,1)S(1)}, bf16[8,128,128]{2,1,0:T(8,128)(2,1)S(1)}, u32[]{:S(2)}, u32[]{:S(2)}) %collective-permute-start.5) | collective-permute-done | bytes 262176 | tf_op jit(solution)/shard_map/ppermute | solution.py:43
  28.9 3.3 %collective-permute-start.8 = (bf16[6,128,128]{2,1,0:T(8,128)(2,1)S(1)}, bf16[6,128,128]{2,1,0:T(8,128)(2,1)S(1)}, u32[]{:S(2)}, u32[]{:S(2)}) collective-permute-start(bf16[6,128,128]{2,1,0:T(8,128)(2,1)S(1)} %slice.291), channel_id=1, source_target_pairs={{0,224},{8,232},{16,240},{24,248},{32,0},{40,8},{48,16},{56,24},{6... | collective-permute-start | bytes 589832 | tf_op jit(solution)/shard_map/ppermute | solution.py:43
  32.3 4.1 %collective-permute-done.7 = bf16[6,128,128]{2,1,0:T(8,128)(2,1)S(1)} collective-permute-done((bf16[6,128,128]{2,1,0:T(8,128)(2,1)S(1)}, bf16[6,128,128]{2,1,0:T(8,128)(2,1)S(1)}, u32[]{:S(2)}, u32[]{:S(2)}) %collective-permute-start.7) | collective-permute-done | bytes 196640 | tf_op jit(solution)/shard_map/ppermute | solution.py:43
  36.5 3.3 %collective-permute-start.10 = (bf16[2,128,128]{2,1,0:T(8,128)(2,1)S(1)}, bf16[2,128,128]{2,1,0:T(8,128)(2,1)S(1)}, u32[]{:S(2)}, u32[]{:S(2)}) collective-permute-start(bf16[2,128,128]{2,1,0:T(8,128)(2,1)S(1)} %slice.293), channel_id=1, source_target_pairs={{0,224},{8,232},{16,240},{24,248},{32,0},{40,8},{48,16},{56,24},{6... | collective-permute-start | bytes 196616 | tf_op jit(solution)/shard_map/ppermute | solution.py:43
  40.6 1.4 collective-permute-done.9
  42.8 1.3 collective-permute-done.15.refs_9_
  44.1 4.3 %forward_product.1 = bf16[32,128,128]{2,1,0:T(8,128)(2,1)S(1)} custom-call(s32[256]{0:T(256)S(1)} %get-tuple-element.109.dst, s32[256]{0:T(256)S(1)} %get-tuple-element.112.src, s32[1]{0:T(128)} %bitcast.154.count, bf16[256,128,128]{2,1,0:T(8,128)(2,1)} %bitcast.159, bf16[16,128,128]{2,1,0:T(8,128)(2,1)S(1)} %pad_maximum_fusion.refs_0_, ...), custom_call_target="tpu_custom_call" | custom-call | flops 1073741824 | bytes 14680064 | tf_op jit(solution)/shard_map/forward_product/pallas_call | solution.py:125
  48.4 20.2 %all_to_all.10.parts = bf16[8,512,128]{2,1,0:T(8,128)(2,1)S(1)} all-to-all(bf16[8,512,128]{2,1,0:T(8,128)(2,1)S(1)} %bitcast.157), channel_id=1, replica_groups=mesh['row'=32,'col'=8] {'col'}, dimensions={0} | all-to-all | bytes 2097152 | tf_op jit(solution)/shard_map/all_to_all | solution.py:365
  68.6 1.0 middle.1
  69.6 19.3 %all_to_all.11 = bf16[8,5,128,128]{3,2,1,0:T(8,128)(2,1)S(1)} all-to-all(bf16[8,5,128,128]{3,2,1,0:T(8,128)(2,1)S(1)} %get-tuple-element.46), channel_id=1, replica_groups=mesh['row'=32,'col'=8] {'col'}, dimensions={0} | all-to-all | bytes 2621440 | tf_op jit(solution)/shard_map/all_to_all | solution.py:367
  88.9 4.5 %backward_product.1 = (bf16[64,128,128]{2,1,0:T(8,128)(2,1)S(1)}, bf16[18,128,128]{2,1,0:T(8,128)(2,1)S(1)}, bf16[48,128,128]{2,1,0:T(8,128)(2,1)S(1)}, f32[128,128]{1,0:T(8,128)S(1)}) custom-call(s32[256]{0:T(256)S(1)} %get-tuple-element.113.dst, s32[256]{0:T(256)S(1)} %get-tuple-element.108.src, s32[1]{0:T(128)} %bitcast.155.count, ...), custom_call_target="tpu_custom_call" | custom-call | flops 1073741824 | bytes 14680064 | tf_op jit(solution)/shard_map/backward_product/pallas_call | solution.py:125
  94.0 1.5 %collective-permute-done.17 = bf16[18,128,128]{2,1,0:T(8,128)(2,1)S(1)} collective-permute-done((bf16[18,128,128]{2,1,0:T(8,128)(2,1)S(1)}, bf16[18,128,128]{2,1,0:T(8,128)(2,1)S(1)}, u32[]{:S(2)}, u32[]{:S(2)}) %collective-permute-start.17) | collective-permute-done | bytes 589856 | tf_op jit(solution)/shard_map/ppermute | solution.py:47
  95.7 4.2 %collective-permute-start.19 = (bf16[3,128,128]{2,1,0:T(8,128)(2,1)S(1)}, bf16[3,128,128]{2,1,0:T(8,128)(2,1)S(1)}, u32[]{:S(2)}, u32[]{:S(2)}) collective-permute-start(bf16[3,128,128]{2,1,0:T(8,128)(2,1)S(1)} %get-tuple-element.52), channel_id=1, source_target_pairs={{0,224},{8,232},{16,240},{24,248},{32,0},{40,8},{48,16},{56,24},{6... | collective-permute-start | bytes 294920 | tf_op jit(solution)/shard_map/ppermute | solution.py:43
  99.9 3.0 %collective-permute-done.18 = bf16[3,128,128]{2,1,0:T(8,128)(2,1)S(1)} collective-permute-done((bf16[3,128,128]{2,1,0:T(8,128)(2,1)S(1)}, bf16[3,128,128]{2,1,0:T(8,128)(2,1)S(1)}, u32[]{:S(2)}, u32[]{:S(2)}) %collective-permute-start.18) | collective-permute-done | bytes 98336 | tf_op jit(solution)/shard_map/ppermute | solution.py:43
  103.2 2.6 %collective-permute-start.20 = (bf16[7,128,128]{2,1,0:T(8,128)(2,1)S(1)}, bf16[7,128,128]{2,1,0:T(8,128)(2,1)S(1)}, u32[]{:S(2)}, u32[]{:S(2)}) collective-permute-start(bf16[7,128,128]{2,1,0:T(8,128)(2,1)S(1)} %pad_maximum_fusion.9), channel_id=1, source_target_pairs={{0,32},{8,40},{16,48},{24,56},{32,64},{40,72},{48,80},{56,88},{64,... | collective-permute-start | bytes 688136 | tf_op jit(solution)/shard_map/ppermute | solution.py:43
  106.5 5.1 %collective-permute-done.20 = bf16[7,128,128]{2,1,0:T(8,128)(2,1)S(1)} collective-permute-done((bf16[7,128,128]{2,1,0:T(8,128)(2,1)S(1)}, bf16[7,128,128]{2,1,0:T(8,128)(2,1)S(1)}, u32[]{:S(2)}, u32[]{:S(2)}) %collective-permute-start.20) | collective-permute-done | bytes 229408 | tf_op jit(solution)/shard_map/ppermute | solution.py:43
  113.0 2.1 %collective-permute-start.22 = (bf16[9,128,128]{2,1,0:T(8,128)(2,1)S(1)}, bf16[9,128,128]{2,1,0:T(8,128)(2,1)S(1)}, u32[]{:S(2)}, u32[]{:S(2)}) collective-permute-start(bf16[9,128,128]{2,1,0:T(8,128)(2,1)S(1)} %pad_maximum_fusion.3), channel_id=1, source_target_pairs={{0,32},{8,40},{16,48},{24,56},{32,64},{40,72},{48,80},{56,88},{64,... | collective-permute-start | bytes 884744 | tf_op jit(solution)/shard_map/ppermute | solution.py:43
  115.0 1.3 collective-permute-start.23
  116.3 5.0 %collective-permute-done.22 = bf16[9,128,128]{2,1,0:T(8,128)(2,1)S(1)} collective-permute-done((bf16[9,128,128]{2,1,0:T(8,128)(2,1)S(1)}, bf16[9,128,128]{2,1,0:T(8,128)(2,1)S(1)}, u32[]{:S(2)}, u32[]{:S(2)}) %collective-permute-start.22) | collective-permute-done | bytes 294944 | tf_op jit(solution)/shard_map/ppermute | solution.py:43
  122.1 2.1 %collective-permute-start.24 = (bf16[9,128,128]{2,1,0:T(8,128)(2,1)S(1)}, bf16[9,128,128]{2,1,0:T(8,128)(2,1)S(1)}, u32[]{:S(2)}, u32[]{:S(2)}) collective-permute-start(bf16[9,128,128]{2,1,0:T(8,128)(2,1)S(1)} %pad_maximum_fusion.5), channel_id=1, source_target_pairs={{0,32},{8,40},{16,48},{24,56},{32,64},{40,72},{48,80},{56,88},{64,... | collective-permute-start | bytes 884744 | tf_op jit(solution)/shard_map/ppermute | solution.py:43
  124.2 1.2 collective-permute-start.25
  125.4 4.7 %collective-permute-done.24 = bf16[9,128,128]{2,1,0:T(8,128)(2,1)S(1)} collective-permute-done((bf16[9,128,128]{2,1,0:T(8,128)(2,1)S(1)}, bf16[9,128,128]{2,1,0:T(8,128)(2,1)S(1)}, u32[]{:S(2)}, u32[]{:S(2)}) %collective-permute-start.24) | collective-permute-done | bytes 294944 | tf_op jit(solution)/shard_map/ppermute | solution.py:43
  131.1 1.8 %collective-permute-start.26 = (bf16[4,128,128]{2,1,0:T(8,128)(2,1)S(1)}, bf16[4,128,128]{2,1,0:T(8,128)(2,1)S(1)}, u32[]{:S(2)}, u32[]{:S(2)}) collective-permute-start(bf16[4,128,128]{2,1,0:T(8,128)(2,1)S(1)} %get-tuple-element.72), channel_id=1, source_target_pairs={{0,32},{8,40},{16,48},{24,56},{32,64},{40,72},{48,80},{56,88},{64,... | collective-permute-start | bytes 393224 | tf_op jit(solution)/shard_map/ppermute | solution.py:43
  132.9 1.5 %collective-permute-start.27 = (bf16[4,128,128]{2,1,0:T(8,128)(2,1)S(1)}, bf16[4,128,128]{2,1,0:T(8,128)(2,1)S(1)}, u32[]{:S(2)}, u32[]{:S(2)}) collective-permute-start(bf16[4,128,128]{2,1,0:T(8,128)(2,1)S(1)} %get-tuple-element.73), channel_id=1, source_target_pairs={{0,224},{8,232},{16,240},{24,248},{32,0},{40,8},{48,16},{56,24},{6... | collective-permute-start | bytes 393224 | tf_op jit(solution)/shard_map/ppermute | solution.py:43
  134.7 3.1 %collective-permute-start.28 = (bf16[5,128,128]{2,1,0:T(8,128)(2,1)S(1)}, bf16[5,128,128]{2,1,0:T(8,128)(2,1)S(1)}, u32[]{:S(2)}, u32[]{:S(2)}) collective-permute-start(bf16[5,128,128]{2,1,0:T(8,128)(2,1)S(1)} %pad_maximum_fusion.11), channel_id=1, source_target_pairs={{0,16},{8,24},{16,0},{24,8},{32,48},{40,56},{48,32},{56,40},{64,80... | collective-permute-start | bytes 491528 | tf_op jit(solution)/shard_map/ppermute | solution.py:47
  137.9 3.6 %collective-permute-done.28.refs_1_ = bf16[5,128,128]{2,1,0:T(8,128)(2,1)S(1)} collective-permute-done((bf16[5,128,128]{2,1,0:T(8,128)(2,1)S(1)}, bf16[5,128,128]{2,1,0:T(8,128)(2,1)S(1)}, u32[]{:S(2)}, u32[]{:S(2)}) %collective-permute-start.28) | collective-permute-done | bytes 163872 | tf_op jit(solution)/shard_map/ppermute | solution.py:47
  (85 shorter events, 10.1 us)
Async XLA Ops:
  0.6 9.0 %collective-permute-start.2 = (bf16[4,128,128]{2,1,0:T(8,128)(2,1)}, bf16[4,128,128]{2,1,0:T(8,128)(2,1)S(1)}, u32[]{:S(2)}, u32[]{:S(2)}) collective-permute-start(bf16[4,128,128]{2,1,0:T(8,128)(2,1)} %bitcast.162), channel_id=1, source_target_pairs={{0,224},{8,232},{16,240},{24,248},{32,0},{40,8},{48,16},{56,24},{6... | collective-permute-start | bytes 393224 | tf_op jit(solution)/shard_map/ppermute | solution.py:43
  6.6 6.4 %collective-permute-start.1 = (bf16[4,128,128]{2,1,0:T(8,128)(2,1)}, bf16[4,128,128]{2,1,0:T(8,128)(2,1)S(1)}, u32[]{:S(2)}, u32[]{:S(2)}) collective-permute-start(bf16[4,128,128]{2,1,0:T(8,128)(2,1)} %bitcast.163), channel_id=1, source_target_pairs={{0,32},{8,40},{16,48},{24,56},{32,64},{40,72},{48,80},{56,88},{64,... | collective-permute-start | bytes 393224 | tf_op jit(solution)/shard_map/ppermute | solution.py:43
  6.6 6.7 %collective-permute-start = (bf16[4,128,128]{2,1,0:T(8,128)(2,1)}, bf16[4,128,128]{2,1,0:T(8,128)(2,1)S(1)}, u32[]{:S(2)}, u32[]{:S(2)}) collective-permute-start(bf16[4,128,128]{2,1,0:T(8,128)(2,1)} %bitcast.164), channel_id=1, source_target_pairs={{0,16},{8,24},{16,0},{24,8},{32,48},{40,56},{48,32},{56,40},{64,80... | collective-permute-start | bytes 393224 | tf_op jit(solution)/shard_map/ppermute | solution.py:47
  13.3 7.9 %collective-permute-start.3 = (bf16[8,128,128]{2,1,0:T(8,128)(2,1)S(1)}, bf16[8,128,128]{2,1,0:T(8,128)(2,1)S(1)}, u32[]{:S(2)}, u32[]{:S(2)}) collective-permute-start(bf16[8,128,128]{2,1,0:T(8,128)(2,1)S(1)} %get-tuple-element.102), channel_id=1, source_target_pairs={{0,32},{8,40},{16,48},{24,56},{32,64},{40,72},{48,80},{56,88},{64,... | collective-permute-start | bytes 786440 | tf_op jit(solution)/shard_map/ppermute | solution.py:43
  13.4 7.8 %collective-permute-start.4 = (bf16[8,128,128]{2,1,0:T(8,128)(2,1)S(1)}, bf16[8,128,128]{2,1,0:T(8,128)(2,1)S(1)}, u32[]{:S(2)}, u32[]{:S(2)}) collective-permute-start(bf16[8,128,128]{2,1,0:T(8,128)(2,1)S(1)} %get-tuple-element.103), channel_id=1, source_target_pairs={{0,224},{8,232},{16,240},{24,248},{32,0},{40,8},{48,16},{56,24},{6... | collective-permute-start | bytes 786440 | tf_op jit(solution)/shard_map/ppermute | solution.py:43
  21.2 7.6 %collective-permute-start.5 = (bf16[8,128,128]{2,1,0:T(8,128)(2,1)S(1)}, bf16[8,128,128]{2,1,0:T(8,128)(2,1)S(1)}, u32[]{:S(2)}, u32[]{:S(2)}) collective-permute-start(bf16[8,128,128]{2,1,0:T(8,128)(2,1)S(1)} %collective-permute-done.3), channel_id=1, source_target_pairs={{0,32},{8,40},{16,48},{24,56},{32,64},{40,72},{48,80},{56,88},{64,... | collective-permute-start | bytes 786440 | tf_op jit(solution)/shard_map/ppermute | solution.py:43
  21.2 7.7 %collective-permute-start.6 = (bf16[8,128,128]{2,1,0:T(8,128)(2,1)S(1)}, bf16[8,128,128]{2,1,0:T(8,128)(2,1)S(1)}, u32[]{:S(2)}, u32[]{:S(2)}) collective-permute-start(bf16[8,128,128]{2,1,0:T(8,128)(2,1)S(1)} %collective-permute-done.4), channel_id=1, source_target_pairs={{0,224},{8,232},{16,240},{24,248},{32,0},{40,8},{48,16},{56,24},{6... | collective-permute-start | bytes 786440 | tf_op jit(solution)/shard_map/ppermute | solution.py:43
  28.8 7.7 %collective-permute-start.7 = (bf16[6,128,128]{2,1,0:T(8,128)(2,1)S(1)}, bf16[6,128,128]{2,1,0:T(8,128)(2,1)S(1)}, u32[]{:S(2)}, u32[]{:S(2)}) collective-permute-start(bf16[6,128,128]{2,1,0:T(8,128)(2,1)S(1)} %slice.290), channel_id=1, source_target_pairs={{0,32},{8,40},{16,48},{24,56},{32,64},{40,72},{48,80},{56,88},{64,... | collective-permute-start | bytes 589832 | tf_op jit(solution)/shard_map/ppermute | solution.py:43
  28.9 7.6 %collective-permute-start.8 = (bf16[6,128,128]{2,1,0:T(8,128)(2,1)S(1)}, bf16[6,128,128]{2,1,0:T(8,128)(2,1)S(1)}, u32[]{:S(2)}, u32[]{:S(2)}) collective-permute-start(bf16[6,128,128]{2,1,0:T(8,128)(2,1)S(1)} %slice.291), channel_id=1, source_target_pairs={{0,224},{8,232},{16,240},{24,248},{32,0},{40,8},{48,16},{56,24},{6... | collective-permute-start | bytes 589832 | tf_op jit(solution)/shard_map/ppermute | solution.py:43
  36.5 5.5 %collective-permute-start.9 = (bf16[2,128,128]{2,1,0:T(8,128)(2,1)S(1)}, bf16[2,128,128]{2,1,0:T(8,128)(2,1)S(1)}, u32[]{:S(2)}, u32[]{:S(2)}) collective-permute-start(bf16[2,128,128]{2,1,0:T(8,128)(2,1)S(1)} %slice.292), channel_id=1, source_target_pairs={{0,32},{8,40},{16,48},{24,56},{32,64},{40,72},{48,80},{56,88},{64,... | collective-permute-start | bytes 196616 | tf_op jit(solution)/shard_map/ppermute | solution.py:43
  36.5 5.5 %collective-permute-start.10 = (bf16[2,128,128]{2,1,0:T(8,128)(2,1)S(1)}, bf16[2,128,128]{2,1,0:T(8,128)(2,1)S(1)}, u32[]{:S(2)}, u32[]{:S(2)}) collective-permute-start(bf16[2,128,128]{2,1,0:T(8,128)(2,1)S(1)} %slice.293), channel_id=1, source_target_pairs={{0,224},{8,232},{16,240},{24,248},{32,0},{40,8},{48,16},{56,24},{6... | collective-permute-start | bytes 196616 | tf_op jit(solution)/shard_map/ppermute | solution.py:43
  39.8 4.3 %collective-permute-start.11 = (bf16[16,128,128]{2,1,0:T(8,128)(2,1)S(1)}, bf16[16,128,128]{2,1,0:T(8,128)(2,1)S(1)}, u32[]{:S(2)}, u32[]{:S(2)}) collective-permute-start(bf16[16,128,128]{2,1,0:T(8,128)(2,1)S(1)} %pad_maximum_fusion.refs_0_), channel_id=1, source_target_pairs={{0,8},{8,0},{16,24},{24,16},{32,40},{40,32},{48,56},{56,48},{64,72... | collective-permute-start | bytes 1572872 | tf_op jit(solution)/shard_map/ppermute | solution.py:47
  39.9 4.2 %collective-permute-start.12 = (bf16[16,128,128]{2,1,0:T(8,128)(2,1)S(1)}, bf16[16,128,128]{2,1,0:T(8,128)(2,1)S(1)}, u32[]{:S(2)}, u32[]{:S(2)}) collective-permute-start(bf16[16,128,128]{2,1,0:T(8,128)(2,1)S(1)} %pad_maximum_fusion.1.refs_1_), channel_id=1, source_target_pairs={{0,8},{8,0},{16,24},{24,16},{32,40},{40,32},{48,56},{56,48},{64,72... | collective-permute-start | bytes 1572872 | tf_op jit(solution)/shard_map/ppermute | solution.py:47
  40.4 3.7 %collective-permute-start.13 = (bf16[16,128,128]{2,1,0:T(8,128)(2,1)S(1)}, bf16[16,128,128]{2,1,0:T(8,128)(2,1)S(1)}, u32[]{:S(2)}, u32[]{:S(2)}) collective-permute-start(bf16[16,128,128]{2,1,0:T(8,128)(2,1)S(1)} %pad_maximum_fusion.2.refs_2_), channel_id=1, source_target_pairs={{0,8},{8,0},{16,24},{24,16},{32,40},{40,32},{48,56},{56,48},{64,72... | collective-permute-start | bytes 1572872 | tf_op jit(solution)/shard_map/ppermute | solution.py:47
  41.9 2.1 %collective-permute-start.14 = (bf16[12,128,128]{2,1,0:T(8,128)(2,1)S(1)}, bf16[12,128,128]{2,1,0:T(8,128)(2,1)S(1)}, u32[]{:S(2)}, u32[]{:S(2)}) collective-permute-start(bf16[12,128,128]{2,1,0:T(8,128)(2,1)S(1)} %constant_dynamic-update-slice_fusion.refs_3_), channel_id=1, source_target_pairs={{0,8},{8,0},{16,24},{24,16},{32,40},{40,32},{48,56},{56,48},{64,72... | collective-permute-start | bytes 1179656 | tf_op jit(solution)/shard_map/ppermute | solution.py:47
  42.0 2.1 %collective-permute-start.15 = (bf16[4,128,128]{2,1,0:T(8,128)(2,1)S(1)}, bf16[4,128,128]{2,1,0:T(8,128)(2,1)S(1)}, u32[]{:S(2)}, u32[]{:S(2)}) collective-permute-start(bf16[4,128,128]{2,1,0:T(8,128)(2,1)S(1)} %constant_dynamic-update-slice_fusion.2.refs_4_), channel_id=1, source_target_pairs={{0,8},{8,0},{16,24},{24,16},{32,40},{40,32},{48,56},{56,48},{64,72... | collective-permute-start | bytes 393224 | tf_op jit(solution)/shard_map/ppermute | solution.py:47
  48.4 20.2 %copy-start = (bf16[512,128]{1,0:T(8,128)(2,1)S(1)}, bf16[512,128]{1,0:T(8,128)(2,1)}, u32[]{:S(2)}) copy-start(bf16[512,128]{1,0:T(8,128)(2,1)} %cotangent.1) | copy-start | bytes 393220
  48.4 20.2 %copy-start.1 = (bf16[128,128]{1,0:T(8,128)(2,1)S(1)}, bf16[128,128]{1,0:T(8,128)(2,1)}, u32[]{:S(2)}) copy-start(bf16[128,128]{1,0:T(8,128)(2,1)} %refs_3_.1) | copy-start | bytes 98308
  93.4 2.1 %collective-permute-start.17 = (bf16[18,128,128]{2,1,0:T(8,128)(2,1)S(1)}, bf16[18,128,128]{2,1,0:T(8,128)(2,1)S(1)}, u32[]{:S(2)}, u32[]{:S(2)}) collective-permute-start(bf16[18,128,128]{2,1,0:T(8,128)(2,1)S(1)} %get-tuple-element.49), channel_id=1, source_target_pairs={{0,8},{8,0},{16,24},{24,16},{32,40},{40,32},{48,56},{56,48},{64,72... | collective-permute-start | bytes 1769480 | tf_op jit(solution)/shard_map/ppermute | solution.py:47
  93.5 18.8 %collective-permute-start.16 = (bf16[48,128,128]{2,1,0:T(8,128)(2,1)S(1)}, bf16[48,128,128]{2,1,0:T(8,128)(2,1)S(1)}, u32[]{:S(2)}, u32[]{:S(2)}) collective-permute-start(bf16[48,128,128]{2,1,0:T(8,128)(2,1)S(1)} %get-tuple-element.48), channel_id=1, source_target_pairs={{0,8},{8,0},{16,24},{24,16},{32,40},{40,32},{48,56},{56,48},{64,72... | collective-permute-start | bytes 4718600 | tf_op jit(solution)/shard_map/ppermute | solution.py:47
  95.6 7.3 %collective-permute-start.18 = (bf16[3,128,128]{2,1,0:T(8,128)(2,1)S(1)}, bf16[3,128,128]{2,1,0:T(8,128)(2,1)S(1)}, u32[]{:S(2)}, u32[]{:S(2)}) collective-permute-start(bf16[3,128,128]{2,1,0:T(8,128)(2,1)S(1)} %get-tuple-element.51), channel_id=1, source_target_pairs={{0,32},{8,40},{16,48},{24,56},{32,64},{40,72},{48,80},{56,88},{64,... | collective-permute-start | bytes 294920 | tf_op jit(solution)/shard_map/ppermute | solution.py:43
  95.7 7.2 %collective-permute-start.19 = (bf16[3,128,128]{2,1,0:T(8,128)(2,1)S(1)}, bf16[3,128,128]{2,1,0:T(8,128)(2,1)S(1)}, u32[]{:S(2)}, u32[]{:S(2)}) collective-permute-start(bf16[3,128,128]{2,1,0:T(8,128)(2,1)S(1)} %get-tuple-element.52), channel_id=1, source_target_pairs={{0,224},{8,232},{16,240},{24,248},{32,0},{40,8},{48,16},{56,24},{6... | collective-permute-start | bytes 294920 | tf_op jit(solution)/shard_map/ppermute | solution.py:43
  103.2 8.4 %collective-permute-start.20 = (bf16[7,128,128]{2,1,0:T(8,128)(2,1)S(1)}, bf16[7,128,128]{2,1,0:T(8,128)(2,1)S(1)}, u32[]{:S(2)}, u32[]{:S(2)}) collective-permute-start(bf16[7,128,128]{2,1,0:T(8,128)(2,1)S(1)} %pad_maximum_fusion.9), channel_id=1, source_target_pairs={{0,32},{8,40},{16,48},{24,56},{32,64},{40,72},{48,80},{56,88},{64,... | collective-permute-start | bytes 688136 | tf_op jit(solution)/shard_map/ppermute | solution.py:43
  105.7 6.5 %collective-permute-start.21 = (bf16[7,128,128]{2,1,0:T(8,128)(2,1)S(1)}, bf16[7,128,128]{2,1,0:T(8,128)(2,1)S(1)}, u32[]{:S(2)}, u32[]{:S(2)}) collective-permute-start(bf16[7,128,128]{2,1,0:T(8,128)(2,1)S(1)} %pad_maximum_fusion.10), channel_id=1, source_target_pairs={{0,224},{8,232},{16,240},{24,248},{32,0},{40,8},{48,16},{56,24},{6... | collective-permute-start | bytes 688136 | tf_op jit(solution)/shard_map/ppermute | solution.py:43
  113.0 8.3 %collective-permute-start.22 = (bf16[9,128,128]{2,1,0:T(8,128)(2,1)S(1)}, bf16[9,128,128]{2,1,0:T(8,128)(2,1)S(1)}, u32[]{:S(2)}, u32[]{:S(2)}) collective-permute-start(bf16[9,128,128]{2,1,0:T(8,128)(2,1)S(1)} %pad_maximum_fusion.3), channel_id=1, source_target_pairs={{0,32},{8,40},{16,48},{24,56},{32,64},{40,72},{48,80},{56,88},{64,... | collective-permute-start | bytes 884744 | tf_op jit(solution)/shard_map/ppermute | solution.py:43
  115.0 6.7 %collective-permute-start.23 = (bf16[9,128,128]{2,1,0:T(8,128)(2,1)S(1)}, bf16[9,128,128]{2,1,0:T(8,128)(2,1)S(1)}, u32[]{:S(2)}, u32[]{:S(2)}) collective-permute-start(bf16[9,128,128]{2,1,0:T(8,128)(2,1)S(1)} %pad_maximum_fusion.4), channel_id=1, source_target_pairs={{0,224},{8,232},{16,240},{24,248},{32,0},{40,8},{48,16},{56,24},{6... | collective-permute-start | bytes 884744 | tf_op jit(solution)/shard_map/ppermute | solution.py:43
  122.1 8.0 %collective-permute-start.24 = (bf16[9,128,128]{2,1,0:T(8,128)(2,1)S(1)}, bf16[9,128,128]{2,1,0:T(8,128)(2,1)S(1)}, u32[]{:S(2)}, u32[]{:S(2)}) collective-permute-start(bf16[9,128,128]{2,1,0:T(8,128)(2,1)S(1)} %pad_maximum_fusion.5), channel_id=1, source_target_pairs={{0,32},{8,40},{16,48},{24,56},{32,64},{40,72},{48,80},{56,88},{64,... | collective-permute-start | bytes 884744 | tf_op jit(solution)/shard_map/ppermute | solution.py:43
  124.2 6.7 %collective-permute-start.25 = (bf16[9,128,128]{2,1,0:T(8,128)(2,1)S(1)}, bf16[9,128,128]{2,1,0:T(8,128)(2,1)S(1)}, u32[]{:S(2)}, u32[]{:S(2)}) collective-permute-start(bf16[9,128,128]{2,1,0:T(8,128)(2,1)S(1)} %pad_maximum_fusion.6), channel_id=1, source_target_pairs={{0,224},{8,232},{16,240},{24,248},{32,0},{40,8},{48,16},{56,24},{6... | collective-permute-start | bytes 884744 | tf_op jit(solution)/shard_map/ppermute | solution.py:43
  131.1 6.7 %collective-permute-start.26 = (bf16[4,128,128]{2,1,0:T(8,128)(2,1)S(1)}, bf16[4,128,128]{2,1,0:T(8,128)(2,1)S(1)}, u32[]{:S(2)}, u32[]{:S(2)}) collective-permute-start(bf16[4,128,128]{2,1,0:T(8,128)(2,1)S(1)} %get-tuple-element.72), channel_id=1, source_target_pairs={{0,32},{8,40},{16,48},{24,56},{32,64},{40,72},{48,80},{56,88},{64,... | collective-permute-start | bytes 393224 | tf_op jit(solution)/shard_map/ppermute | solution.py:43
  132.9 5.0 %collective-permute-start.27 = (bf16[4,128,128]{2,1,0:T(8,128)(2,1)S(1)}, bf16[4,128,128]{2,1,0:T(8,128)(2,1)S(1)}, u32[]{:S(2)}, u32[]{:S(2)}) collective-permute-start(bf16[4,128,128]{2,1,0:T(8,128)(2,1)S(1)} %get-tuple-element.73), channel_id=1, source_target_pairs={{0,224},{8,232},{16,240},{24,248},{32,0},{40,8},{48,16},{56,24},{6... | collective-permute-start | bytes 393224 | tf_op jit(solution)/shard_map/ppermute | solution.py:43
  134.7 6.9 %collective-permute-start.28 = (bf16[5,128,128]{2,1,0:T(8,128)(2,1)S(1)}, bf16[5,128,128]{2,1,0:T(8,128)(2,1)S(1)}, u32[]{:S(2)}, u32[]{:S(2)}) collective-permute-start(bf16[5,128,128]{2,1,0:T(8,128)(2,1)S(1)} %pad_maximum_fusion.11), channel_id=1, source_target_pairs={{0,16},{8,24},{16,0},{24,8},{32,48},{40,56},{48,32},{56,40},{64,80... | collective-permute-start | bytes 491528 | tf_op jit(solution)/shard_map/ppermute | solution.py:47
